TPU v7x, 32 devices: a whole 2x2x4 slice. The times are simulated.
32 devices in a mesh: plane: 16 (over z, y, x), cuts: 2 (over core).
Axes of the slice: x: 2, y: 2, z: 4, core: 2. Of those that a mesh axis runs over, the one named last changes fastest.
Arguments:
- image: float32 [256, 128, 256], P('plane', None, 'cuts'), may hold values from 0 to 2
- projection_weight_tiles: bfloat16 [1536, 256, 256], P('plane'), may hold values from -0.0390625 to 0.0390625
- pair_tile_index: int32 [1536], P('plane'), may hold values from 0 to 7
- pair_ray_block: int32 [1536], P('plane'), may hold values from 0 to 15
- ray_owner: int32 [16], replicated, may hold values from 0 to 15, each once
- active_pair_count: int32 [16], P('plane'), may hold values from 12 to 96, as said below
- measured: float32 [16, 256, 256], P('plane', None, 'cuts'), may hold values from -6 to 6
Outputs:
- volume: float32 [256, 128, 256], P('plane', None, 'cuts')
- residual: bfloat16 [16, 256, 256], P('plane', None, 'cuts')
Inputs may be any that keep to these rules, and one draw needn't show every extreme that they name: The first active_pair_count[d] pairs of plane index d are live and the rest are not; some index has all 96 pairs live. `ray_owner`: each owner position is taken by exactly one ray block.
All inputs are finite; a program needn't handle non-finite values.
Results may differ from a plain program's by a relative error of at most 0.0045.
Values may be sent and summed in bfloat16 or wider, within the bound.
No kernel may reach another device: no remote copies, remote signals or barrier semaphores. Data moves between devices by JAX's collectives and lax.ppermute only.
A program may use at most 128 MiB of HBM per device.

v0:
```python
import jax
import jax.numpy as jnp
from jax import lax
from jax.sharding import PartitionSpec as P

TILE = 16
SWEEPS = 4


smooth_square = 0.09
flow_step = 0.04
relax_step = 4.0
group_width = 32


def with_halo(block, sides, width):
    for axis, dim in sides:
        count = lax.axis_size(axis)
        forward = [(i, i + 1) for i in range(count - 1)]
        backward = [(target, source) for source, target in forward]
        low = lax.ppermute(
            lax.slice_in_dim(block, block.shape[dim] - width, None, axis=dim), axis, forward
        )
        high = lax.ppermute(lax.slice_in_dim(block, 0, width, axis=dim), axis, backward)
        block = jnp.concatenate([low, block, high], axis=dim)
    return block


def smooth_sweep(volume, inside):
    rise_rows = jnp.concatenate([volume[1:] - volume[:-1], -volume[-1:]], axis=0)
    rise_cols = jnp.concatenate([volume[:, 1:] - volume[:, :-1], -volume[:, -1:]], axis=1)
    rise_slices = jnp.concatenate(
        [volume[:, :, 1:] - volume[:, :, :-1], -volume[:, :, -1:]], axis=2
    )
    length = jnp.sqrt(
        smooth_square + rise_rows * rise_rows + rise_cols * rise_cols + rise_slices * rise_slices
    )
    flow_rows = rise_rows / length * inside
    flow_cols = rise_cols / length * inside
    flow_slices = rise_slices / length * inside
    diverge = flow_rows - jnp.concatenate([jnp.zeros_like(flow_rows[:1]), flow_rows[:-1]], axis=0)
    diverge = (
        diverge
        + flow_cols
        - jnp.concatenate([jnp.zeros_like(flow_cols[:, :1]), flow_cols[:, :-1]], axis=1)
    )
    diverge = (
        diverge
        + flow_slices
        - jnp.concatenate([jnp.zeros_like(flow_slices[:, :, :1]), flow_slices[:, :, :-1]], axis=2)
    )
    return (volume + flow_step * diverge) * inside


def per_device(
    image,
    projection_weight_tiles,
    pair_tile_index,
    pair_ray_block,
    ray_owner,
    active_pair_count,
    measured,
):
    row_count, col_count, slice_count = image.shape
    slot_total, voxels, ray_count = projection_weight_tiles.shape
    tile_rows = row_count // TILE
    tile_cols = col_count // TILE
    tiles_here = tile_rows * tile_cols
    block_count = slot_total // group_width
    ray_blocks = ray_owner.shape[0]
    grouped = (
        image.reshape(tile_rows, TILE, tile_cols, TILE, slice_count)
        .transpose(0, 2, 1, 3, 4)
        .reshape(tiles_here, voxels, slice_count)
        .astype(jnp.bfloat16)
    )
    owner_of = ray_owner[pair_ray_block]
    active_pair = jnp.arange(slot_total, dtype=jnp.int32) < active_pair_count[0]

    def block_parts(block_index):
        first_slot = block_index * group_width
        weights = lax.dynamic_slice_in_dim(projection_weight_tiles, first_slot, group_width, 0)
        tile_ids = lax.dynamic_slice_in_dim(pair_tile_index, first_slot, group_width, 0)
        owners = lax.dynamic_slice_in_dim(owner_of, first_slot, group_width, 0)
        live_part = lax.dynamic_slice_in_dim(active_pair, first_slot, group_width, 0)
        return (weights, tile_ids, owners, live_part)

    def forward(block_index, running):
        weights, tile_ids, owners, live_part = block_parts(block_index)
        values = jnp.take(grouped, tile_ids, axis=0)
        product = jnp.einsum("svr,svc->src", weights, values, preferred_element_type=jnp.float32)
        product = jnp.where(live_part[:, None, None], product, 0.0)
        return running.at[owners].add(product)

    partials = lax.fori_loop(
        0, block_count, forward, jnp.zeros((ray_blocks, ray_count, slice_count), jnp.float32)
    )
    own_sums = lax.psum_scatter(partials, "plane", scatter_dimension=0, tiled=True)
    mismatch = measured - own_sums
    residual = (mismatch / jnp.sqrt(1.0 + mismatch * mismatch)).astype(jnp.bfloat16)
    spread = lax.all_gather(residual, "plane", axis=0, tiled=True)

    def backward(block_index, running):
        weights, tile_ids, owners, live_part = block_parts(block_index)
        values = jnp.take(spread, owners, axis=0)
        product = jnp.einsum("svr,src->svc", weights, values, preferred_element_type=jnp.float32)
        product = jnp.where(live_part[:, None, None], product, 0.0)
        return running.at[tile_ids].add(product)

    update = lax.fori_loop(
        0, block_count, backward, jnp.zeros((tiles_here, voxels, slice_count), jnp.float32)
    )
    update = (
        update.reshape(tile_rows, tile_cols, TILE, TILE, slice_count)
        .transpose(0, 2, 1, 3, 4)
        .reshape(row_count, col_count, slice_count)
    )
    volume = jnp.maximum(image + relax_step * update, 0.0)
    row_start = lax.axis_index("plane") * row_count - 1
    slice_start = lax.axis_index("cuts") * slice_count - 1
    row_ids = row_start + jnp.arange(row_count + 2 * 1, dtype=jnp.int32)
    slice_ids = slice_start + jnp.arange(slice_count + 2 * 1, dtype=jnp.int32)
    row_inside = (row_ids >= 0) & (row_ids < row_count * lax.axis_size("plane"))
    slice_inside = (slice_ids >= 0) & (slice_ids < slice_count * lax.axis_size("cuts"))
    inside = (row_inside[:, None, None] & slice_inside[None, None, :]).astype(jnp.float32)
    for repeat in range(SWEEPS):
        padded = with_halo(volume, (("plane", 0), ("cuts", 2)), 1)
        volume = smooth_sweep(padded, inside)[1:-1, :, 1:-1]
    return (volume, residual)


def solution(mesh):
    placed = (
        P("plane", None, "cuts"),
        P("plane", None, None),
        P("plane"),
        P("plane"),
        P(),
        P("plane"),
        P("plane", None, "cuts"),
    )
    return jax.shard_map(
        per_device,
        mesh=mesh,
        in_specs=placed,
        out_specs=(P("plane", None, "cuts"), P("plane", None, "cuts")),
        check_vma=False,
    )
```

profile of v0, /device:TPU:1, one launch (start us, length us, event | category | flops | bytes accessed | tf_op | source)
XLA Modules:
  0.0 396.7 jit_solution(3301748017085012818)
XLA Ops:
  11.2 10.0 %compare_select_fusion.5 = s32[96]{0:T(128)S(1)} fusion(s32[96]{0:T(128)S(1)} %copy-done.27, s32[]{:T(128)} %bitcast.1, s32[]{:T(128)} %bitcast.2, s32[]{:T(128)} %bitcast.3, s32[]{:T(128)} %bitcast.4, s32[]{:T(128)} %bitcast.5, s32[]{:T(128)} %bitcast.6, s32[]{:T(128)} %bitcast.7, s32[]{:T(128)} %bitcast.8, s32[]{:T(128)} %bitcast.9, s32[]{:T(128)} %bitcast.10, ...), kind=kLoop, calls=%fused_computation.99 | loop fusion | flops 3168 | bytes 832 | tf_op jit(solution)/shard_map/gather | solution.py:77
  21.5 46.2 %while.26 = (s32[]{:T(128)}, f32[16,256,128]{2,1,0:T(8,128)S(1)}, s32[96]{0:T(128)S(1)}, pred[96]{0:T(512)(128)(4,1)S(1)}, bf16[96,256,256]{2,1,0:T(8,128)(2,1)}...) while((s32[]{:T(128)}, f32[16,256,128]{2,1,0:T(8,128)S(1)}, ...), condition=%wide.region_2.3_spmd, body=%wide.region_0.2_spmd.sunk | while | flops 540017984 | bytes 27268300 | solution.py:95
  23.8 6.5 %fusion.39 = f32[32,256,128]{2,1,0:T(8,128)} fusion(bf16[96,256,256]{2,1,0:T(8,128)(2,1)} %get-tuple-element.485, s32[]{:T(128)S(6)} %select_n.112, bf16[32,256,128]{2,1,0:T(8,128)(2,1)} %gather_fusion, pred[32]{0:T(512)(128)(4,1)S(1)} %get-tuple-element.449, pred[32]{0:T(512)(128)(4,1)S(1)} %dynamic_slice.78), kind=kOutput, calls=%fused_computation.6.clone.1 | convolution fusion | flops 538968064 | bytes 10485828 | tf_op jit(solution)/shard_map/while/body/eval_jaxpr/svr,svc->src/dot_general | solution.py:91
  30.4 6.5 %scatter_fusion = f32[16,256,128]{2,1,0:T(8,128)S(1)} fusion(f32[16,256,128]{2,1,0:T(8,128)S(1)} %get-tuple-element.471, s32[32]{0:T(128)S(1)} %compare_select_fusion.24, f32[32,256,128]{2,1,0:T(8,128)} %fusion.39), kind=kCustom, calls=%fused_computation.2.clone.1 | custom fusion | flops 1048576 | bytes 12583040 | tf_op jit(solution)/shard_map/while/body/eval_jaxpr/scatter-add | solution.py:93
  39.2 6.5 %fusion.39 = f32[32,256,128]{2,1,0:T(8,128)} fusion(bf16[96,256,256]{2,1,0:T(8,128)(2,1)} %get-tuple-element.485, s32[]{:T(128)S(6)} %select_n.112, bf16[32,256,128]{2,1,0:T(8,128)(2,1)} %gather_fusion, pred[32]{0:T(512)(128)(4,1)S(1)} %get-tuple-element.449, pred[32]{0:T(512)(128)(4,1)S(1)} %dynamic_slice.78), kind=kOutput, calls=%fused_computation.6.clone.1 | convolution fusion | flops 538968064 | bytes 10485828 | tf_op jit(solution)/shard_map/while/body/eval_jaxpr/svr,svc->src/dot_general | solution.py:91
  45.8 6.5 %scatter_fusion = f32[16,256,128]{2,1,0:T(8,128)S(1)} fusion(f32[16,256,128]{2,1,0:T(8,128)S(1)} %get-tuple-element.471, s32[32]{0:T(128)S(1)} %compare_select_fusion.24, f32[32,256,128]{2,1,0:T(8,128)} %fusion.39), kind=kCustom, calls=%fused_computation.2.clone.1 | custom fusion | flops 1048576 | bytes 12583040 | tf_op jit(solution)/shard_map/while/body/eval_jaxpr/scatter-add | solution.py:93
  54.6 6.5 %fusion.39 = f32[32,256,128]{2,1,0:T(8,128)} fusion(bf16[96,256,256]{2,1,0:T(8,128)(2,1)} %get-tuple-element.485, s32[]{:T(128)S(6)} %select_n.112, bf16[32,256,128]{2,1,0:T(8,128)(2,1)} %gather_fusion, pred[32]{0:T(512)(128)(4,1)S(1)} %get-tuple-element.449, pred[32]{0:T(512)(128)(4,1)S(1)} %dynamic_slice.78), kind=kOutput, calls=%fused_computation.6.clone.1 | convolution fusion | flops 538968064 | bytes 10485828 | tf_op jit(solution)/shard_map/while/body/eval_jaxpr/svr,svc->src/dot_general | solution.py:91
  61.1 6.5 %scatter_fusion = f32[16,256,128]{2,1,0:T(8,128)S(1)} fusion(f32[16,256,128]{2,1,0:T(8,128)S(1)} %get-tuple-element.471, s32[32]{0:T(128)S(1)} %compare_select_fusion.24, f32[32,256,128]{2,1,0:T(8,128)} %fusion.39), kind=kCustom, calls=%fused_computation.2.clone.1 | custom fusion | flops 1048576 | bytes 12583040 | tf_op jit(solution)/shard_map/while/body/eval_jaxpr/scatter-add | solution.py:93
  69.0 71.7 %reduce-scatter.2.cloned.1.call-done = f32[1,256,128]{2,1,0:T(8,128)} async-done(((f32[16,256,128]{2,1,0:T(8,128)}), f32[1,256,128]{2,1,0:T(8,128)}) %reduce-scatter.2.cloned.1.call-update) | async-done | bytes 131088 | tf_op jit(solution)/shard_map/reduce_scatter | solution.py:98
  142.4 63.8 %all-gather.2.cloned.1.call-done = bf16[16,256,128]{2,1,0:T(8,128)(2,1)} async-done(((bf16[1,256,128]{2,1,0:T(8,128)(2,1)}), bf16[16,256,128]{2,1,0:T(8,128)(2,1)}) %all-gather.2.cloned.1.call-update) | async-done | bytes 1048592 | tf_op jit(solution)/shard_map/all_gather | solution.py:101
  206.3 43.2 %while.27 = (s32[]{:T(128)}, f32[8,256,128]{2,1,0:T(8,128)S(1)}, s32[96]{0:T(128)S(1)}, pred[96]{0:T(512)(128)(4,1)S(1)}, bf16[96,256,256]{2,1,0:T(8,128)(2,1)},...) while((s32[]{:T(128)}, f32[8,256,128]{2,1,0:T(8,128)S(1)}, ...), condition=%wide.region_6.7_spmd, body=%wide.region_4.6_spmd.sunk | while | flops 540017984 | bytes 27268300 | solution.py:110
  208.6 5.5 %fusion.42 = f32[32,256,128]{2,1,0:T(8,128)} fusion(bf16[96,256,256]{2,1,0:T(8,128)(2,1)} %get-tuple-element.518, s32[]{:T(128)S(6)} %select_n.116, bf16[32,256,128]{2,1,0:T(8,128)(2,1)S(1)} %gather_fusion.1, pred[32]{0:T(512)(128)(4,1)S(1)} %get-tuple-element.458, pred[32]{0:T(512)(128)(4,1)S(1)} %dynamic_slice.81), kind=kOutput, calls=%fused_computation.18.clone.1 | convolution fusion | flops 538968064 | bytes 10485828 | tf_op jit(solution)/shard_map/while/body/eval_jaxpr/svr,src->svc/dot_general | solution.py:106
  214.2 6.4 %scatter_fusion.1 = f32[8,256,128]{2,1,0:T(8,128)S(1)} fusion(f32[8,256,128]{2,1,0:T(8,128)S(1)} %get-tuple-element.504, s32[32]{0:T(128)S(1)} %compare_select_fusion.25, f32[32,256,128]{2,1,0:T(8,128)} %fusion.42), kind=kCustom, calls=%fused_computation.3.clone.1 | custom fusion | flops 1048576 | bytes 12583040 | tf_op jit(solution)/shard_map/while/body/eval_jaxpr/scatter-add | solution.py:108
  223.0 5.5 %fusion.42 = f32[32,256,128]{2,1,0:T(8,128)} fusion(bf16[96,256,256]{2,1,0:T(8,128)(2,1)} %get-tuple-element.518, s32[]{:T(128)S(6)} %select_n.116, bf16[32,256,128]{2,1,0:T(8,128)(2,1)S(1)} %gather_fusion.1, pred[32]{0:T(512)(128)(4,1)S(1)} %get-tuple-element.458, pred[32]{0:T(512)(128)(4,1)S(1)} %dynamic_slice.81), kind=kOutput, calls=%fused_computation.18.clone.1 | convolution fusion | flops 538968064 | bytes 10485828 | tf_op jit(solution)/shard_map/while/body/eval_jaxpr/svr,src->svc/dot_general | solution.py:106
  228.6 6.5 %scatter_fusion.1 = f32[8,256,128]{2,1,0:T(8,128)S(1)} fusion(f32[8,256,128]{2,1,0:T(8,128)S(1)} %get-tuple-element.504, s32[32]{0:T(128)S(1)} %compare_select_fusion.25, f32[32,256,128]{2,1,0:T(8,128)} %fusion.42), kind=kCustom, calls=%fused_computation.3.clone.1 | custom fusion | flops 1048576 | bytes 12583040 | tf_op jit(solution)/shard_map/while/body/eval_jaxpr/scatter-add | solution.py:108
  237.4 5.5 %fusion.42 = f32[32,256,128]{2,1,0:T(8,128)} fusion(bf16[96,256,256]{2,1,0:T(8,128)(2,1)} %get-tuple-element.518, s32[]{:T(128)S(6)} %select_n.116, bf16[32,256,128]{2,1,0:T(8,128)(2,1)S(1)} %gather_fusion.1, pred[32]{0:T(512)(128)(4,1)S(1)} %get-tuple-element.458, pred[32]{0:T(512)(128)(4,1)S(1)} %dynamic_slice.81), kind=kOutput, calls=%fused_computation.18.clone.1 | convolution fusion | flops 538968064 | bytes 10485828 | tf_op jit(solution)/shard_map/while/body/eval_jaxpr/svr,src->svc/dot_general | solution.py:106
  243.0 6.4 %scatter_fusion.1 = f32[8,256,128]{2,1,0:T(8,128)S(1)} fusion(f32[8,256,128]{2,1,0:T(8,128)S(1)} %get-tuple-element.504, s32[32]{0:T(128)S(1)} %compare_select_fusion.25, f32[32,256,128]{2,1,0:T(8,128)} %fusion.42), kind=kCustom, calls=%fused_computation.3.clone.1 | custom fusion | flops 1048576 | bytes 12583040 | tf_op jit(solution)/shard_map/while/body/eval_jaxpr/scatter-add | solution.py:108
  255.2 4.1 %collective-permute-done.1 = f32[1,128,128]{2,1,0:T(8,128)S(1)} collective-permute-done((f32[1,128,128]{2,1,0:T(8,128)S(1)}, f32[1,128,128]{2,1,0:T(8,128)S(1)}, u32[]{:S(2)}, u32[]{:S(2)}) %collective-permute-start.1) | collective-permute-done | bytes 65568 | tf_op jit(solution)/shard_map/ppermute | solution.py:24
  262.7 5.4 %collective-permute-start.3 = (f32[18,128,1]{1,0,2:T(8,128)S(1)}, f32[18,128,1]{1,0,2:T(8,128)S(1)}, u32[]{:S(2)}, u32[]{:S(2)}) collective-permute-start(f32[18,128,1]{1,0,2:T(8,128)S(1)} %copy.82), channel_id=1, source_target_pairs={{1,0},{3,2},{5,4},{7,6},{9,8},{11,10},{13,12},{15,14},{17,16},{19,... | collective-permute-start | bytes 27656 | tf_op jit(solution)/shard_map/ppermute | solution.py:24
  285.2 4.0 %collective-permute-start.4 = (f32[1,128,128]{2,1,0:T(8,128)S(1)}, f32[1,128,128]{2,1,0:T(8,128)S(1)}, u32[]{:S(2)}, u32[]{:S(2)}) collective-permute-start(f32[1,128,128]{2,1,0:T(8,128)S(1)} %get-tuple-element.337), channel_id=1, source_target_pairs={{0,2},{2,4},{4,6},{6,8},{8,10},{10,12},{12,14},{14,16},{16,18},{18... | collective-permute-start | bytes 196616 | tf_op jit(solution)/shard_map/ppermute | solution.py:21
  297.7 3.7 collective-permute-start.7
  328.0 3.7 collective-permute-start.11
  351.8 4.3 %collective-permute-start.12 = (f32[1,128,128]{2,1,0:T(8,128)S(1)}, f32[1,128,128]{2,1,0:T(8,128)S(1)}, u32[]{:S(2)}, u32[]{:S(2)}) collective-permute-start(f32[1,128,128]{2,1,0:T(8,128)S(1)} %get-tuple-element.333), channel_id=1, source_target_pairs={{0,2},{2,4},{4,6},{6,8},{8,10},{10,12},{12,14},{14,16},{16,18},{18... | collective-permute-start | bytes 196616 | tf_op jit(solution)/shard_map/ppermute | solution.py:21
  364.5 3.8 collective-permute-start.15
  (205 shorter events, 131.7 us)
Async XLA Ops:
  7.2 4.0 %copy-start.27 = (s32[96]{0:T(128)S(1)}, s32[96]{0:T(128)}, u32[]{:S(2)}) copy-start(s32[96]{0:T(128)} %param.14) | copy-start | bytes 1156
  7.2 133.6 %reduce-scatter.2.cloned.1.call-start = ((), (), s32[]{:S(2)}) async-start(), calls=%async_computation.1 | async-start | bytes 2228224 | tf_op jit(solution)/shard_map/reduce_scatter | solution.py:98
  9.8 11.6 %copy-start.26 = (s32[96]{0:T(128)S(1)}, s32[96]{0:T(128)}, u32[]{:S(2)}) copy-start(s32[96]{0:T(128)} %param.13) | copy-start | bytes 1156
  21.4 119.3 %copy-start.25 = (f32[1,256,128]{2,1,0:T(8,128)S(1)}, f32[1,256,128]{2,1,0:T(8,128)}, u32[]{:S(2)}) copy-start(f32[1,256,128]{2,1,0:T(8,128)} %param.17) | copy-start | bytes 393220
  69.0 137.2 %all-gather.2.cloned.1.call-start = ((), (), s32[]{:S(2)}) async-start(), calls=%async_computation.2 | async-start | bytes 1114112 | tf_op jit(solution)/shard_map/all_gather | solution.py:101
  250.8 4.4 %collective-permute-start = (f32[1,128,128]{2,1,0:T(8,128)S(1)}, f32[1,128,128]{2,1,0:T(8,128)S(1)}, u32[]{:S(2)}, u32[]{:S(2)}) collective-permute-start(f32[1,128,128]{2,1,0:T(8,128)S(1)} %get-tuple-element.347), channel_id=1, source_target_pairs={{0,2},{2,4},{4,6},{6,8},{8,10},{10,12},{12,14},{14,16},{16,18},{18... | collective-permute-start | bytes 196616 | tf_op jit(solution)/shard_map/ppermute | solution.py:21
  253.9 5.4 %collective-permute-start.1 = (f32[1,128,128]{2,1,0:T(8,128)S(1)}, f32[1,128,128]{2,1,0:T(8,128)S(1)}, u32[]{:S(2)}, u32[]{:S(2)}) collective-permute-start(f32[1,128,128]{2,1,0:T(8,128)S(1)} %get-tuple-element.348), channel_id=1, source_target_pairs={{2,0},{4,2},{6,4},{8,6},{10,8},{12,10},{14,12},{16,14},{18,16},{20... | collective-permute-start | bytes 196616 | tf_op jit(solution)/shard_map/ppermute | solution.py:24
  260.9 7.3 %collective-permute-start.2 = (f32[18,128,1]{1,0,2:T(8,128)S(1)}, f32[18,128,1]{1,0,2:T(8,128)S(1)}, u32[]{:S(2)}, u32[]{:S(2)}) collective-permute-start(f32[18,128,1]{1,0,2:T(8,128)S(1)} %copy.81), channel_id=1, source_target_pairs={{0,1},{2,3},{4,5},{6,7},{8,9},{10,11},{12,13},{14,15},{16,17},{18,... | collective-permute-start | bytes 27656 | tf_op jit(solution)/shard_map/ppermute | solution.py:21
  262.7 5.9 %collective-permute-start.3 = (f32[18,128,1]{1,0,2:T(8,128)S(1)}, f32[18,128,1]{1,0,2:T(8,128)S(1)}, u32[]{:S(2)}, u32[]{:S(2)}) collective-permute-start(f32[18,128,1]{1,0,2:T(8,128)S(1)} %copy.82), channel_id=1, source_target_pairs={{1,0},{3,2},{5,4},{7,6},{9,8},{11,10},{13,12},{15,14},{17,16},{19,... | collective-permute-start | bytes 27656 | tf_op jit(solution)/shard_map/ppermute | solution.py:24
  285.2 5.7 %collective-permute-start.4 = (f32[1,128,128]{2,1,0:T(8,128)S(1)}, f32[1,128,128]{2,1,0:T(8,128)S(1)}, u32[]{:S(2)}, u32[]{:S(2)}) collective-permute-start(f32[1,128,128]{2,1,0:T(8,128)S(1)} %get-tuple-element.337), channel_id=1, source_target_pairs={{0,2},{2,4},{4,6},{6,8},{8,10},{10,12},{12,14},{14,16},{16,18},{18... | collective-permute-start | bytes 196616 | tf_op jit(solution)/shard_map/ppermute | solution.py:21
  289.3 5.0 %collective-permute-start.5 = (f32[1,128,128]{2,1,0:T(8,128)S(1)}, f32[1,128,128]{2,1,0:T(8,128)S(1)}, u32[]{:S(2)}, u32[]{:S(2)}) collective-permute-start(f32[1,128,128]{2,1,0:T(8,128)S(1)} %get-tuple-element.338), channel_id=1, source_target_pairs={{2,0},{4,2},{6,4},{8,6},{10,8},{12,10},{14,12},{16,14},{18,16},{20... | collective-permute-start | bytes 196616 | tf_op jit(solution)/shard_map/ppermute | solution.py:24
  295.9 5.4 %collective-permute-start.6 = (f32[18,128,1]{1,0,2:T(8,128)S(1)}, f32[18,128,1]{1,0,2:T(8,128)S(1)}, u32[]{:S(2)}, u32[]{:S(2)}) collective-permute-start(f32[18,128,1]{1,0,2:T(8,128)S(1)} %copy.89), channel_id=1, source_target_pairs={{0,1},{2,3},{4,5},{6,7},{8,9},{10,11},{12,13},{14,15},{16,17},{18,... | collective-permute-start | bytes 27656 | tf_op jit(solution)/shard_map/ppermute | solution.py:21
  297.7 4.3 %collective-permute-start.7 = (f32[18,128,1]{1,0,2:T(8,128)S(1)}, f32[18,128,1]{1,0,2:T(8,128)S(1)}, u32[]{:S(2)}, u32[]{:S(2)}) collective-permute-start(f32[18,128,1]{1,0,2:T(8,128)S(1)} %copy.90), channel_id=1, source_target_pairs={{1,0},{3,2},{5,4},{7,6},{9,8},{11,10},{13,12},{15,14},{17,16},{19,... | collective-permute-start | bytes 27656 | tf_op jit(solution)/shard_map/ppermute | solution.py:24
  318.5 4.4 %collective-permute-start.8 = (f32[1,128,128]{2,1,0:T(8,128)S(1)}, f32[1,128,128]{2,1,0:T(8,128)S(1)}, u32[]{:S(2)}, u32[]{:S(2)}) collective-permute-start(f32[1,128,128]{2,1,0:T(8,128)S(1)} %get-tuple-element.335), channel_id=1, source_target_pairs={{0,2},{2,4},{4,6},{6,8},{8,10},{10,12},{12,14},{14,16},{16,18},{18... | collective-permute-start | bytes 196616 | tf_op jit(solution)/shard_map/ppermute | solution.py:21
  321.4 5.0 %collective-permute-start.9 = (f32[1,128,128]{2,1,0:T(8,128)S(1)}, f32[1,128,128]{2,1,0:T(8,128)S(1)}, u32[]{:S(2)}, u32[]{:S(2)}) collective-permute-start(f32[1,128,128]{2,1,0:T(8,128)S(1)} %get-tuple-element.336), channel_id=1, source_target_pairs={{2,0},{4,2},{6,4},{8,6},{10,8},{12,10},{14,12},{16,14},{18,16},{20... | collective-permute-start | bytes 196616 | tf_op jit(solution)/shard_map/ppermute | solution.py:24
  328.0 5.7 %collective-permute-start.11 = (f32[18,128,1]{1,0,2:T(8,128)S(1)}, f32[18,128,1]{1,0,2:T(8,128)S(1)}, u32[]{:S(2)}, u32[]{:S(2)}) collective-permute-start(f32[18,128,1]{1,0,2:T(8,128)S(1)} %copy.98), channel_id=1, source_target_pairs={{1,0},{3,2},{5,4},{7,6},{9,8},{11,10},{13,12},{15,14},{17,16},{19,... | collective-permute-start | bytes 27656 | tf_op jit(solution)/shard_map/ppermute | solution.py:24
  332.1 3.1 collective-permute-start.10
  351.8 5.9 %collective-permute-start.12 = (f32[1,128,128]{2,1,0:T(8,128)S(1)}, f32[1,128,128]{2,1,0:T(8,128)S(1)}, u32[]{:S(2)}, u32[]{:S(2)}) collective-permute-start(f32[1,128,128]{2,1,0:T(8,128)S(1)} %get-tuple-element.333), channel_id=1, source_target_pairs={{0,2},{2,4},{4,6},{6,8},{8,10},{10,12},{12,14},{14,16},{16,18},{18... | collective-permute-start | bytes 196616 | tf_op jit(solution)/shard_map/ppermute | solution.py:21
  356.1 5.0 %collective-permute-start.13 = (f32[1,128,128]{2,1,0:T(8,128)S(1)}, f32[1,128,128]{2,1,0:T(8,128)S(1)}, u32[]{:S(2)}, u32[]{:S(2)}) collective-permute-start(f32[1,128,128]{2,1,0:T(8,128)S(1)} %get-tuple-element.334), channel_id=1, source_target_pairs={{2,0},{4,2},{6,4},{8,6},{10,8},{12,10},{14,12},{16,14},{18,16},{20... | collective-permute-start | bytes 196616 | tf_op jit(solution)/shard_map/ppermute | solution.py:24
  362.7 5.6 %collective-permute-start.14 = (f32[18,128,1]{1,0,2:T(8,128)S(1)}, f32[18,128,1]{1,0,2:T(8,128)S(1)}, u32[]{:S(2)}, u32[]{:S(2)}) collective-permute-start(f32[18,128,1]{1,0,2:T(8,128)S(1)} %copy.105), channel_id=1, source_target_pairs={{0,1},{2,3},{4,5},{6,7},{8,9},{10,11},{12,13},{14,15},{16,17},{18,... | collective-permute-start | bytes 27656 | tf_op jit(solution)/shard_map/ppermute | solution.py:21
  364.5 5.3 %collective-permute-start.15 = (f32[18,128,1]{1,0,2:T(8,128)S(1)}, f32[18,128,1]{1,0,2:T(8,128)S(1)}, u32[]{:S(2)}, u32[]{:S(2)}) collective-permute-start(f32[18,128,1]{1,0,2:T(8,128)S(1)} %copy.106), channel_id=1, source_target_pairs={{1,0},{3,2},{5,4},{7,6},{9,8},{11,10},{13,12},{15,14},{17,16},{19,... | collective-permute-start | bytes 27656 | tf_op jit(solution)/shard_map/ppermute | solution.py:24
  379.5 3.1 copy-start.2
  379.5 3.4 copy-start.3
  379.5 3.4 copy-start.14
  (22 other events, 38.8 us)
Sparse Core Ops, SparseCore 0:
  69.1 71.6 reduce-scatter.1
  144.1 62.0 all-gather.1
where the time goes:
time: 405 us; the launch traced here: 397 us
  waiting for transfers between devices  151 us (37%)
  other arithmetic  107 us (26%)
  local copies, waits for them, and re-layouts  45.2 us (11%)
  starting transfers between devices  41.3 us (10%)
  matrix products  35.9 us (9%)
  between operations  15.7 us (4%)
    reduce_scatter x1, waiting for transfers between devices, per_device(): lax.psum_scatter(partials, 'plane', scatter_dimension=0, tiled=True)  71.7 us
    all_gather x1, waiting for transfers between devices, per_device(): spread = lax.all_gather(residual, 'plane', axis=0, tiled=True)  63.8 us
    ppermute x8, starting transfers between devices, with_halo(): lax.ppermute(lax.slice_in_dim(block, 0, width, axis=dim), axis, backward)  21.7 us
    ppermute x8, starting transfers between devices, with_halo(): lax.ppermute(lax.slice_in_dim(block, block.shape[dim] - width, None, axis...  19.5 us
    scatter-add x3, other arithmetic, forward(): return running.at[owners].add(product)  19.4 us
    dot_general x3, matrix products, forward(): jnp.einsum('svr,svc->src', weights, values, preferred_element_type=jnp.fl...  19.4 us
    scatter-add x3, other arithmetic, backward(): return running.at[tile_ids].add(product)  19.4 us
    dot_general x3, matrix products, backward(): jnp.einsum('svr,src->svc', weights, values, preferred_element_type=jnp.fl...  16.5 us
  transfers between devices with their start and end apart: 18, of which 8 were waited for; matrix products, arithmetic and copies ran while one was open for 1% of the time, Pallas kernels for 0%

commit v1 on v0

v1 whole, which is shorter than its diff:
```python
import functools

import jax
import jax.numpy as jnp
from jax import lax
from jax.experimental import pallas as pl
from jax.experimental.pallas import tpu as pltpu
from jax.sharding import PartitionSpec as P

TILE = 16
SWEEPS = 4
EDGE = 8
GROUP = 8

smooth_square = 0.09
flow_step = 0.04
relax_step = 4.0

SMEM = pl.BlockSpec(memory_space=pltpu.SMEM)
VMEM = pl.BlockSpec(memory_space=pltpu.VMEM)
ANY = pl.BlockSpec(memory_space=pl.ANY)
PARAMS = pltpu.CompilerParams(vmem_limit_bytes=48 * 1024 * 1024)


def relative_block(bits, position):
    block = 0
    for stage, bit in enumerate(bits):
        block |= ((position >> (len(bits) - 1 - stage)) & 1) << bit
    return block


def weight_copies(weights, held, sems):
    slots = held.shape[0]
    return [
        pltpu.make_async_copy(
            weights.at[pl.ds(first, GROUP)], held.at[pl.ds(first, GROUP)], sems.at[first // GROUP]
        )
        for first in range(0, slots, GROUP)
    ]


def forward_kernel(
    orders, me, tile_ids, blocks, owner, count, image, weights,
    a_keep, a_send, b_keep, b_send, pixels, held, turned, total, image_sem, sems,
):
    slots, voxels, rays = held.shape
    parts = total.shape[0] - 1
    half = rays // 2
    image_copy = pltpu.make_async_copy(image, pixels, image_sem)
    image_copy.start()
    for copy in weight_copies(weights, held, sems):
        copy.start()
    total[...] = jnp.zeros_like(total)
    image_copy.wait()
    for t in range(turned.shape[0]):
        tile = pixels[:, t * TILE : (t + 1) * TILE, :].reshape(voxels, pixels.shape[2])
        turned[t] = tile.T.astype(jnp.bfloat16)

    def step(group, carry):
        first = pl.multiple_of(group * GROUP, GROUP)
        pltpu.make_async_copy(
            weights.at[pl.ds(first, GROUP)], held.at[pl.ds(first, GROUP)], sems.at[group]
        ).wait()
        for k in range(GROUP):
            s = first + k
            to = jnp.where(s < count[0], owner[blocks[s]] ^ me[0], parts)
            total[to] += jnp.dot(
                turned[tile_ids[s]], held[s], preferred_element_type=jnp.float32
            )
        return carry

    lax.fori_loop(0, slots // GROUP, step, 0)
    for keep, send, order, low in ((a_keep, a_send, orders[0], 0), (b_keep, b_send, orders[1], half)):
        for p in range(parts // 2):
            keep[p] = total[relative_block(order, p), :, low : low + half]
            send[p] = total[relative_block(order, p + parts // 2), :, low : low + half].astype(jnp.bfloat16)


def residual_kernel(low, keep, got, measured, residual):
    half = residual.shape[1]
    projection = (keep[0] + got[0].astype(jnp.float32)).T
    mismatch = measured[0, low : low + half, :] - projection
    residual[0] = (mismatch / jnp.sqrt(1.0 + mismatch * mismatch)).astype(jnp.bfloat16)


def backward_kernel(
    orders, me, cut, tile_ids, blocks, owner, count, a_low, a_high, b_low, b_high, image, weights,
    relaxed, first_rows, last_rows, strip, pixels, held, spread, total, image_sem, sems,
):
    slots, voxels, rays = held.shape
    parts = spread.shape[0]
    tiles = total.shape[0] - 1
    half = rays // 2
    rows, cols, slices = relaxed.shape
    image_copy = pltpu.make_async_copy(image, pixels, image_sem)
    image_copy.start()
    for copy in weight_copies(weights, held, sems):
        copy.start()
    total[...] = jnp.zeros_like(total)
    for p in range(parts // 2):
        spread[relative_block(orders[0], p), :half] = a_low[p]
        spread[relative_block(orders[0], p + parts // 2), :half] = a_high[p]
        spread[relative_block(orders[1], p), half:] = b_low[p]
        spread[relative_block(orders[1], p + parts // 2), half:] = b_high[p]

    def step(group, carry):
        first = pl.multiple_of(group * GROUP, GROUP)
        pltpu.make_async_copy(
            weights.at[pl.ds(first, GROUP)], held.at[pl.ds(first, GROUP)], sems.at[group]
        ).wait()
        for k in range(GROUP):
            s = first + k
            to = jnp.where(s < count[0], tile_ids[s], tiles)
            total[to] += jnp.dot(
                held[s], spread[owner[blocks[s]] ^ me[0]], preferred_element_type=jnp.float32
            )
        return carry

    lax.fori_loop(0, slots // GROUP, step, 0)
    image_copy.wait()
    for t in range(tiles):
        span = slice(t * TILE, (t + 1) * TILE)
        update = total[t].reshape(rows, TILE, slices)
        relaxed[:, span, :] = jnp.maximum(pixels[:, span, :] + relax_step * update, 0.0)
    for i in range(SWEEPS):
        first_rows[i * cols : (i + 1) * cols] = relaxed[i].astype(jnp.bfloat16)
        last_rows[i * cols : (i + 1) * cols] = relaxed[rows - SWEEPS + i].astype(jnp.bfloat16)
    lane = lax.broadcasted_iota(jnp.int32, (cols, slices), 1)
    start = jnp.where(cut[0] == 0, slices - EDGE, 0)
    edges = jnp.zeros((cols, slices), jnp.float32)
    for i in range(rows):
        moved = pltpu.roll(relaxed[i], (i * EDGE - start + slices) % slices, 1)
        edges = jnp.where(lane // EDGE == i, moved, edges)
    strip[...] = edges.T.reshape(rows, EDGE, cols)


def shifted(x, axis, by):
    size = x.shape[axis]
    place = lax.broadcasted_iota(jnp.int32, x.shape, axis)
    if by > 0:
        return jnp.where(place == 0, 0.0, pltpu.roll(x, 1, axis))
    return jnp.where(place == size - 1, 0.0, pltpu.roll(x, size - 1, axis))


def flows(cell, below):
    rise_rows = below - cell
    rise_inner = shifted(cell, 0, -1) - cell
    rise_outer = shifted(cell, 1, -1) - cell
    scale = lax.rsqrt(
        smooth_square + rise_rows * rise_rows + rise_inner * rise_inner + rise_outer * rise_outer
    )
    return rise_rows * scale, rise_inner * scale, rise_outer * scale


def sweeps_over(field, rows, has_low, has_high):
    for sweep in range(1, SWEEPS + 1):

        @pl.when(has_low == 0)
        def _():
            field[SWEEPS - 1] = field[SWEEPS]

        @pl.when(has_high == 0)
        def _():
            field[SWEEPS + rows] = jnp.zeros(field.shape[1:], field.dtype)

        def body(i, before):
            cell = field[i]
            flow_rows, flow_inner, flow_outer = flows(cell, field[i + 1])
            diverge = flow_rows - before
            diverge = diverge + (flow_inner - shifted(flow_inner, 0, 1))
            diverge = diverge + (flow_outer - shifted(flow_outer, 1, 1))
            field[i] = cell + flow_step * diverge
            return flow_rows

        before = flows(field[sweep - 1], field[sweep])[0]
        lax.fori_loop(sweep, rows + 2 * SWEEPS - sweep, body, before)


def sweep_kernel(me, cut, relaxed, strip, from_low, from_high, volume, field, narrow, *, planes):
    rows, cols, slices = relaxed.shape
    body = SWEEPS * cols
    field[SWEEPS : SWEEPS + rows] = relaxed[...]
    narrow[SWEEPS : SWEEPS + rows] = strip[...]
    for start, halo in ((0, from_low), (SWEEPS + rows, from_high)):
        field[start : start + SWEEPS] = halo[:body].astype(jnp.float32).reshape(SWEEPS, cols, slices)
        narrow[start : start + SWEEPS] = (
            halo[body:].astype(jnp.float32).reshape(SWEEPS, 2 * EDGE, cols)
        )
    has_low = (me[0] > 0).astype(jnp.int32)
    has_high = (me[0] < planes - 1).astype(jnp.int32)
    sweeps_over(narrow, rows, has_low, has_high)
    sweeps_over(field, rows, has_low, has_high)
    low_side = cut[0] == 0
    mine = narrow[SWEEPS : SWEEPS + rows]
    mine = jnp.where(low_side, mine[:, :EDGE], mine[:, EDGE:])
    turned = mine.reshape(rows * EDGE, cols).T
    lane = lax.broadcasted_iota(jnp.int32, (cols, slices), 1)
    start = jnp.where(low_side, slices - EDGE, 0)
    first = jnp.where(low_side, slices - SWEEPS, 0)
    patch = (lane >= first) & (lane < first + SWEEPS)
    for i in range(rows):
        moved = pltpu.roll(turned, (start - i * EDGE + slices) % slices, 1)
        volume[i] = jnp.where(patch, moved, field[SWEEPS + i])


def sum_chain(keep, send, order, planes):
    for stage, bit in enumerate(order):
        got = lax.ppermute(send, "plane", [(i, i ^ (1 << bit)) for i in range(planes)])
        if stage == len(order) - 1:
            return keep, got
        total = keep + got.astype(jnp.float32)
        left = total.shape[0] // 2
        keep, send = total[:left], total[left:].astype(jnp.bfloat16)


def spread_chain(piece, order, planes):
    for stage, bit in reversed(list(enumerate(order))):
        got = lax.ppermute(piece, "plane", [(i, i ^ (1 << bit)) for i in range(planes)])
        if stage == 0:
            return piece, got
        piece = jnp.concatenate([piece, got], axis=0)


def per_device(
    image,
    projection_weight_tiles,
    pair_tile_index,
    pair_ray_block,
    ray_owner,
    active_pair_count,
    measured,
):
    rows, cols, slices = image.shape
    slots, voxels, rays = projection_weight_tiles.shape
    tiles = (rows // TILE) * (cols // TILE)
    planes = lax.axis_size("plane")
    parts = ray_owner.shape[0]
    half = rays // 2
    bits = planes.bit_length() - 1
    plain = tuple(range(bits))
    swapped = (1, 0) + plain[2:]
    orders = (plain, swapped)
    me = lax.axis_index("plane").astype(jnp.int32).reshape(1)
    cut = lax.axis_index("cuts").astype(jnp.int32).reshape(1)
    shape = jax.ShapeDtypeStruct
    f32, bf16 = jnp.float32, jnp.bfloat16

    kept, sent = shape((parts // 2, slices, half), f32), shape((parts // 2, slices, half), bf16)
    a_keep, a_send, b_keep, b_send = pl.pallas_call(
        functools.partial(forward_kernel, orders),
        out_shape=(kept, sent, kept, sent),
        in_specs=[SMEM] * 5 + [ANY, ANY],
        out_specs=(VMEM,) * 4,
        scratch_shapes=[
            pltpu.VMEM((rows, cols, slices), f32),
            pltpu.VMEM((slots, voxels, rays), bf16),
            pltpu.VMEM((tiles, slices, voxels), bf16),
            pltpu.VMEM((parts + 1, slices, rays), f32),
            pltpu.SemaphoreType.DMA,
            pltpu.SemaphoreType.DMA((slots // GROUP,)),
        ],
        compiler_params=PARAMS,
        name="forward",
    )(me, pair_tile_index, pair_ray_block, ray_owner, active_pair_count, image, projection_weight_tiles)

    pieces = []
    for low, keep, send, order in ((0, a_keep, a_send, plain), (half, b_keep, b_send, swapped)):
        keep, got = sum_chain(keep, send, order, planes)
        pieces.append(
            pl.pallas_call(
                functools.partial(residual_kernel, low),
                out_shape=shape((1, half, slices), bf16),
                in_specs=[VMEM] * 3,
                out_specs=VMEM,
                name="residual",
            )(keep, got, measured)
        )
    residual = jnp.concatenate(pieces, axis=1)
    a_low, a_high = spread_chain(pieces[0], plain, planes)
    b_low, b_high = spread_chain(pieces[1], swapped, planes)

    relaxed, first_rows, last_rows, strip = pl.pallas_call(
        functools.partial(backward_kernel, orders),
        out_shape=(
            shape((rows, cols, slices), f32),
            shape((SWEEPS * cols, slices), bf16),
            shape((SWEEPS * cols, slices), bf16),
            shape((rows, EDGE, cols), f32),
        ),
        in_specs=[SMEM] * 6 + [VMEM] * 4 + [ANY, ANY],
        out_specs=(VMEM,) * 4,
        scratch_shapes=[
            pltpu.VMEM((rows, cols, slices), f32),
            pltpu.VMEM((slots, voxels, rays), bf16),
            pltpu.VMEM((parts, rays, slices), bf16),
            pltpu.VMEM((tiles + 1, voxels, slices), f32),
            pltpu.SemaphoreType.DMA,
            pltpu.SemaphoreType.DMA((slots // GROUP,)),
        ],
        compiler_params=PARAMS,
        name="backward",
    )(
        me, cut, pair_tile_index, pair_ray_block, ray_owner, active_pair_count,
        a_low, a_high, b_low, b_high, image, projection_weight_tiles,
    )

    other = lax.ppermute(strip, "cuts", [(0, 1), (1, 0)])
    both = jnp.where(
        cut[0] == 0, jnp.concatenate([strip, other], 1), jnp.concatenate([other, strip], 1)
    )

    def with_strip(main, part):
        return jnp.concatenate([main, part.astype(bf16).reshape(-1, cols)], axis=0)

    upward = [(i, i + 1) for i in range(planes - 1)]
    downward = [(i + 1, i) for i in range(planes - 1)]
    from_low = lax.ppermute(with_strip(last_rows, both[rows - SWEEPS :]), "plane", upward)
    from_high = lax.ppermute(with_strip(first_rows, both[:SWEEPS]), "plane", downward)

    volume = pl.pallas_call(
        functools.partial(sweep_kernel, planes=planes),
        out_shape=shape((rows, cols, slices), f32),
        in_specs=[SMEM, SMEM] + [VMEM] * 4,
        out_specs=VMEM,
        scratch_shapes=[
            pltpu.VMEM((rows + 2 * SWEEPS, cols, slices), f32),
            pltpu.VMEM((rows + 2 * SWEEPS, 2 * EDGE, cols), f32),
        ],
        compiler_params=PARAMS,
        name="sweeps",
    )(me, cut, relaxed, both, from_low, from_high)
    return (volume, residual)


def solution(mesh):
    placed = (
        P("plane", None, "cuts"),
        P("plane", None, None),
        P("plane"),
        P("plane"),
        P(),
        P("plane"),
        P("plane", None, "cuts"),
    )
    return jax.shard_map(
        per_device,
        mesh=mesh,
        in_specs=placed,
        out_specs=(P("plane", None, "cuts"), P("plane", None, "cuts")),
        check_vma=False,
    )
```

time: 405 us -> 115 us (0.28); the launches traced: 397 us -> 114 us
  waiting for transfers between devices: 151 us -> 22.3 us
  other arithmetic: 107 us -> 5.53 us
  Pallas kernels: 0 us -> 43.8 us
  local copies, waits for them, and re-layouts: 45.2 us -> 5.78 us
  matrix products: 35.9 us -> 0 us
  between operations: 15.7 us -> 1.53 us
  starting transfers between devices: 41.3 us -> 34.5 us
    reduce_scatter x1 -> x0, waiting for transfers between devices: 71.7 us -> none  [per_device(): lax.psum_scatter(partials, 'plane', scatter_dimension=0, tiled=True)]
    all_gather x1 -> x0, waiting for transfers between devices: 63.8 us -> none  [per_device(): spread = lax.all_gather(residual, 'plane', axis=0, tiled=True)]
    pallas_call x0 -> x5, Pallas kernels: none -> 43.8 us  [the longest x1 26.8 us: per_device(): pl.pallas_call(functools.partial(sweep_kernel, planes=planes), out_shape=...]
    scatter-add x6 -> x0, other arithmetic: 38.8 us -> none  [the longest x3 19.4 us: forward(): return running.at[owners].add(product)]
    dot_general x6 -> x0, matrix products: 35.9 us -> none  [the longest x3 19.4 us: forward(): jnp.einsum('svr,svc->src', weights, values, preferred_element_type=jnp.fl...]
    sub x12 -> x0, other arithmetic: 20.8 us -> none  [the longest x4 7.59 us: smooth_sweep(): volume[:, :, 1:] - volume[:, :, :-1]]
    mul x9 -> x0, other arithmetic: 19.6 us -> none  [the longest x4 11 us: smooth_sweep(): return (volume + flow_step * diverge) * inside]
    gather x7 -> x0, local copies, waits for them, and re-layouts: 15 us -> none  [the longest x3 6.53 us: backward(): values = jnp.take(spread, owners, axis=0)]
  transfers between devices with their start and end apart: 18 -> 19, of which waited for: 8 -> 11; matrix products, arithmetic and copies ran while one was open for 1% -> 6% of each run, Pallas kernels for 0% -> 3%
where the time goes in v1:
time: 115 us; the launch traced here: 114 us
  Pallas kernels  43.8 us (38%)
  starting transfers between devices  34.5 us (30%)
  waiting for transfers between devices  22.3 us (19%)
  local copies, waits for them, and re-layouts  5.78 us (5%)
  other arithmetic  5.53 us (5%)
  between operations  1.53 us (1%)
    pallas_call x1, Pallas kernels, per_device(): pl.pallas_call(functools.partial(sweep_kernel, planes=planes), out_shape=...  26.8 us
    ppermute x8, starting transfers between devices, sum_chain(): lax.ppermute(send, 'plane', [(i, i ^ 1 << bit) for i in range(planes)])  12.1 us
    ppermute x8, starting transfers between devices, spread_chain(): lax.ppermute(piece, 'plane', [(i, i ^ 1 << bit) for i in range(planes)])  10.2 us
    ppermute x1, starting transfers between devices, per_device(): other = lax.ppermute(strip, 'cuts', [(0, 1), (1, 0)])  8.13 us
    ppermute x8, waiting for transfers between devices, spread_chain(): lax.ppermute(piece, 'plane', [(i, i ^ 1 << bit) for i in range(planes)])  7.78 us
    pallas_call x1, Pallas kernels, per_device(): pl.pallas_call(functools.partial(backward_kernel, orders), out_shape=(sha...  7.68 us
    ppermute x8, waiting for transfers between devices, sum_chain(): lax.ppermute(send, 'plane', [(i, i ^ 1 << bit) for i in range(planes)])  6.81 us
    ppermute x1, waiting for transfers between devices, per_device(): lax.ppermute(with_strip(first_rows, both[:SWEEPS]), 'plane', downward)  5.96 us
  transfers between devices with their start and end apart: 19, of which 11 were waited for; matrix products, arithmetic and copies ran while one was open for 6% of the time, Pallas kernels for 3%

profile of v1, /device:TPU:1, one launch (start us, length us, event | category | flops | bytes accessed | tf_op | source)
XLA Modules:
  0.0 113.5 jit_solution(8962500532269319699)
XLA Ops:
  4.5 5.9 %forward.1 = (f32[8,128,128]{2,1,0:T(8,128)S(1)}, bf16[8,128,128]{2,1,0:T(8,128)(2,1)S(1)}, f32[8,128,128]{2,1,0:T(8,128)S(1)}, bf16[8,128,128]{2,1,0:T(8,128)(2,1)S(1)}) custom-call(s32[1]{0:T(128)} %bitcast.me, s32[96]{0:T(128)S(1)} %copy-done.2, s32[96]{0:T(128)S(1)} %copy-done.4, s32[16]{0:T(128)S(1)} %copy-done.6, s32[1]{0:T(128)S(6)} %copy.9.count, ...), custom_call_target="tpu_custom_call" | custom-call | tf_op jit(solution)/shard_map/forward/pallas_call | solution.py:249
  10.5 2.1 %collective-permute-start = (bf16[8,128,128]{2,1,0:T(8,128)(2,1)S(1)}, bf16[8,128,128]{2,1,0:T(8,128)(2,1)S(1)}, u32[]{:S(2)}, u32[]{:S(2)}) collective-permute-start(bf16[8,128,128]{2,1,0:T(8,128)(2,1)S(1)} %get-tuple-element.11), channel_id=1, source_target_pairs={{0,2},{2,0},{4,6},{6,4},{8,10},{10,8},{12,14},{14,12},{16,18},{18,... | collective-permute-start | bytes 786440 | tf_op jit(solution)/shard_map/ppermute | solution.py:208
  13.8 4.8 %collective-permute-done = bf16[8,128,128]{2,1,0:T(8,128)(2,1)S(1)} collective-permute-done((bf16[8,128,128]{2,1,0:T(8,128)(2,1)S(1)}, bf16[8,128,128]{2,1,0:T(8,128)(2,1)S(1)}, u32[]{:S(2)}, u32[]{:S(2)}) %collective-permute-start) | collective-permute-done | bytes 262176 | tf_op jit(solution)/shard_map/ppermute | solution.py:208
  22.6 1.3 %collective-permute-start.2 = (bf16[2,128,128]{2,1,0:T(8,128)(2,1)S(1)}, bf16[2,128,128]{2,1,0:T(8,128)(2,1)S(1)}, u32[]{:S(2)}, u32[]{:S(2)}) collective-permute-start(bf16[2,128,128]{2,1,0:T(8,128)(2,1)S(1)} %slice.91), channel_id=1, source_target_pairs={{0,8},{2,10},{4,12},{6,14},{8,0},{10,2},{12,4},{14,6},{16,24},{18,... | collective-permute-start | bytes 196616 | tf_op jit(solution)/shard_map/ppermute | solution.py:208
  24.3 1.4 %collective-permute-start.10 = (bf16[2,128,128]{2,1,0:T(8,128)(2,1)S(1)}, bf16[2,128,128]{2,1,0:T(8,128)(2,1)S(1)}, u32[]{:S(2)}, u32[]{:S(2)}) collective-permute-start(bf16[2,128,128]{2,1,0:T(8,128)(2,1)S(1)} %slice.90), channel_id=1, source_target_pairs={{0,8},{2,10},{4,12},{6,14},{8,0},{10,2},{12,4},{14,6},{16,24},{18,... | collective-permute-start | bytes 196616 | tf_op jit(solution)/shard_map/ppermute | solution.py:208
  26.1 2.3 %collective-permute-start.3 = (bf16[1,128,128]{2,1,0:T(8,128)(2,1)S(1)}, bf16[1,128,128]{2,1,0:T(8,128)(2,1)S(1)}, u32[]{:S(2)}, u32[]{:S(2)}) collective-permute-start(bf16[1,128,128]{2,1,0:T(8,128)(2,1)S(1)} %slice.93), channel_id=1, source_target_pairs={{0,16},{2,18},{4,20},{6,22},{8,24},{10,26},{12,28},{14,30},{16,0},... | collective-permute-start | bytes 98312 | tf_op jit(solution)/shard_map/ppermute | solution.py:208
  29.1 1.3 %collective-permute-start.11 = (bf16[1,128,128]{2,1,0:T(8,128)(2,1)S(1)}, bf16[1,128,128]{2,1,0:T(8,128)(2,1)S(1)}, u32[]{:S(2)}, u32[]{:S(2)}) collective-permute-start(bf16[1,128,128]{2,1,0:T(8,128)(2,1)S(1)} %slice.92), channel_id=1, source_target_pairs={{0,16},{2,18},{4,20},{6,22},{8,24},{10,26},{12,28},{14,30},{16,0},... | collective-permute-start | bytes 98312 | tf_op jit(solution)/shard_map/ppermute | solution.py:208
  31.0 1.7 %residual.2 = bf16[1,128,128]{2,1,0:T(8,128)(2,1)} custom-call(f32[1,128,128]{2,1,0:T(8,128)} %slice.68.keep, bf16[1,128,128]{2,1,0:T(8,128)(2,1)} %copy-done.10, f32[1,256,128]{2,1,0:T(8,128)} %measured.3), custom_call_target="tpu_custom_call" | custom-call | tf_op jit(solution)/shard_map/residual/pallas_call | solution.py:270
  32.7 1.7 %collective-permute-start.4 = (bf16[1,128,128]{2,1,0:T(8,128)(2,1)}, bf16[1,128,128]{2,1,0:T(8,128)(2,1)S(1)}, u32[]{:S(2)}, u32[]{:S(2)}) collective-permute-start(bf16[1,128,128]{2,1,0:T(8,128)(2,1)} %residual.2), channel_id=1, source_target_pairs={{0,16},{2,18},{4,20},{6,22},{8,24},{10,26},{12,28},{14,30},{16,0},... | collective-permute-start | bytes 98312 | tf_op jit(solution)/shard_map/ppermute | solution.py:218
  35.7 1.7 %residual.3 = bf16[1,128,128]{2,1,0:T(8,128)(2,1)} custom-call(f32[1,128,128]{2,1,0:T(8,128)} %slice.74.keep, bf16[1,128,128]{2,1,0:T(8,128)(2,1)} %copy-done.11, f32[1,256,128]{2,1,0:T(8,128)} %measured.3), custom_call_target="tpu_custom_call" | custom-call | tf_op jit(solution)/shard_map/residual/pallas_call | solution.py:270
  38.8 1.3 %collective-permute-start.5 = (bf16[2,128,128]{2,1,0:T(8,128)(2,1)S(1)}, bf16[2,128,128]{2,1,0:T(8,128)(2,1)S(1)}, u32[]{:S(2)}, u32[]{:S(2)}) collective-permute-start(bf16[2,128,128]{2,1,0:T(8,128)(2,1)S(1)} %pad_maximum_fusion.6), channel_id=1, source_target_pairs={{0,8},{2,10},{4,12},{6,14},{8,0},{10,2},{12,4},{14,6},{16,24},{18,... | collective-permute-start | bytes 196616 | tf_op jit(solution)/shard_map/ppermute | solution.py:218
  40.1 1.6 %collective-permute-done.12 = bf16[1,128,128]{2,1,0:T(8,128)(2,1)S(1)} collective-permute-done((bf16[1,128,128]{2,1,0:T(8,128)(2,1)}, bf16[1,128,128]{2,1,0:T(8,128)(2,1)S(1)}, u32[]{:S(2)}, u32[]{:S(2)}) %collective-permute-start.12) | collective-permute-done | bytes 32800 | tf_op jit(solution)/shard_map/ppermute | solution.py:218
  42.5 1.4 %collective-permute-start.13 = (bf16[2,128,128]{2,1,0:T(8,128)(2,1)S(1)}, bf16[2,128,128]{2,1,0:T(8,128)(2,1)S(1)}, u32[]{:S(2)}, u32[]{:S(2)}) collective-permute-start(bf16[2,128,128]{2,1,0:T(8,128)(2,1)S(1)} %pad_maximum_fusion.7), channel_id=1, source_target_pairs={{0,8},{2,10},{4,12},{6,14},{8,0},{10,2},{12,4},{14,6},{16,24},{18,... | collective-permute-start | bytes 196616 | tf_op jit(solution)/shard_map/ppermute | solution.py:218
  46.6 1.4 %collective-permute-start.14 = (bf16[4,128,128]{2,1,0:T(8,128)(2,1)S(1)}, bf16[4,128,128]{2,1,0:T(8,128)(2,1)S(1)}, u32[]{:S(2)}, u32[]{:S(2)}) collective-permute-start(bf16[4,128,128]{2,1,0:T(8,128)(2,1)S(1)} %pad_maximum_fusion.5), channel_id=1, source_target_pairs={{0,2},{2,0},{4,6},{6,4},{8,10},{10,8},{12,14},{14,12},{16,18},{18,... | collective-permute-start | bytes 393224 | tf_op jit(solution)/shard_map/ppermute | solution.py:218
  49.3 1.3 %collective-permute-start.7 = (bf16[8,128,128]{2,1,0:T(8,128)(2,1)S(1)}, bf16[8,128,128]{2,1,0:T(8,128)(2,1)S(1)}, u32[]{:S(2)}, u32[]{:S(2)}) collective-permute-start(bf16[8,128,128]{2,1,0:T(8,128)(2,1)S(1)} %pad_maximum_fusion.a_low), channel_id=1, source_target_pairs={{0,2},{2,0},{4,6},{6,4},{8,10},{10,8},{12,14},{14,12},{16,18},{18,... | collective-permute-start | bytes 786440 | tf_op jit(solution)/shard_map/ppermute | solution.py:218
  51.4 1.3 %collective-permute-start.15 = (bf16[8,128,128]{2,1,0:T(8,128)(2,1)S(1)}, bf16[8,128,128]{2,1,0:T(8,128)(2,1)S(1)}, u32[]{:S(2)}, u32[]{:S(2)}) collective-permute-start(bf16[8,128,128]{2,1,0:T(8,128)(2,1)S(1)} %pad_maximum_fusion.1.b_low), channel_id=1, source_target_pairs={{0,4},{2,6},{4,0},{6,2},{8,12},{10,14},{12,8},{14,10},{16,20},{18,... | collective-permute-start | bytes 786440 | tf_op jit(solution)/shard_map/ppermute | solution.py:218
  52.7 2.2 %collective-permute-done.7.a_high = bf16[8,128,128]{2,1,0:T(8,128)(2,1)S(1)} collective-permute-done((bf16[8,128,128]{2,1,0:T(8,128)(2,1)S(1)}, bf16[8,128,128]{2,1,0:T(8,128)(2,1)S(1)}, u32[]{:S(2)}, u32[]{:S(2)}) %collective-permute-start.7) | collective-permute-done | bytes 262176 | tf_op jit(solution)/shard_map/ppermute | solution.py:218
  54.9 3.4 %collective-permute-done.15.b_high = bf16[8,128,128]{2,1,0:T(8,128)(2,1)S(1)} collective-permute-done((bf16[8,128,128]{2,1,0:T(8,128)(2,1)S(1)}, bf16[8,128,128]{2,1,0:T(8,128)(2,1)S(1)}, u32[]{:S(2)}, u32[]{:S(2)}) %collective-permute-start.15) | collective-permute-done | bytes 262176 | tf_op jit(solution)/shard_map/ppermute | solution.py:218
  58.3 7.7 %backward.1 = (f32[16,128,128]{2,1,0:T(8,128)S(1)}, bf16[512,128]{1,0:T(8,128)(2,1)S(1)}, bf16[512,128]{1,0:T(8,128)(2,1)S(1)}, f32[16,8,128]{2,1,0:T(8,128)S(1)}) custom-call(s32[1]{0:T(128)} %bitcast.me, s32[1]{0:T(128)} %bitcast.1.cut, s32[96]{0:T(128)S(1)} %copy-done.3, s32[96]{0:T(128)S(1)} %copy-done.5, s32[16]{0:T(128)S(1)} %copy-done.7, ...), custom_call_target="tpu_custom_call" | custom-call | tf_op jit(solution)/shard_map/backward/pallas_call | solution.py:282
  66.0 8.1 %collective-permute-start.16 = (f32[16,8,128]{2,1,0:T(8,128)S(1)}, f32[16,8,128]{2,1,0:T(8,128)S(1)}, u32[]{:S(2)}, u32[]{:S(2)}) collective-permute-start(f32[16,8,128]{2,1,0:T(8,128)S(1)} %get-tuple-element.15), channel_id=1, source_target_pairs={{0,1},{1,0},{2,3},{3,2},{4,5},{5,4},{6,7},{7,6},{8,9},{9,8},{10,11... | collective-permute-start | bytes 196616 | tf_op jit(solution)/shard_map/ppermute | solution.py:307
  75.1 2.8 %collective-permute-start.17 = (bf16[576,128]{1,0:T(8,128)(2,1)S(1)}, bf16[576,128]{1,0:T(8,128)(2,1)S(1)}, u32[]{:S(2)}, u32[]{:S(2)}) collective-permute-start(bf16[576,128]{1,0:T(8,128)(2,1)S(1)} %pad_maximum_fusion.2), channel_id=1, source_target_pairs={{0,2},{2,4},{4,6},{6,8},{8,10},{10,12},{12,14},{14,16},{16,18},{18... | collective-permute-start | bytes 442376 | tf_op jit(solution)/shard_map/ppermute | solution.py:317
  77.9 1.3 %collective-permute-start.18 = (bf16[576,128]{1,0:T(8,128)(2,1)S(1)}, bf16[576,128]{1,0:T(8,128)(2,1)S(1)}, u32[]{:S(2)}, u32[]{:S(2)}) collective-permute-start(bf16[576,128]{1,0:T(8,128)(2,1)S(1)} %pad_maximum_fusion.3), channel_id=1, source_target_pairs={{2,0},{4,2},{6,4},{8,6},{10,8},{12,10},{14,12},{16,14},{18,16},{20... | collective-permute-start | bytes 442376 | tf_op jit(solution)/shard_map/ppermute | solution.py:318
  80.7 6.0 %collective-permute-done.18.from_high = bf16[576,128]{1,0:T(8,128)(2,1)S(1)} collective-permute-done((bf16[576,128]{1,0:T(8,128)(2,1)S(1)}, bf16[576,128]{1,0:T(8,128)(2,1)S(1)}, u32[]{:S(2)}, u32[]{:S(2)}) %collective-permute-start.18) | collective-permute-done | bytes 147488 | tf_op jit(solution)/shard_map/ppermute | solution.py:318
  86.7 26.8 %sweeps.1 = f32[16,128,128]{2,1,0:T(8,128)} custom-call(s32[1]{0:T(128)} %bitcast.me, s32[1]{0:T(128)} %bitcast.1.cut, f32[16,128,128]{2,1,0:T(8,128)S(1)} %get-tuple-element.14.relaxed, f32[16,16,128]{2,1,0:T(8,128)S(1)} %get-tuple-element.19.strip, bf16[576,128]{1,0:T(8,128)(2,1)S(1)} %collective-permute-done.17.from_low, ...), custom_call_target="tpu_custom_call" | custom-call | tf_op jit(solution)/shard_map/sweeps/pallas_call | solution.py:320
  (68 shorter events, 21.2 us)
Async XLA Ops:
  0.6 57.7 %copy-start.7 = (s32[16]{0:T(128)S(1)}, s32[16]{0:T(128)}, u32[]{:S(2)}) copy-start(s32[16]{0:T(128)} %owner.3) | copy-start | bytes 196
  0.6 57.7 %copy-start.5 = (s32[96]{0:T(128)S(1)}, s32[96]{0:T(128)}, u32[]{:S(2)}) copy-start(s32[96]{0:T(128)} %blocks.3) | copy-start | bytes 1156
  0.7 57.7 %copy-start.3 = (s32[96]{0:T(128)S(1)}, s32[96]{0:T(128)}, u32[]{:S(2)}) copy-start(s32[96]{0:T(128)} %tile_ids.3) | copy-start | bytes 1156
  4.5 53.8 %copy-start.1 = (f32[16,128,128]{2,1,0:T(8,128)S(1)}, f32[16,128,128]{2,1,0:T(8,128)}, u32[]{:S(2)}) copy-start(f32[16,128,128]{2,1,0:T(8,128)} %image.3) | copy-start | bytes 3145732
  10.5 8.1 %collective-permute-start = (bf16[8,128,128]{2,1,0:T(8,128)(2,1)S(1)}, bf16[8,128,128]{2,1,0:T(8,128)(2,1)S(1)}, u32[]{:S(2)}, u32[]{:S(2)}) collective-permute-start(bf16[8,128,128]{2,1,0:T(8,128)(2,1)S(1)} %get-tuple-element.11), channel_id=1, source_target_pairs={{0,2},{2,0},{4,6},{6,4},{8,10},{10,8},{12,14},{14,12},{16,18},{18,... | collective-permute-start | bytes 786440 | tf_op jit(solution)/shard_map/ppermute | solution.py:208
  12.6 7.4 %collective-permute-start.8 = (bf16[8,128,128]{2,1,0:T(8,128)(2,1)S(1)}, bf16[8,128,128]{2,1,0:T(8,128)(2,1)S(1)}, u32[]{:S(2)}, u32[]{:S(2)}) collective-permute-start(bf16[8,128,128]{2,1,0:T(8,128)(2,1)S(1)} %get-tuple-element.13), channel_id=1, source_target_pairs={{0,4},{2,6},{4,0},{6,2},{8,12},{10,14},{12,8},{14,10},{16,20},{18,... | collective-permute-start | bytes 786440 | tf_op jit(solution)/shard_map/ppermute | solution.py:208
  18.7 3.9 %collective-permute-start.1 = (bf16[4,128,128]{2,1,0:T(8,128)(2,1)S(1)}, bf16[4,128,128]{2,1,0:T(8,128)(2,1)S(1)}, u32[]{:S(2)}, u32[]{:S(2)}) collective-permute-start(bf16[4,128,128]{2,1,0:T(8,128)(2,1)S(1)} %slice.89), channel_id=1, source_target_pairs={{0,4},{2,6},{4,0},{6,2},{8,12},{10,14},{12,8},{14,10},{16,20},{18,... | collective-permute-start | bytes 393224 | tf_op jit(solution)/shard_map/ppermute | solution.py:208
  20.0 4.2 %collective-permute-start.9 = (bf16[4,128,128]{2,1,0:T(8,128)(2,1)S(1)}, bf16[4,128,128]{2,1,0:T(8,128)(2,1)S(1)}, u32[]{:S(2)}, u32[]{:S(2)}) collective-permute-start(bf16[4,128,128]{2,1,0:T(8,128)(2,1)S(1)} %slice.88), channel_id=1, source_target_pairs={{0,2},{2,0},{4,6},{6,4},{8,10},{10,8},{12,14},{14,12},{16,18},{18,... | collective-permute-start | bytes 393224 | tf_op jit(solution)/shard_map/ppermute | solution.py:208
  22.6 3.5 %collective-permute-start.2 = (bf16[2,128,128]{2,1,0:T(8,128)(2,1)S(1)}, bf16[2,128,128]{2,1,0:T(8,128)(2,1)S(1)}, u32[]{:S(2)}, u32[]{:S(2)}) collective-permute-start(bf16[2,128,128]{2,1,0:T(8,128)(2,1)S(1)} %slice.91), channel_id=1, source_target_pairs={{0,8},{2,10},{4,12},{6,14},{8,0},{10,2},{12,4},{14,6},{16,24},{18,... | collective-permute-start | bytes 196616 | tf_op jit(solution)/shard_map/ppermute | solution.py:208
  24.3 4.2 %collective-permute-start.10 = (bf16[2,128,128]{2,1,0:T(8,128)(2,1)S(1)}, bf16[2,128,128]{2,1,0:T(8,128)(2,1)S(1)}, u32[]{:S(2)}, u32[]{:S(2)}) collective-permute-start(bf16[2,128,128]{2,1,0:T(8,128)(2,1)S(1)} %slice.90), channel_id=1, source_target_pairs={{0,8},{2,10},{4,12},{6,14},{8,0},{10,2},{12,4},{14,6},{16,24},{18,... | collective-permute-start | bytes 196616 | tf_op jit(solution)/shard_map/ppermute | solution.py:208
  26.1 4.3 %collective-permute-start.3 = (bf16[1,128,128]{2,1,0:T(8,128)(2,1)S(1)}, bf16[1,128,128]{2,1,0:T(8,128)(2,1)S(1)}, u32[]{:S(2)}, u32[]{:S(2)}) collective-permute-start(bf16[1,128,128]{2,1,0:T(8,128)(2,1)S(1)} %slice.93), channel_id=1, source_target_pairs={{0,16},{2,18},{4,20},{6,22},{8,24},{10,26},{12,28},{14,30},{16,0},... | collective-permute-start | bytes 98312 | tf_op jit(solution)/shard_map/ppermute | solution.py:208
  29.1 6.0 %collective-permute-start.11 = (bf16[1,128,128]{2,1,0:T(8,128)(2,1)S(1)}, bf16[1,128,128]{2,1,0:T(8,128)(2,1)S(1)}, u32[]{:S(2)}, u32[]{:S(2)}) collective-permute-start(bf16[1,128,128]{2,1,0:T(8,128)(2,1)S(1)} %slice.92), channel_id=1, source_target_pairs={{0,16},{2,18},{4,20},{6,22},{8,24},{10,26},{12,28},{14,30},{16,0},... | collective-permute-start | bytes 98312 | tf_op jit(solution)/shard_map/ppermute | solution.py:208
  32.7 46.5 %copy-start.8 = (bf16[1,128,128]{2,1,0:T(8,128)(2,1)S(1)}, bf16[1,128,128]{2,1,0:T(8,128)(2,1)}, u32[]{:S(2)}) copy-start(bf16[1,128,128]{2,1,0:T(8,128)(2,1)} %residual.2) | copy-start | bytes 98308
  32.7 5.3 %collective-permute-start.4 = (bf16[1,128,128]{2,1,0:T(8,128)(2,1)}, bf16[1,128,128]{2,1,0:T(8,128)(2,1)S(1)}, u32[]{:S(2)}, u32[]{:S(2)}) collective-permute-start(bf16[1,128,128]{2,1,0:T(8,128)(2,1)} %residual.2), channel_id=1, source_target_pairs={{0,16},{2,18},{4,20},{6,22},{8,24},{10,26},{12,28},{14,30},{16,0},... | collective-permute-start | bytes 98312 | tf_op jit(solution)/shard_map/ppermute | solution.py:218
  37.4 4.3 %collective-permute-start.12 = (bf16[1,128,128]{2,1,0:T(8,128)(2,1)}, bf16[1,128,128]{2,1,0:T(8,128)(2,1)S(1)}, u32[]{:S(2)}, u32[]{:S(2)}) collective-permute-start(bf16[1,128,128]{2,1,0:T(8,128)(2,1)} %residual.3), channel_id=1, source_target_pairs={{0,16},{2,18},{4,20},{6,22},{8,24},{10,26},{12,28},{14,30},{16,0},... | collective-permute-start | bytes 98312 | tf_op jit(solution)/shard_map/ppermute | solution.py:218
  38.8 5.1 %collective-permute-start.5 = (bf16[2,128,128]{2,1,0:T(8,128)(2,1)S(1)}, bf16[2,128,128]{2,1,0:T(8,128)(2,1)S(1)}, u32[]{:S(2)}, u32[]{:S(2)}) collective-permute-start(bf16[2,128,128]{2,1,0:T(8,128)(2,1)S(1)} %pad_maximum_fusion.6), channel_id=1, source_target_pairs={{0,8},{2,10},{4,12},{6,14},{8,0},{10,2},{12,4},{14,6},{16,24},{18,... | collective-permute-start | bytes 196616 | tf_op jit(solution)/shard_map/ppermute | solution.py:218
  42.5 3.3 %collective-permute-start.13 = (bf16[2,128,128]{2,1,0:T(8,128)(2,1)S(1)}, bf16[2,128,128]{2,1,0:T(8,128)(2,1)S(1)}, u32[]{:S(2)}, u32[]{:S(2)}) collective-permute-start(bf16[2,128,128]{2,1,0:T(8,128)(2,1)S(1)} %pad_maximum_fusion.7), channel_id=1, source_target_pairs={{0,8},{2,10},{4,12},{6,14},{8,0},{10,2},{12,4},{14,6},{16,24},{18,... | collective-permute-start | bytes 196616 | tf_op jit(solution)/shard_map/ppermute | solution.py:218
  44.6 3.9 %collective-permute-start.6 = (bf16[4,128,128]{2,1,0:T(8,128)(2,1)S(1)}, bf16[4,128,128]{2,1,0:T(8,128)(2,1)S(1)}, u32[]{:S(2)}, u32[]{:S(2)}) collective-permute-start(bf16[4,128,128]{2,1,0:T(8,128)(2,1)S(1)} %pad_maximum_fusion.4), channel_id=1, source_target_pairs={{0,4},{2,6},{4,0},{6,2},{8,12},{10,14},{12,8},{14,10},{16,20},{18,... | collective-permute-start | bytes 393224 | tf_op jit(solution)/shard_map/ppermute | solution.py:218
  46.6 4.0 %collective-permute-start.14 = (bf16[4,128,128]{2,1,0:T(8,128)(2,1)S(1)}, bf16[4,128,128]{2,1,0:T(8,128)(2,1)S(1)}, u32[]{:S(2)}, u32[]{:S(2)}) collective-permute-start(bf16[4,128,128]{2,1,0:T(8,128)(2,1)S(1)} %pad_maximum_fusion.5), channel_id=1, source_target_pairs={{0,2},{2,0},{4,6},{6,4},{8,10},{10,8},{12,14},{14,12},{16,18},{18,... | collective-permute-start | bytes 393224 | tf_op jit(solution)/shard_map/ppermute | solution.py:218
  49.3 5.6 %collective-permute-start.7 = (bf16[8,128,128]{2,1,0:T(8,128)(2,1)S(1)}, bf16[8,128,128]{2,1,0:T(8,128)(2,1)S(1)}, u32[]{:S(2)}, u32[]{:S(2)}) collective-permute-start(bf16[8,128,128]{2,1,0:T(8,128)(2,1)S(1)} %pad_maximum_fusion.a_low), channel_id=1, source_target_pairs={{0,2},{2,0},{4,6},{6,4},{8,10},{10,8},{12,14},{14,12},{16,18},{18,... | collective-permute-start | bytes 786440 | tf_op jit(solution)/shard_map/ppermute | solution.py:218
  51.4 6.9 %collective-permute-start.15 = (bf16[8,128,128]{2,1,0:T(8,128)(2,1)S(1)}, bf16[8,128,128]{2,1,0:T(8,128)(2,1)S(1)}, u32[]{:S(2)}, u32[]{:S(2)}) collective-permute-start(bf16[8,128,128]{2,1,0:T(8,128)(2,1)S(1)} %pad_maximum_fusion.1.b_low), channel_id=1, source_target_pairs={{0,4},{2,6},{4,0},{6,2},{8,12},{10,14},{12,8},{14,10},{16,20},{18,... | collective-permute-start | bytes 786440 | tf_op jit(solution)/shard_map/ppermute | solution.py:218
  66.0 9.0 %collective-permute-start.16 = (f32[16,8,128]{2,1,0:T(8,128)S(1)}, f32[16,8,128]{2,1,0:T(8,128)S(1)}, u32[]{:S(2)}, u32[]{:S(2)}) collective-permute-start(f32[16,8,128]{2,1,0:T(8,128)S(1)} %get-tuple-element.15), channel_id=1, source_target_pairs={{0,1},{1,0},{2,3},{3,2},{4,5},{5,4},{6,7},{7,6},{8,9},{9,8},{10,11... | collective-permute-start | bytes 196616 | tf_op jit(solution)/shard_map/ppermute | solution.py:307
  75.1 5.6 %collective-permute-start.17 = (bf16[576,128]{1,0:T(8,128)(2,1)S(1)}, bf16[576,128]{1,0:T(8,128)(2,1)S(1)}, u32[]{:S(2)}, u32[]{:S(2)}) collective-permute-start(bf16[576,128]{1,0:T(8,128)(2,1)S(1)} %pad_maximum_fusion.2), channel_id=1, source_target_pairs={{0,2},{2,4},{4,6},{6,8},{8,10},{10,12},{12,14},{14,16},{16,18},{18... | collective-permute-start | bytes 442376 | tf_op jit(solution)/shard_map/ppermute | solution.py:317
  77.9 8.8 %collective-permute-start.18 = (bf16[576,128]{1,0:T(8,128)(2,1)S(1)}, bf16[576,128]{1,0:T(8,128)(2,1)S(1)}, u32[]{:S(2)}, u32[]{:S(2)}) collective-permute-start(bf16[576,128]{1,0:T(8,128)(2,1)S(1)} %pad_maximum_fusion.3), channel_id=1, source_target_pairs={{2,0},{4,2},{6,4},{8,6},{10,8},{12,10},{14,12},{16,14},{18,16},{20... | collective-permute-start | bytes 442376 | tf_op jit(solution)/shard_map/ppermute | solution.py:318
  (7 other events, 46.2 us)

commit v2 on v1

--- a/solution.py
+++ b/solution.py
@@ -16,9 +16,8 @@
 flow_step = 0.04
 relax_step = 4.0
 
-SMEM = pl.BlockSpec(memory_space=pltpu.SMEM)
 VMEM = pl.BlockSpec(memory_space=pltpu.VMEM)
-ANY = pl.BlockSpec(memory_space=pl.ANY)
+HBM = pl.BlockSpec(memory_space=pltpu.HBM)
 PARAMS = pltpu.CompilerParams(vmem_limit_bytes=48 * 1024 * 1024)
 
 
@@ -39,10 +38,20 @@
     ]
 
 
+def list_copies(lists, scalars):
+    held, sem = scalars[:-1], scalars[-1]
+    copies = [pltpu.make_async_copy(a, b, sem.at[i]) for i, (a, b) in enumerate(zip(lists, held))]
+    for copy in copies:
+        copy.start()
+    return copies, held
+
+
 def forward_kernel(
-    orders, me, tile_ids, blocks, owner, count, image, weights,
-    a_keep, a_send, b_keep, b_send, pixels, held, turned, total, image_sem, sems,
+    orders, tile_ids, blocks, owner, count, image, weights,
+    a_keep, a_send, b_keep, b_send, pixels, held, turned, total, image_sem, sems, *scalars,
 ):
+    me = lax.axis_index("plane")
+    lists, (tile_ids, blocks, owner, count) = list_copies((tile_ids, blocks, owner, count), scalars)
     slots, voxels, rays = held.shape
     parts = total.shape[0] - 1
     half = rays // 2
@@ -56,6 +65,9 @@
         tile = pixels[:, t * TILE : (t + 1) * TILE, :].reshape(voxels, pixels.shape[2])
         turned[t] = tile.T.astype(jnp.bfloat16)
 
+    for copy in lists:
+        copy.wait()
+
     def step(group, carry):
         first = pl.multiple_of(group * GROUP, GROUP)
         pltpu.make_async_copy(
@@ -63,7 +75,7 @@
         ).wait()
         for k in range(GROUP):
             s = first + k
-            to = jnp.where(s < count[0], owner[blocks[s]] ^ me[0], parts)
+            to = jnp.where(s < count[0], owner[blocks[s]] ^ me, parts)
             total[to] += jnp.dot(
                 turned[tile_ids[s]], held[s], preferred_element_type=jnp.float32
             )
@@ -84,9 +96,12 @@
 
 
 def backward_kernel(
-    orders, me, cut, tile_ids, blocks, owner, count, a_low, a_high, b_low, b_high, image, weights,
-    relaxed, first_rows, last_rows, strip, pixels, held, spread, total, image_sem, sems,
+    orders, tile_ids, blocks, owner, count, a_low, a_high, b_low, b_high, image, weights,
+    relaxed, first_rows, last_rows, strip, pixels, held, spread, total, image_sem, sems, *scalars,
 ):
+    me = lax.axis_index("plane")
+    cut = lax.axis_index("cuts")
+    lists, (tile_ids, blocks, owner, count) = list_copies((tile_ids, blocks, owner, count), scalars)
     slots, voxels, rays = held.shape
     parts = spread.shape[0]
     tiles = total.shape[0] - 1
@@ -103,6 +118,9 @@
         spread[relative_block(orders[1], p), half:] = b_low[p]
         spread[relative_block(orders[1], p + parts // 2), half:] = b_high[p]
 
+    for copy in lists:
+        copy.wait()
+
     def step(group, carry):
         first = pl.multiple_of(group * GROUP, GROUP)
         pltpu.make_async_copy(
@@ -112,7 +130,7 @@
             s = first + k
             to = jnp.where(s < count[0], tile_ids[s], tiles)
             total[to] += jnp.dot(
-                held[s], spread[owner[blocks[s]] ^ me[0]], preferred_element_type=jnp.float32
+                held[s], spread[owner[blocks[s]] ^ me], preferred_element_type=jnp.float32
             )
         return carry
 
@@ -126,7 +144,7 @@
         first_rows[i * cols : (i + 1) * cols] = relaxed[i].astype(jnp.bfloat16)
         last_rows[i * cols : (i + 1) * cols] = relaxed[rows - SWEEPS + i].astype(jnp.bfloat16)
     lane = lax.broadcasted_iota(jnp.int32, (cols, slices), 1)
-    start = jnp.where(cut[0] == 0, slices - EDGE, 0)
+    start = jnp.where(cut == 0, slices - EDGE, 0)
     edges = jnp.zeros((cols, slices), jnp.float32)
     for i in range(rows):
         moved = pltpu.roll(relaxed[i], (i * EDGE - start + slices) % slices, 1)
@@ -152,32 +170,38 @@
     return rise_rows * scale, rise_inner * scale, rise_outer * scale
 
 
-def sweeps_over(field, rows, has_low, has_high):
+def sweeps_over(fields, rows, has_low, has_high):
+    def advance(field, i, before):
+        cell = field[i]
+        flow_rows, flow_inner, flow_outer = flows(cell, field[i + 1])
+        diverge = flow_rows - before
+        diverge = diverge + (flow_inner - shifted(flow_inner, 0, 1))
+        diverge = diverge + (flow_outer - shifted(flow_outer, 1, 1))
+        field[i] = cell + flow_step * diverge
+        return flow_rows
+
     for sweep in range(1, SWEEPS + 1):
 
         @pl.when(has_low == 0)
         def _():
-            field[SWEEPS - 1] = field[SWEEPS]
+            for field in fields:
+                field[SWEEPS - 1] = field[SWEEPS]
 
         @pl.when(has_high == 0)
         def _():
-            field[SWEEPS + rows] = jnp.zeros(field.shape[1:], field.dtype)
+            for field in fields:
+                field[SWEEPS + rows] = jnp.zeros(field.shape[1:], field.dtype)
 
         def body(i, before):
-            cell = field[i]
-            flow_rows, flow_inner, flow_outer = flows(cell, field[i + 1])
-            diverge = flow_rows - before
-            diverge = diverge + (flow_inner - shifted(flow_inner, 0, 1))
-            diverge = diverge + (flow_outer - shifted(flow_outer, 1, 1))
-            field[i] = cell + flow_step * diverge
-            return flow_rows
-
-        before = flows(field[sweep - 1], field[sweep])[0]
-        lax.fori_loop(sweep, rows + 2 * SWEEPS - sweep, body, before)
-
-
-def sweep_kernel(me, cut, relaxed, strip, from_low, from_high, volume, field, narrow, *, planes):
+            return tuple(advance(field, i, flow) for field, flow in zip(fields, before))
+
+        before = tuple(flows(field[sweep - 1], field[sweep])[0] for field in fields)
+        lax.fori_loop(sweep, rows + 2 * SWEEPS - sweep, body, before, unroll=3)
+
+
+def sweep_kernel(relaxed, strip, from_low, from_high, volume, field, narrow, *, planes):
     rows, cols, slices = relaxed.shape
+    me, cut = lax.axis_index("plane"), lax.axis_index("cuts")
     body = SWEEPS * cols
     field[SWEEPS : SWEEPS + rows] = relaxed[...]
     narrow[SWEEPS : SWEEPS + rows] = strip[...]
@@ -186,11 +210,10 @@
         narrow[start : start + SWEEPS] = (
             halo[body:].astype(jnp.float32).reshape(SWEEPS, 2 * EDGE, cols)
         )
-    has_low = (me[0] > 0).astype(jnp.int32)
-    has_high = (me[0] < planes - 1).astype(jnp.int32)
-    sweeps_over(narrow, rows, has_low, has_high)
-    sweeps_over(field, rows, has_low, has_high)
-    low_side = cut[0] == 0
+    has_low = (me > 0).astype(jnp.int32)
+    has_high = (me < planes - 1).astype(jnp.int32)
+    sweeps_over((field, narrow), rows, has_low, has_high)
+    low_side = cut == 0
     mine = narrow[SWEEPS : SWEEPS + rows]
     mine = jnp.where(low_side, mine[:, :EDGE], mine[:, EDGE:])
     turned = mine.reshape(rows * EDGE, cols).T
@@ -240,16 +263,20 @@
     plain = tuple(range(bits))
     swapped = (1, 0) + plain[2:]
     orders = (plain, swapped)
-    me = lax.axis_index("plane").astype(jnp.int32).reshape(1)
-    cut = lax.axis_index("cuts").astype(jnp.int32).reshape(1)
+    cut = lax.axis_index("cuts")
     shape = jax.ShapeDtypeStruct
     f32, bf16 = jnp.float32, jnp.bfloat16
+
+    scalars = [
+        *(pltpu.SMEM(a.shape, jnp.int32) for a in (pair_tile_index, pair_ray_block, ray_owner, active_pair_count)),
+        pltpu.SemaphoreType.DMA((4,)),
+    ]
 
     kept, sent = shape((parts // 2, slices, half), f32), shape((parts // 2, slices, half), bf16)
     a_keep, a_send, b_keep, b_send = pl.pallas_call(
         functools.partial(forward_kernel, orders),
         out_shape=(kept, sent, kept, sent),
-        in_specs=[SMEM] * 5 + [ANY, ANY],
+        in_specs=[HBM] * 6,
         out_specs=(VMEM,) * 4,
         scratch_shapes=[
             pltpu.VMEM((rows, cols, slices), f32),
@@ -258,10 +285,11 @@
             pltpu.VMEM((parts + 1, slices, rays), f32),
             pltpu.SemaphoreType.DMA,
             pltpu.SemaphoreType.DMA((slots // GROUP,)),
+            *scalars,
         ],
         compiler_params=PARAMS,
         name="forward",
-    )(me, pair_tile_index, pair_ray_block, ray_owner, active_pair_count, image, projection_weight_tiles)
+    )(pair_tile_index, pair_ray_block, ray_owner, active_pair_count, image, projection_weight_tiles)
 
     pieces = []
     for low, keep, send, order in ((0, a_keep, a_send, plain), (half, b_keep, b_send, swapped)):
@@ -272,6 +300,7 @@
                 out_shape=shape((1, half, slices), bf16),
                 in_specs=[VMEM] * 3,
                 out_specs=VMEM,
+                compiler_params=PARAMS,
                 name="residual",
             )(keep, got, measured)
         )
@@ -287,7 +316,7 @@
             shape((SWEEPS * cols, slices), bf16),
             shape((rows, EDGE, cols), f32),
         ),
-        in_specs=[SMEM] * 6 + [VMEM] * 4 + [ANY, ANY],
+        in_specs=[HBM] * 4 + [VMEM] * 4 + [HBM, HBM],
         out_specs=(VMEM,) * 4,
         scratch_shapes=[
             pltpu.VMEM((rows, cols, slices), f32),
@@ -296,17 +325,18 @@
             pltpu.VMEM((tiles + 1, voxels, slices), f32),
             pltpu.SemaphoreType.DMA,
             pltpu.SemaphoreType.DMA((slots // GROUP,)),
+            *scalars,
         ],
         compiler_params=PARAMS,
         name="backward",
     )(
-        me, cut, pair_tile_index, pair_ray_block, ray_owner, active_pair_count,
+        pair_tile_index, pair_ray_block, ray_owner, active_pair_count,
         a_low, a_high, b_low, b_high, image, projection_weight_tiles,
     )
 
     other = lax.ppermute(strip, "cuts", [(0, 1), (1, 0)])
     both = jnp.where(
-        cut[0] == 0, jnp.concatenate([strip, other], 1), jnp.concatenate([other, strip], 1)
+        cut == 0, jnp.concatenate([strip, other], 1), jnp.concatenate([other, strip], 1)
     )
 
     def with_strip(main, part):
@@ -320,7 +350,7 @@
     volume = pl.pallas_call(
         functools.partial(sweep_kernel, planes=planes),
         out_shape=shape((rows, cols, slices), f32),
-        in_specs=[SMEM, SMEM] + [VMEM] * 4,
+        in_specs=[VMEM] * 4,
         out_specs=VMEM,
         scratch_shapes=[
             pltpu.VMEM((rows + 2 * SWEEPS, cols, slices), f32),
@@ -328,7 +358,7 @@
         ],
         compiler_params=PARAMS,
         name="sweeps",
-    )(me, cut, relaxed, both, from_low, from_high)
+    )(relaxed, both, from_low, from_high)
     return (volume, residual)
 
 

time: 115 us -> 87.4 us (0.76)
  Pallas kernels: 43.8 us -> 20.6 us
  other arithmetic: 5.53 us -> 0.98 us
  starting transfers between devices: 34.5 us -> 37 us
  local copies, waits for them, and re-layouts: 5.78 us -> 3.3 us
    pallas_call x1, Pallas kernels: 26.8 us -> 7.71 us  [per_device(): pl.pallas_call(functools.partial(sweep_kernel, planes=planes), out_shape=...]
    concatenate x6, other arithmetic: 4.65 us -> 0.1 us  [spread_chain(): piece = jnp.concatenate([piece, got], axis=0)]
    pallas_call x2, Pallas kernels: 3.39 us -> 0.24 us  [per_device(): pl.pallas_call(functools.partial(residual_kernel, low), out_shape=shape((...]
    ppermute x8, starting transfers between devices: 10.2 us -> 12.8 us  [spread_chain(): lax.ppermute(piece, 'plane', [(i, i ^ 1 << bit) for i in range(planes)])]
    slice x8, local copies, waits for them, and re-layouts: 1.34 us -> 0.09 us  [sum_chain(): keep, send = (total[:left], total[left:].astype(jnp.bfloat16))]
    unnamed x24 -> x18, local copies, waits for them, and re-layouts: 4.44 us -> 3.2 us
  transfers between devices with their start and end apart: 19 -> 19, of which waited for: 11 -> 14; matrix products, arithmetic and copies ran while one was open for 6% -> 1% of each run, Pallas kernels for 3% -> 0%
where the time goes in v2:
time: 87.4 us; the launch traced here: 86 us
  starting transfers between devices  37 us (42%)
  waiting for transfers between devices  22.6 us (26%)
  Pallas kernels  20.6 us (24%)
  local copies, waits for them, and re-layouts  3.3 us (4%)
  between operations  1.54 us (2%)
  other arithmetic  0.98 us (1%)
    ppermute x8, starting transfers between devices, spread_chain(): lax.ppermute(piece, 'plane', [(i, i ^ 1 << bit) for i in range(planes)])  12.8 us
    ppermute x8, starting transfers between devices, sum_chain(): lax.ppermute(send, 'plane', [(i, i ^ 1 << bit) for i in range(planes)])  12.2 us
    ppermute x1, starting transfers between devices, per_device(): other = lax.ppermute(strip, 'cuts', [(0, 1), (1, 0)])  8.33 us
    ppermute x8, waiting for transfers between devices, spread_chain(): lax.ppermute(piece, 'plane', [(i, i ^ 1 << bit) for i in range(planes)])  7.98 us
    pallas_call x1, Pallas kernels, per_device(): pl.pallas_call(functools.partial(sweep_kernel, planes=planes), out_shape=...  7.71 us
    pallas_call x1, Pallas kernels, per_device(): pl.pallas_call(functools.partial(backward_kernel, orders), out_shape=(sha...  7.16 us
    ppermute x8, waiting for transfers between devices, sum_chain(): lax.ppermute(send, 'plane', [(i, i ^ 1 << bit) for i in range(planes)])  6.81 us
    ppermute x1, waiting for transfers between devices, per_device(): lax.ppermute(with_strip(first_rows, both[:SWEEPS]), 'plane', downward)  5.99 us
  transfers between devices with their start and end apart: 19, of which 14 were waited for; matrix products, arithmetic and copies ran while one was open for 1% of the time, Pallas kernels for 0%

profile of v2, /device:TPU:1, one launch (start us, length us, event | category | flops | bytes accessed | tf_op | source)
XLA Modules:
  0.0 86.0 jit_solution(9477935171533249615)
XLA Ops:
  4.5 5.5 %forward.1 = (f32[8,128,128]{2,1,0:T(8,128)S(1)}, bf16[8,128,128]{2,1,0:T(8,128)(2,1)S(1)}, f32[8,128,128]{2,1,0:T(8,128)S(1)}, bf16[8,128,128]{2,1,0:T(8,128)(2,1)S(1)}) custom-call(s32[96]{0:T(128)S(1)} %copy-done.3, s32[96]{0:T(128)S(1)} %copy-done.5, s32[16]{0:T(128)S(1)} %copy-done.7, s32[1]{0:T(128)S(6)} %copy.9.count, f32[16,128,128]{2,1,0:T(8,128)S(1)} %copy-done, ...), custom_call_target="tpu_custom_call" | custom-call | tf_op jit(solution)/shard_map/forward/pallas_call | solution.py:276
  10.0 2.1 %collective-permute-start = (bf16[8,128,128]{2,1,0:T(8,128)(2,1)S(1)}, bf16[8,128,128]{2,1,0:T(8,128)(2,1)S(1)}, u32[]{:S(2)}, u32[]{:S(2)}) collective-permute-start(bf16[8,128,128]{2,1,0:T(8,128)(2,1)S(1)} %get-tuple-element.11), channel_id=1, source_target_pairs={{0,2},{2,0},{4,6},{6,4},{8,10},{10,8},{12,14},{14,12},{16,18},{18,... | collective-permute-start | bytes 786440 | tf_op jit(solution)/shard_map/ppermute | solution.py:231
  13.4 4.8 %collective-permute-done = bf16[8,128,128]{2,1,0:T(8,128)(2,1)S(1)} collective-permute-done((bf16[8,128,128]{2,1,0:T(8,128)(2,1)S(1)}, bf16[8,128,128]{2,1,0:T(8,128)(2,1)S(1)}, u32[]{:S(2)}, u32[]{:S(2)}) %collective-permute-start) | collective-permute-done | bytes 262176 | tf_op jit(solution)/shard_map/ppermute | solution.py:231
  19.6 1.3 %collective-permute-start.9 = (bf16[4,128,128]{2,1,0:T(8,128)(2,1)S(1)}, bf16[4,128,128]{2,1,0:T(8,128)(2,1)S(1)}, u32[]{:S(2)}, u32[]{:S(2)}) collective-permute-start(bf16[4,128,128]{2,1,0:T(8,128)(2,1)S(1)} %slice.88), channel_id=1, source_target_pairs={{0,2},{2,0},{4,6},{6,4},{8,10},{10,8},{12,14},{14,12},{16,18},{18,... | collective-permute-start | bytes 393224 | tf_op jit(solution)/shard_map/ppermute | solution.py:231
  22.2 1.3 %collective-permute-start.2 = (bf16[2,128,128]{2,1,0:T(8,128)(2,1)S(1)}, bf16[2,128,128]{2,1,0:T(8,128)(2,1)S(1)}, u32[]{:S(2)}, u32[]{:S(2)}) collective-permute-start(bf16[2,128,128]{2,1,0:T(8,128)(2,1)S(1)} %slice.91), channel_id=1, source_target_pairs={{0,8},{2,10},{4,12},{6,14},{8,0},{10,2},{12,4},{14,6},{16,24},{18,... | collective-permute-start | bytes 196616 | tf_op jit(solution)/shard_map/ppermute | solution.py:231
  23.8 1.4 %collective-permute-start.10 = (bf16[2,128,128]{2,1,0:T(8,128)(2,1)S(1)}, bf16[2,128,128]{2,1,0:T(8,128)(2,1)S(1)}, u32[]{:S(2)}, u32[]{:S(2)}) collective-permute-start(bf16[2,128,128]{2,1,0:T(8,128)(2,1)S(1)} %slice.90), channel_id=1, source_target_pairs={{0,8},{2,10},{4,12},{6,14},{8,0},{10,2},{12,4},{14,6},{16,24},{18,... | collective-permute-start | bytes 196616 | tf_op jit(solution)/shard_map/ppermute | solution.py:231
  25.7 2.3 %collective-permute-start.3 = (bf16[1,128,128]{2,1,0:T(8,128)(2,1)S(1)}, bf16[1,128,128]{2,1,0:T(8,128)(2,1)S(1)}, u32[]{:S(2)}, u32[]{:S(2)}) collective-permute-start(bf16[1,128,128]{2,1,0:T(8,128)(2,1)S(1)} %slice.93), channel_id=1, source_target_pairs={{0,16},{2,18},{4,20},{6,22},{8,24},{10,26},{12,28},{14,30},{16,0},... | collective-permute-start | bytes 98312 | tf_op jit(solution)/shard_map/ppermute | solution.py:231
  28.1 1.4 %collective-permute-start.11 = (bf16[1,128,128]{2,1,0:T(8,128)(2,1)S(1)}, bf16[1,128,128]{2,1,0:T(8,128)(2,1)S(1)}, u32[]{:S(2)}, u32[]{:S(2)}) collective-permute-start(bf16[1,128,128]{2,1,0:T(8,128)(2,1)S(1)} %slice.92), channel_id=1, source_target_pairs={{0,16},{2,18},{4,20},{6,22},{8,24},{10,26},{12,28},{14,30},{16,0},... | collective-permute-start | bytes 98312 | tf_op jit(solution)/shard_map/ppermute | solution.py:231
  29.6 2.3 %collective-permute-start.4 = (bf16[1,128,128]{2,1,0:T(8,128)(2,1)S(1)}, bf16[1,128,128]{2,1,0:T(8,128)(2,1)S(1)}, u32[]{:S(2)}, u32[]{:S(2)}) collective-permute-start(bf16[1,128,128]{2,1,0:T(8,128)(2,1)S(1)} %residual.2), channel_id=1, source_target_pairs={{0,16},{2,18},{4,20},{6,22},{8,24},{10,26},{12,28},{14,30},{16,0},... | collective-permute-start | bytes 98312 | tf_op jit(solution)/shard_map/ppermute | solution.py:241
  32.0 1.3 %collective-permute-start.12 = (bf16[1,128,128]{2,1,0:T(8,128)(2,1)S(1)}, bf16[1,128,128]{2,1,0:T(8,128)(2,1)S(1)}, u32[]{:S(2)}, u32[]{:S(2)}) collective-permute-start(bf16[1,128,128]{2,1,0:T(8,128)(2,1)S(1)} %residual.3), channel_id=1, source_target_pairs={{0,16},{2,18},{4,20},{6,22},{8,24},{10,26},{12,28},{14,30},{16,0},... | collective-permute-start | bytes 98312 | tf_op jit(solution)/shard_map/ppermute | solution.py:241
  33.9 1.4 %collective-permute-start.5 = (bf16[2,128,128]{2,1,0:T(8,128)(2,1)S(1)}, bf16[2,128,128]{2,1,0:T(8,128)(2,1)S(1)}, u32[]{:S(2)}, u32[]{:S(2)}) collective-permute-start(bf16[2,128,128]{2,1,0:T(8,128)(2,1)S(1)} %pad_maximum_fusion.6), channel_id=1, source_target_pairs={{0,8},{2,10},{4,12},{6,14},{8,0},{10,2},{12,4},{14,6},{16,24},{18,... | collective-permute-start | bytes 196616 | tf_op jit(solution)/shard_map/ppermute | solution.py:241
  35.8 2.1 %collective-permute-start.13 = (bf16[2,128,128]{2,1,0:T(8,128)(2,1)S(1)}, bf16[2,128,128]{2,1,0:T(8,128)(2,1)S(1)}, u32[]{:S(2)}, u32[]{:S(2)}) collective-permute-start(bf16[2,128,128]{2,1,0:T(8,128)(2,1)S(1)} %pad_maximum_fusion.7), channel_id=1, source_target_pairs={{0,8},{2,10},{4,12},{6,14},{8,0},{10,2},{12,4},{14,6},{16,24},{18,... | collective-permute-start | bytes 196616 | tf_op jit(solution)/shard_map/ppermute | solution.py:241
  37.9 1.5 %collective-permute-start.6 = (bf16[4,128,128]{2,1,0:T(8,128)(2,1)S(1)}, bf16[4,128,128]{2,1,0:T(8,128)(2,1)S(1)}, u32[]{:S(2)}, u32[]{:S(2)}) collective-permute-start(bf16[4,128,128]{2,1,0:T(8,128)(2,1)S(1)} %pad_maximum_fusion.4), channel_id=1, source_target_pairs={{0,4},{2,6},{4,0},{6,2},{8,12},{10,14},{12,8},{14,10},{16,20},{18,... | collective-permute-start | bytes 393224 | tf_op jit(solution)/shard_map/ppermute | solution.py:241
  39.6 1.3 %collective-permute-start.14 = (bf16[4,128,128]{2,1,0:T(8,128)(2,1)S(1)}, bf16[4,128,128]{2,1,0:T(8,128)(2,1)S(1)}, u32[]{:S(2)}, u32[]{:S(2)}) collective-permute-start(bf16[4,128,128]{2,1,0:T(8,128)(2,1)S(1)} %pad_maximum_fusion.5), channel_id=1, source_target_pairs={{0,2},{2,0},{4,6},{6,4},{8,10},{10,8},{12,14},{14,12},{16,18},{18,... | collective-permute-start | bytes 393224 | tf_op jit(solution)/shard_map/ppermute | solution.py:241
  41.9 1.3 %collective-permute-start.7 = (bf16[8,128,128]{2,1,0:T(8,128)(2,1)S(1)}, bf16[8,128,128]{2,1,0:T(8,128)(2,1)S(1)}, u32[]{:S(2)}, u32[]{:S(2)}) collective-permute-start(bf16[8,128,128]{2,1,0:T(8,128)(2,1)S(1)} %pad_maximum_fusion.a_low), channel_id=1, source_target_pairs={{0,2},{2,0},{4,6},{6,4},{8,10},{10,8},{12,14},{14,12},{16,18},{18,... | collective-permute-start | bytes 786440 | tf_op jit(solution)/shard_map/ppermute | solution.py:241
  43.5 1.7 %collective-permute-start.15 = (bf16[8,128,128]{2,1,0:T(8,128)(2,1)S(1)}, bf16[8,128,128]{2,1,0:T(8,128)(2,1)S(1)}, u32[]{:S(2)}, u32[]{:S(2)}) collective-permute-start(bf16[8,128,128]{2,1,0:T(8,128)(2,1)S(1)} %pad_maximum_fusion.1.b_low), channel_id=1, source_target_pairs={{0,4},{2,6},{4,0},{6,2},{8,12},{10,14},{12,8},{14,10},{16,20},{18,... | collective-permute-start | bytes 786440 | tf_op jit(solution)/shard_map/ppermute | solution.py:241
  45.2 2.0 %collective-permute-done.7.a_high = bf16[8,128,128]{2,1,0:T(8,128)(2,1)S(1)} collective-permute-done((bf16[8,128,128]{2,1,0:T(8,128)(2,1)S(1)}, bf16[8,128,128]{2,1,0:T(8,128)(2,1)S(1)}, u32[]{:S(2)}, u32[]{:S(2)}) %collective-permute-start.7) | collective-permute-done | bytes 262176 | tf_op jit(solution)/shard_map/ppermute | solution.py:241
  47.2 3.5 %collective-permute-done.15.b_high = bf16[8,128,128]{2,1,0:T(8,128)(2,1)S(1)} collective-permute-done((bf16[8,128,128]{2,1,0:T(8,128)(2,1)S(1)}, bf16[8,128,128]{2,1,0:T(8,128)(2,1)S(1)}, u32[]{:S(2)}, u32[]{:S(2)}) %collective-permute-start.15) | collective-permute-done | bytes 262176 | tf_op jit(solution)/shard_map/ppermute | solution.py:241
  50.7 7.2 %backward.1 = (f32[16,128,128]{2,1,0:T(8,128)S(1)}, bf16[512,128]{1,0:T(8,128)(2,1)S(1)}, bf16[512,128]{1,0:T(8,128)(2,1)S(1)}, f32[16,8,128]{2,1,0:T(8,128)S(1)}) custom-call(s32[96]{0:T(128)S(1)} %copy-done.4, s32[96]{0:T(128)S(1)} %copy-done.6, s32[16]{0:T(128)S(1)} %copy-done.8, s32[1]{0:T(128)S(6)} %copy.9.count, ...), custom_call_target="tpu_custom_call" | custom-call | tf_op jit(solution)/shard_map/backward/pallas_call | solution.py:311
  57.8 8.3 %collective-permute-start.16 = (f32[16,8,128]{2,1,0:T(8,128)S(1)}, f32[16,8,128]{2,1,0:T(8,128)S(1)}, u32[]{:S(2)}, u32[]{:S(2)}) collective-permute-start(f32[16,8,128]{2,1,0:T(8,128)S(1)} %get-tuple-element.15), channel_id=1, source_target_pairs={{0,1},{1,0},{2,3},{3,2},{4,5},{5,4},{6,7},{7,6},{8,9},{9,8},{10,11... | collective-permute-start | bytes 196616 | tf_op jit(solution)/shard_map/ppermute | solution.py:337
  67.1 2.3 %collective-permute-start.17 = (bf16[576,128]{1,0:T(8,128)(2,1)S(1)}, bf16[576,128]{1,0:T(8,128)(2,1)S(1)}, u32[]{:S(2)}, u32[]{:S(2)}) collective-permute-start(bf16[576,128]{1,0:T(8,128)(2,1)S(1)} %pad_maximum_fusion.2), channel_id=1, source_target_pairs={{0,2},{2,4},{4,6},{6,8},{8,10},{10,12},{12,14},{14,16},{16,18},{18... | collective-permute-start | bytes 442376 | tf_op jit(solution)/shard_map/ppermute | solution.py:347
  69.5 1.3 %collective-permute-start.18 = (bf16[576,128]{1,0:T(8,128)(2,1)S(1)}, bf16[576,128]{1,0:T(8,128)(2,1)S(1)}, u32[]{:S(2)}, u32[]{:S(2)}) collective-permute-start(bf16[576,128]{1,0:T(8,128)(2,1)S(1)} %pad_maximum_fusion.3), channel_id=1, source_target_pairs={{2,0},{4,2},{6,4},{8,6},{10,8},{12,10},{14,12},{16,14},{18,16},{20... | collective-permute-start | bytes 442376 | tf_op jit(solution)/shard_map/ppermute | solution.py:348
  72.3 6.0 %collective-permute-done.18.from_high = bf16[576,128]{1,0:T(8,128)(2,1)S(1)} collective-permute-done((bf16[576,128]{1,0:T(8,128)(2,1)S(1)}, bf16[576,128]{1,0:T(8,128)(2,1)S(1)}, u32[]{:S(2)}, u32[]{:S(2)}) %collective-permute-start.18) | collective-permute-done | bytes 147488 | tf_op jit(solution)/shard_map/ppermute | solution.py:348
  78.3 7.7 %sweeps.1 = f32[16,128,128]{2,1,0:T(8,128)} custom-call(f32[16,128,128]{2,1,0:T(8,128)S(1)} %get-tuple-element.14.relaxed, f32[16,16,128]{2,1,0:T(8,128)S(1)} %get-tuple-element.19.strip, bf16[576,128]{1,0:T(8,128)(2,1)S(1)} %collective-permute-done.17.from_low, bf16[576,128]{1,0:T(8,128)(2,1)S(1)} %collective-permute-done.18.from_high), custom_call_target="tpu_custom_call" | custom-call | tf_op jit(solution)/shard_map/sweeps/pallas_call | solution.py:350
  (62 shorter events, 13.4 us)
Async XLA Ops:
  0.6 50.0 %copy-start.8 = (s32[16]{0:T(128)S(1)}, s32[16]{0:T(128)}, u32[]{:S(2)}) copy-start(s32[16]{0:T(128)} %owner.3) | copy-start | bytes 196
  0.6 50.0 %copy-start.6 = (s32[96]{0:T(128)S(1)}, s32[96]{0:T(128)}, u32[]{:S(2)}) copy-start(s32[96]{0:T(128)} %blocks.3) | copy-start | bytes 1156
  0.7 50.0 %copy-start.4 = (s32[96]{0:T(128)S(1)}, s32[96]{0:T(128)}, u32[]{:S(2)}) copy-start(s32[96]{0:T(128)} %tile_ids.3) | copy-start | bytes 1156
  4.5 24.9 %copy-start.2 = (f32[1,256,128]{2,1,0:T(8,128)S(1)}, f32[1,256,128]{2,1,0:T(8,128)}, u32[]{:S(2)}) copy-start(f32[1,256,128]{2,1,0:T(8,128)} %measured.3) | copy-start | bytes 393220
  4.5 46.1 %copy-start.1 = (f32[16,128,128]{2,1,0:T(8,128)S(1)}, f32[16,128,128]{2,1,0:T(8,128)}, u32[]{:S(2)}) copy-start(f32[16,128,128]{2,1,0:T(8,128)} %image.3) | copy-start | bytes 3145732
  10.0 8.1 %collective-permute-start = (bf16[8,128,128]{2,1,0:T(8,128)(2,1)S(1)}, bf16[8,128,128]{2,1,0:T(8,128)(2,1)S(1)}, u32[]{:S(2)}, u32[]{:S(2)}) collective-permute-start(bf16[8,128,128]{2,1,0:T(8,128)(2,1)S(1)} %get-tuple-element.11), channel_id=1, source_target_pairs={{0,2},{2,0},{4,6},{6,4},{8,10},{10,8},{12,14},{14,12},{16,18},{18,... | collective-permute-start | bytes 786440 | tf_op jit(solution)/shard_map/ppermute | solution.py:231
  12.2 7.4 %collective-permute-start.8 = (bf16[8,128,128]{2,1,0:T(8,128)(2,1)S(1)}, bf16[8,128,128]{2,1,0:T(8,128)(2,1)S(1)}, u32[]{:S(2)}, u32[]{:S(2)}) collective-permute-start(bf16[8,128,128]{2,1,0:T(8,128)(2,1)S(1)} %get-tuple-element.13), channel_id=1, source_target_pairs={{0,4},{2,6},{4,0},{6,2},{8,12},{10,14},{12,8},{14,10},{16,20},{18,... | collective-permute-start | bytes 786440 | tf_op jit(solution)/shard_map/ppermute | solution.py:231
  18.3 3.9 %collective-permute-start.1 = (bf16[4,128,128]{2,1,0:T(8,128)(2,1)S(1)}, bf16[4,128,128]{2,1,0:T(8,128)(2,1)S(1)}, u32[]{:S(2)}, u32[]{:S(2)}) collective-permute-start(bf16[4,128,128]{2,1,0:T(8,128)(2,1)S(1)} %slice.89), channel_id=1, source_target_pairs={{0,4},{2,6},{4,0},{6,2},{8,12},{10,14},{12,8},{14,10},{16,20},{18,... | collective-permute-start | bytes 393224 | tf_op jit(solution)/shard_map/ppermute | solution.py:231
  19.6 4.2 %collective-permute-start.9 = (bf16[4,128,128]{2,1,0:T(8,128)(2,1)S(1)}, bf16[4,128,128]{2,1,0:T(8,128)(2,1)S(1)}, u32[]{:S(2)}, u32[]{:S(2)}) collective-permute-start(bf16[4,128,128]{2,1,0:T(8,128)(2,1)S(1)} %slice.88), channel_id=1, source_target_pairs={{0,2},{2,0},{4,6},{6,4},{8,10},{10,8},{12,14},{14,12},{16,18},{18,... | collective-permute-start | bytes 393224 | tf_op jit(solution)/shard_map/ppermute | solution.py:231
  22.2 3.5 %collective-permute-start.2 = (bf16[2,128,128]{2,1,0:T(8,128)(2,1)S(1)}, bf16[2,128,128]{2,1,0:T(8,128)(2,1)S(1)}, u32[]{:S(2)}, u32[]{:S(2)}) collective-permute-start(bf16[2,128,128]{2,1,0:T(8,128)(2,1)S(1)} %slice.91), channel_id=1, source_target_pairs={{0,8},{2,10},{4,12},{6,14},{8,0},{10,2},{12,4},{14,6},{16,24},{18,... | collective-permute-start | bytes 196616 | tf_op jit(solution)/shard_map/ppermute | solution.py:231
  23.8 4.2 %collective-permute-start.10 = (bf16[2,128,128]{2,1,0:T(8,128)(2,1)S(1)}, bf16[2,128,128]{2,1,0:T(8,128)(2,1)S(1)}, u32[]{:S(2)}, u32[]{:S(2)}) collective-permute-start(bf16[2,128,128]{2,1,0:T(8,128)(2,1)S(1)} %slice.90), channel_id=1, source_target_pairs={{0,8},{2,10},{4,12},{6,14},{8,0},{10,2},{12,4},{14,6},{16,24},{18,... | collective-permute-start | bytes 196616 | tf_op jit(solution)/shard_map/ppermute | solution.py:231
  25.7 3.7 %collective-permute-start.3 = (bf16[1,128,128]{2,1,0:T(8,128)(2,1)S(1)}, bf16[1,128,128]{2,1,0:T(8,128)(2,1)S(1)}, u32[]{:S(2)}, u32[]{:S(2)}) collective-permute-start(bf16[1,128,128]{2,1,0:T(8,128)(2,1)S(1)} %slice.93), channel_id=1, source_target_pairs={{0,16},{2,18},{4,20},{6,22},{8,24},{10,26},{12,28},{14,30},{16,0},... | collective-permute-start | bytes 98312 | tf_op jit(solution)/shard_map/ppermute | solution.py:231
  28.1 3.8 %collective-permute-start.11 = (bf16[1,128,128]{2,1,0:T(8,128)(2,1)S(1)}, bf16[1,128,128]{2,1,0:T(8,128)(2,1)S(1)}, u32[]{:S(2)}, u32[]{:S(2)}) collective-permute-start(bf16[1,128,128]{2,1,0:T(8,128)(2,1)S(1)} %slice.92), channel_id=1, source_target_pairs={{0,16},{2,18},{4,20},{6,22},{8,24},{10,26},{12,28},{14,30},{16,0},... | collective-permute-start | bytes 98312 | tf_op jit(solution)/shard_map/ppermute | solution.py:231
  29.6 4.3 %collective-permute-start.4 = (bf16[1,128,128]{2,1,0:T(8,128)(2,1)S(1)}, bf16[1,128,128]{2,1,0:T(8,128)(2,1)S(1)}, u32[]{:S(2)}, u32[]{:S(2)}) collective-permute-start(bf16[1,128,128]{2,1,0:T(8,128)(2,1)S(1)} %residual.2), channel_id=1, source_target_pairs={{0,16},{2,18},{4,20},{6,22},{8,24},{10,26},{12,28},{14,30},{16,0},... | collective-permute-start | bytes 98312 | tf_op jit(solution)/shard_map/ppermute | solution.py:241
  32.0 3.7 %collective-permute-start.12 = (bf16[1,128,128]{2,1,0:T(8,128)(2,1)S(1)}, bf16[1,128,128]{2,1,0:T(8,128)(2,1)S(1)}, u32[]{:S(2)}, u32[]{:S(2)}) collective-permute-start(bf16[1,128,128]{2,1,0:T(8,128)(2,1)S(1)} %residual.3), channel_id=1, source_target_pairs={{0,16},{2,18},{4,20},{6,22},{8,24},{10,26},{12,28},{14,30},{16,0},... | collective-permute-start | bytes 98312 | tf_op jit(solution)/shard_map/ppermute | solution.py:241
  33.9 4.1 %collective-permute-start.5 = (bf16[2,128,128]{2,1,0:T(8,128)(2,1)S(1)}, bf16[2,128,128]{2,1,0:T(8,128)(2,1)S(1)}, u32[]{:S(2)}, u32[]{:S(2)}) collective-permute-start(bf16[2,128,128]{2,1,0:T(8,128)(2,1)S(1)} %pad_maximum_fusion.6), channel_id=1, source_target_pairs={{0,8},{2,10},{4,12},{6,14},{8,0},{10,2},{12,4},{14,6},{16,24},{18,... | collective-permute-start | bytes 196616 | tf_op jit(solution)/shard_map/ppermute | solution.py:241
  35.8 3.8 %collective-permute-start.13 = (bf16[2,128,128]{2,1,0:T(8,128)(2,1)S(1)}, bf16[2,128,128]{2,1,0:T(8,128)(2,1)S(1)}, u32[]{:S(2)}, u32[]{:S(2)}) collective-permute-start(bf16[2,128,128]{2,1,0:T(8,128)(2,1)S(1)} %pad_maximum_fusion.7), channel_id=1, source_target_pairs={{0,8},{2,10},{4,12},{6,14},{8,0},{10,2},{12,4},{14,6},{16,24},{18,... | collective-permute-start | bytes 196616 | tf_op jit(solution)/shard_map/ppermute | solution.py:241
  37.9 3.9 %collective-permute-start.6 = (bf16[4,128,128]{2,1,0:T(8,128)(2,1)S(1)}, bf16[4,128,128]{2,1,0:T(8,128)(2,1)S(1)}, u32[]{:S(2)}, u32[]{:S(2)}) collective-permute-start(bf16[4,128,128]{2,1,0:T(8,128)(2,1)S(1)} %pad_maximum_fusion.4), channel_id=1, source_target_pairs={{0,4},{2,6},{4,0},{6,2},{8,12},{10,14},{12,8},{14,10},{16,20},{18,... | collective-permute-start | bytes 393224 | tf_op jit(solution)/shard_map/ppermute | solution.py:241
  39.6 3.9 %collective-permute-start.14 = (bf16[4,128,128]{2,1,0:T(8,128)(2,1)S(1)}, bf16[4,128,128]{2,1,0:T(8,128)(2,1)S(1)}, u32[]{:S(2)}, u32[]{:S(2)}) collective-permute-start(bf16[4,128,128]{2,1,0:T(8,128)(2,1)S(1)} %pad_maximum_fusion.5), channel_id=1, source_target_pairs={{0,2},{2,0},{4,6},{6,4},{8,10},{10,8},{12,14},{14,12},{16,18},{18,... | collective-permute-start | bytes 393224 | tf_op jit(solution)/shard_map/ppermute | solution.py:241
  41.9 5.3 %collective-permute-start.7 = (bf16[8,128,128]{2,1,0:T(8,128)(2,1)S(1)}, bf16[8,128,128]{2,1,0:T(8,128)(2,1)S(1)}, u32[]{:S(2)}, u32[]{:S(2)}) collective-permute-start(bf16[8,128,128]{2,1,0:T(8,128)(2,1)S(1)} %pad_maximum_fusion.a_low), channel_id=1, source_target_pairs={{0,2},{2,0},{4,6},{6,4},{8,10},{10,8},{12,14},{14,12},{16,18},{18,... | collective-permute-start | bytes 786440 | tf_op jit(solution)/shard_map/ppermute | solution.py:241
  43.5 7.1 %collective-permute-start.15 = (bf16[8,128,128]{2,1,0:T(8,128)(2,1)S(1)}, bf16[8,128,128]{2,1,0:T(8,128)(2,1)S(1)}, u32[]{:S(2)}, u32[]{:S(2)}) collective-permute-start(bf16[8,128,128]{2,1,0:T(8,128)(2,1)S(1)} %pad_maximum_fusion.1.b_low), channel_id=1, source_target_pairs={{0,4},{2,6},{4,0},{6,2},{8,12},{10,14},{12,8},{14,10},{16,20},{18,... | collective-permute-start | bytes 786440 | tf_op jit(solution)/shard_map/ppermute | solution.py:241
  57.8 9.2 %collective-permute-start.16 = (f32[16,8,128]{2,1,0:T(8,128)S(1)}, f32[16,8,128]{2,1,0:T(8,128)S(1)}, u32[]{:S(2)}, u32[]{:S(2)}) collective-permute-start(f32[16,8,128]{2,1,0:T(8,128)S(1)} %get-tuple-element.15), channel_id=1, source_target_pairs={{0,1},{1,0},{2,3},{3,2},{4,5},{5,4},{6,7},{7,6},{8,9},{9,8},{10,11... | collective-permute-start | bytes 196616 | tf_op jit(solution)/shard_map/ppermute | solution.py:337
  67.1 5.2 %collective-permute-start.17 = (bf16[576,128]{1,0:T(8,128)(2,1)S(1)}, bf16[576,128]{1,0:T(8,128)(2,1)S(1)}, u32[]{:S(2)}, u32[]{:S(2)}) collective-permute-start(bf16[576,128]{1,0:T(8,128)(2,1)S(1)} %pad_maximum_fusion.2), channel_id=1, source_target_pairs={{0,2},{2,4},{4,6},{6,8},{8,10},{10,12},{12,14},{14,16},{16,18},{18... | collective-permute-start | bytes 442376 | tf_op jit(solution)/shard_map/ppermute | solution.py:347
  69.5 8.8 %collective-permute-start.18 = (bf16[576,128]{1,0:T(8,128)(2,1)S(1)}, bf16[576,128]{1,0:T(8,128)(2,1)S(1)}, u32[]{:S(2)}, u32[]{:S(2)}) collective-permute-start(bf16[576,128]{1,0:T(8,128)(2,1)S(1)} %pad_maximum_fusion.3), channel_id=1, source_target_pairs={{2,0},{4,2},{6,4},{8,6},{10,8},{12,10},{14,12},{16,14},{18,16},{20... | collective-permute-start | bytes 442376 | tf_op jit(solution)/shard_map/ppermute | solution.py:348
  (4 other events, 3.2 us)

commit v3 on v2

v3 whole, which is shorter than its diff:
```python
import functools

import jax
import jax.numpy as jnp
from jax import lax
from jax.experimental import pallas as pl
from jax.experimental.pallas import tpu as pltpu
from jax.sharding import PartitionSpec as P

TILE = 16
SWEEPS = 4
EDGE = 8
GROUP = 16
BACK_GROUP = 32

smooth_square = 0.09
flow_step = 0.04
relax_step = 4.0

VMEM = pl.BlockSpec(memory_space=pltpu.VMEM)
HBM = pl.BlockSpec(memory_space=pltpu.HBM)
PARAMS = pltpu.CompilerParams(vmem_limit_bytes=24 * 1024 * 1024)


def relative_block(bits, position):
    block = 0
    for stage, bit in enumerate(bits):
        block |= ((position >> (len(bits) - 1 - stage)) & 1) << bit
    return block


def weight_copy(weights, held, sems, group):
    span = pl.ds(group * GROUP, GROUP)
    return pltpu.make_async_copy(weights.at[span], held.at[span], sems.at[group])


def list_copies(lists, scalars):
    held, sem = scalars[:-1], scalars[-1]
    copies = [pltpu.make_async_copy(a, b, sem.at[i]) for i, (a, b) in enumerate(zip(lists, held))]
    for copy in copies:
        copy.start()
    return copies, held


def forward_kernel(
    orders, tile_ids, blocks, owner, count, image, weights,
    a_keep, a_send, b_keep, b_send, held, pixels, turned, total, image_sem, sems, *scalars,
):
    me = lax.axis_index("plane")
    lists, (tile_ids, blocks, owner, count) = list_copies((tile_ids, blocks, owner, count), scalars)
    slots, voxels, rays = held.shape
    parts = total.shape[0] - 1
    half = rays // 2
    image_copy = pltpu.make_async_copy(image, pixels, image_sem)
    image_copy.start()
    for group in range(slots // GROUP):
        weight_copy(weights, held, sems, group).start()
    total[...] = jnp.zeros_like(total)
    image_copy.wait()
    for t in range(turned.shape[0]):
        tile = pixels[:, t * TILE : (t + 1) * TILE, :].reshape(voxels, pixels.shape[2])
        turned[t] = tile.T.astype(jnp.bfloat16)

    for copy in lists:
        copy.wait()

    def step(group, carry):
        weight_copy(weights, held, sems, group).wait()
        for k in range(GROUP):
            s = group * GROUP + k
            to = jnp.where(s < count[0], owner[blocks[s]] ^ me, parts)
            total[to] += jnp.dot(
                turned[tile_ids[s]], held[s], preferred_element_type=jnp.float32
            )
        return carry

    lax.fori_loop(0, slots // GROUP, step, 0)
    for keep, send, order, low in ((a_keep, a_send, orders[0], 0), (b_keep, b_send, orders[1], half)):
        for p in range(parts // 2):
            keep[p] = total[relative_block(order, p), :, low : low + half]
            send[p] = total[relative_block(order, p + parts // 2), :, low : low + half].astype(jnp.bfloat16)


def residual_kernel(low, keep, got, measured, residual):
    half = residual.shape[1]
    projection = (keep[0] + got[0].astype(jnp.float32)).T
    mismatch = measured[0, low : low + half, :] - projection
    residual[0] = (mismatch / jnp.sqrt(1.0 + mismatch * mismatch)).astype(jnp.bfloat16)


def backward_kernel(
    orders, tile_ids, blocks, owner, count, a_low, a_high, b_low, b_high, image, weights,
    relaxed, to_near, to_far, strip, spread, total, *scalars,
):
    me = lax.axis_index("plane")
    cut = lax.axis_index("cuts")
    lists, (tile_ids, blocks, owner, count) = list_copies((tile_ids, blocks, owner, count), scalars)
    slots, voxels, rays = weights.shape
    parts = spread.shape[0]
    tiles = total.shape[0] - 1
    half = rays // 2
    rows, cols, slices = relaxed.shape
    total[...] = jnp.zeros_like(total)
    for p in range(parts // 2):
        spread[relative_block(orders[0], p), :half] = a_low[p]
        spread[relative_block(orders[0], p + parts // 2), :half] = a_high[p]
        spread[relative_block(orders[1], p), half:] = b_low[p]
        spread[relative_block(orders[1], p + parts // 2), half:] = b_high[p]

    for copy in lists:
        copy.wait()

    def step(group, carry):
        for k in range(BACK_GROUP):
            s = group * BACK_GROUP + k
            to = jnp.where(s < count[0], tile_ids[s], tiles)
            total[to] += jnp.dot(
                weights[s], spread[owner[blocks[s]] ^ me], preferred_element_type=jnp.float32
            )
        return carry

    lax.fori_loop(0, slots // BACK_GROUP, step, 0)
    for t in range(tiles):
        span = slice(t * TILE, (t + 1) * TILE)
        update = total[t].reshape(rows, TILE, slices)
        relaxed[:, span, :] = jnp.maximum(image[:, span, :] + relax_step * update, 0.0)
    even = lax.rem(me, 2) == 0
    for side, start in (
        (to_near, jnp.where(even, rows - SWEEPS, 0)),
        (to_far, jnp.where(even, 0, rows - SWEEPS)),
    ):
        for i in range(SWEEPS):
            side[i * cols : (i + 1) * cols] = relaxed[start + i].astype(jnp.bfloat16)
    lane = lax.broadcasted_iota(jnp.int32, (cols, slices), 1)
    start = jnp.where(cut == 0, slices - EDGE, 0)
    edges = jnp.zeros((cols, slices), jnp.float32)
    for i in range(rows):
        moved = pltpu.roll(relaxed[i], (i * EDGE - start + slices) % slices, 1)
        edges = jnp.where(lane // EDGE == i, moved, edges)
    strip[...] = edges.T.reshape(rows, EDGE, cols)


def shifted(x, axis, by):
    size = x.shape[axis]
    place = lax.broadcasted_iota(jnp.int32, x.shape, axis)
    if by > 0:
        return jnp.where(place == 0, 0.0, pltpu.roll(x, 1, axis))
    return jnp.where(place == size - 1, 0.0, pltpu.roll(x, size - 1, axis))


def flows(cell, below):
    rise_rows = below - cell
    rise_inner = shifted(cell, 0, -1) - cell
    rise_outer = shifted(cell, 1, -1) - cell
    scale = lax.rsqrt(
        smooth_square + rise_rows * rise_rows + rise_inner * rise_inner + rise_outer * rise_outer
    )
    return rise_rows * scale, rise_inner * scale, rise_outer * scale


def advance(cell, below, before):
    flow_rows, flow_inner, flow_outer = flows(cell, below)
    diverge = flow_rows - before
    diverge = diverge + (flow_inner - shifted(flow_inner, 0, 1))
    diverge = diverge + (flow_outer - shifted(flow_outer, 1, 1))
    return cell + flow_step * diverge, flow_rows


def inner_kernel(relaxed, strip, *refs):
    rows = relaxed.shape[0]
    fields, results, saves = refs[4:6], refs[0:2], refs[2:4]
    for field, start in zip(fields, (relaxed, strip)):
        field[...] = start[...]
    for k in range(SWEEPS):
        for field, save in zip(fields, saves):
            save[k, 0:2] = field[k : k + 2]
            save[k, 2:4] = field[rows - 2 - k : rows - k]

        def body(i, before):
            after = []
            for field, flow in zip(fields, before):
                field[i], flow = advance(field[i], field[i + 1], flow)
                after.append(flow)
            return tuple(after)

        before = tuple(flows(field[k], field[k + 1])[0] for field in fields)
        lax.fori_loop(k + 1, rows - 1 - k, body, before, unroll=3)
    for field, result in zip(fields, results):
        result[...] = field[SWEEPS : rows - SWEEPS]


def edge_kernel(
    inner, inner_strip, saved, saved_strip, from_near, from_far, volume,
    low_field, low_strip, high_field, high_strip, *, planes,
):
    rows, cols, slices = volume.shape
    me, cut = lax.axis_index("plane"), lax.axis_index("cuts")
    body_rows = SWEEPS * cols
    even = lax.rem(me, 2) == 0
    for other, this, field, strip, at in (
        (from_near, from_far, low_field, low_strip, (slice(0, 4),)),
        (from_far, from_near, high_field, high_strip, (0, slice(2, 6))),
    ):
        halo = jnp.where(even, this[...], other[...])
        field[at] = halo[:body_rows].astype(jnp.float32).reshape(SWEEPS, cols, slices)
        strip[at] = halo[body_rows:].astype(jnp.float32).reshape(SWEEPS, 2 * EDGE, cols)
    pairs = ((low_field, high_field, saved), (low_strip, high_strip, saved_strip))
    for k in range(SWEEPS):
        now, later = k % 2, (k + 1) % 2
        for low, high, save in pairs:
            low[4:6] = save[k, 0:2]
            high[now, 0:2] = save[k, 2:4]

        @pl.when(me == 0)
        def _():
            for low, _, _ in pairs:
                low[3 - k] = low[4 - k]

        @pl.when(me == planes - 1)
        def _():
            for _, high, _ in pairs:
                high[now, 2 + k] = jnp.zeros(high.shape[2:], high.dtype)

        def body(i, before):
            after = []
            for (low, high, _), (flow_low, flow_high) in zip(pairs, before):
                low[i - 1], flow_low = advance(low[i], low[i + 1], flow_low)
                high[later, i + 1], flow_high = advance(high[now, i], high[now, i + 1], flow_high)
                after.append((flow_low, flow_high))
            return tuple(after)

        before = tuple(
            (flows(low[0], low[1])[0], flows(high[now, 0], high[now, 1])[0]) for low, high, _ in pairs
        )
        lax.fori_loop(1, SWEEPS + 1, body, before, unroll=2)
    last = SWEEPS % 2
    low_side = cut == 0
    mine = jnp.concatenate([low_strip[0:4], inner_strip[...], high_strip[last, 2:6]], axis=0)
    mine = jnp.where(low_side, mine[:, :EDGE], mine[:, EDGE:])
    turned = mine.reshape(rows * EDGE, cols).T
    lane = lax.broadcasted_iota(jnp.int32, (cols, slices), 1)
    start = jnp.where(low_side, slices - EDGE, 0)
    first = jnp.where(low_side, slices - SWEEPS, 0)
    patch = (lane >= first) & (lane < first + SWEEPS)
    for i in range(rows):
        if i < SWEEPS:
            row = low_field[i]
        elif i < rows - SWEEPS:
            row = inner[i - SWEEPS]
        else:
            row = high_field[last, i - (rows - SWEEPS) + 2]
        moved = pltpu.roll(turned, (start - i * EDGE + slices) % slices, 1)
        volume[i] = jnp.where(patch, moved, row)


def sum_chain(keep, send, order, planes):
    for stage, bit in enumerate(order):
        got = lax.ppermute(send, "plane", [(i, i ^ (1 << bit)) for i in range(planes)])
        if stage == len(order) - 1:
            return keep, got
        total = keep + got.astype(jnp.float32)
        left = total.shape[0] // 2
        keep, send = total[:left], total[left:].astype(jnp.bfloat16)


def spread_chain(piece, order, planes):
    for stage, bit in reversed(list(enumerate(order))):
        got = lax.ppermute(piece, "plane", [(i, i ^ (1 << bit)) for i in range(planes)])
        if stage == 0:
            return piece, got
        piece = jnp.concatenate([piece, got], axis=0)


def per_device(
    image,
    projection_weight_tiles,
    pair_tile_index,
    pair_ray_block,
    ray_owner,
    active_pair_count,
    measured,
):
    rows, cols, slices = image.shape
    slots, voxels, rays = projection_weight_tiles.shape
    tiles = (rows // TILE) * (cols // TILE)
    planes = lax.axis_size("plane")
    parts = ray_owner.shape[0]
    half = rays // 2
    bits = planes.bit_length() - 1
    plain = tuple(range(bits))
    swapped = (1, 0) + plain[2:]
    orders = (plain, swapped)
    cut = lax.axis_index("cuts")
    shape = jax.ShapeDtypeStruct
    f32, bf16 = jnp.float32, jnp.bfloat16

    weights = pltpu.with_memory_space_constraint(projection_weight_tiles, pltpu.HBM)
    lists = [
        pltpu.with_memory_space_constraint(a, pltpu.HBM)
        for a in (pair_tile_index, pair_ray_block, ray_owner)
    ] + [active_pair_count]
    far_image = pltpu.with_memory_space_constraint(image, pltpu.HBM)
    scalars = [
        *(pltpu.SMEM(a.shape, jnp.int32) for a in (pair_tile_index, pair_ray_block, ray_owner, active_pair_count)),
        pltpu.SemaphoreType.DMA((4,)),
    ]

    kept, sent = shape((parts // 2, slices, half), f32), shape((parts // 2, slices, half), bf16)
    a_keep, a_send, b_keep, b_send, held = pl.pallas_call(
        functools.partial(forward_kernel, orders),
        out_shape=(kept, sent, kept, sent, shape(weights.shape, bf16)),
        in_specs=[HBM] * 6,
        out_specs=(VMEM,) * 5,
        scratch_shapes=[
            pltpu.VMEM((rows, cols, slices), f32),
            pltpu.VMEM((tiles, slices, voxels), bf16),
            pltpu.VMEM((parts + 1, slices, rays), f32),
            pltpu.SemaphoreType.DMA,
            pltpu.SemaphoreType.DMA((slots // GROUP,)),
            *scalars,
        ],
        compiler_params=PARAMS,
        name="forward",
    )(*lists, far_image, weights)

    pieces = []
    for low, keep, send, order in ((0, a_keep, a_send, plain), (half, b_keep, b_send, swapped)):
        keep, got = sum_chain(keep, send, order, planes)
        pieces.append(
            pl.pallas_call(
                functools.partial(residual_kernel, low),
                out_shape=shape((1, half, slices), bf16),
                in_specs=[VMEM] * 3,
                out_specs=VMEM,
                compiler_params=PARAMS,
                name="residual",
            )(keep, got, measured)
        )
    residual = jnp.concatenate(pieces, axis=1)
    a_low, a_high = spread_chain(pieces[0], plain, planes)
    b_low, b_high = spread_chain(pieces[1], swapped, planes)

    relaxed, to_near, to_far, strip = pl.pallas_call(
        functools.partial(backward_kernel, orders),
        out_shape=(
            shape((rows, cols, slices), f32),
            shape((SWEEPS * cols, slices), bf16),
            shape((SWEEPS * cols, slices), bf16),
            shape((rows, EDGE, cols), f32),
        ),
        in_specs=[HBM] * 4 + [VMEM] * 6,
        out_specs=(VMEM,) * 4,
        scratch_shapes=[
            pltpu.VMEM((parts, rays, slices), bf16),
            pltpu.VMEM((tiles + 1, voxels, slices), f32),
            *scalars,
        ],
        compiler_params=PARAMS,
        name="backward",
    )(*lists, a_low, a_high, b_low, b_high, image, held)

    other = lax.ppermute(strip, "cuts", [(0, 1), (1, 0)])
    both = jnp.where(
        cut == 0, jnp.concatenate([strip, other], 1), jnp.concatenate([other, strip], 1)
    )

    even = lax.rem(lax.axis_index("plane"), 2) == 0
    ends = both[rows - SWEEPS :], both[:SWEEPS]

    def trade(main, end_even, end_odd, pairs):
        end = jnp.where(even, end_even, end_odd).astype(bf16).reshape(-1, cols)
        return lax.ppermute(jnp.concatenate([main, end], axis=0), "plane", pairs)

    near = [(i, i ^ 1) for i in range(planes)]
    far = [(i, i + 1 if i % 2 else i - 1) for i in range(1, planes - 1)]
    from_far = trade(to_far, ends[1], ends[0], far)
    from_near = trade(to_near, ends[0], ends[1], near)

    spans = (cols, slices), (2 * EDGE, cols)
    *inner, saved, saved_strip = pl.pallas_call(
        inner_kernel,
        out_shape=[
            *(shape((rows - 2 * SWEEPS, *span), f32) for span in spans),
            *(shape((SWEEPS, 4, *span), f32) for span in spans),
        ],
        in_specs=[VMEM] * 2,
        out_specs=[VMEM] * 4,
        scratch_shapes=[pltpu.VMEM((rows, *span), f32) for span in spans],
        compiler_params=PARAMS,
        name="inner_sweeps",
    )(relaxed, both)
    volume = pl.pallas_call(
        functools.partial(edge_kernel, planes=planes),
        out_shape=shape((rows, cols, slices), f32),
        in_specs=[VMEM] * 6,
        out_specs=VMEM,
        scratch_shapes=[
            *(pltpu.VMEM((6, *span), f32) for span in spans),
            *(pltpu.VMEM((2, 6, *span), f32) for span in spans),
        ],
        compiler_params=PARAMS,
        name="edge_sweeps",
    )(*inner, saved, saved_strip, from_near, from_far)
    return (volume, residual)


def solution(mesh):
    placed = (
        P("plane", None, "cuts"),
        P("plane", None, None),
        P("plane"),
        P("plane"),
        P(),
        P("plane"),
        P("plane", None, "cuts"),
    )
    return jax.shard_map(
        per_device,
        mesh=mesh,
        in_specs=placed,
        out_specs=(P("plane", None, "cuts"), P("plane", None, "cuts")),
        check_vma=False,
    )
```

time: 87.4 us -> 81.7 us (0.935)
  waiting for transfers between devices: 22.6 us -> 17.6 us
  local copies, waits for them, and re-layouts: 3.3 us -> 0.1 us
  Pallas kernels: 20.6 us -> 22.2 us
  starting transfers between devices: 37 us -> 38 us
    ppermute x2, waiting for transfers between devices: 6.88 us -> 2.07 us  [trade(): return lax.ppermute(jnp.concatenate([main, end], axis=0), 'plane', pairs)]
    unnamed x18 -> x4, local copies, waits for them, and re-layouts: 3.2 us -> 0.01 us
    pallas_call x1, Pallas kernels: 5.51 us -> 8.11 us  [per_device(): pl.pallas_call(functools.partial(forward_kernel, orders), out_shape=(kept...]
    pallas_call x1, Pallas kernels: 7.16 us -> 5.03 us  [per_device(): pl.pallas_call(functools.partial(backward_kernel, orders), out_shape=(sha...]
    pallas_call x1 -> x2, Pallas kernels: 7.71 us -> 8.85 us  [the longest x1 4.86 us: per_device(): pl.pallas_call(functools.partial(edge_kernel, planes=planes), out_shape=s...]
  transfers between devices with their start and end apart: 19 -> 19, of which waited for: 14 -> 14; matrix products, arithmetic and copies ran while one was open for 1% -> 1% of each run, Pallas kernels for 0% -> 5%
where the time goes in v3:
time: 81.7 us; the launch traced here: 80.5 us
  starting transfers between devices  38 us (47%)
  Pallas kernels  22.2 us (27%)
  waiting for transfers between devices  17.6 us (22%)
  between operations  1.58 us (2%)
  other arithmetic  0.99 us (1%)
    ppermute x8, starting transfers between devices, spread_chain(): lax.ppermute(piece, 'plane', [(i, i ^ 1 << bit) for i in range(planes)])  12.9 us
    ppermute x8, starting transfers between devices, sum_chain(): lax.ppermute(send, 'plane', [(i, i ^ 1 << bit) for i in range(planes)])  12.2 us
    ppermute x1, starting transfers between devices, per_device(): other = lax.ppermute(strip, 'cuts', [(0, 1), (1, 0)])  8.98 us
    pallas_call x1, Pallas kernels, per_device(): pl.pallas_call(functools.partial(forward_kernel, orders), out_shape=(kept...  8.11 us
    ppermute x8, waiting for transfers between devices, spread_chain(): lax.ppermute(piece, 'plane', [(i, i ^ 1 << bit) for i in range(planes)])  7.89 us
    ppermute x8, waiting for transfers between devices, sum_chain(): lax.ppermute(send, 'plane', [(i, i ^ 1 << bit) for i in range(planes)])  6.71 us
    pallas_call x1, Pallas kernels, per_device(): pl.pallas_call(functools.partial(backward_kernel, orders), out_shape=(sha...  5.03 us
    pallas_call x1, Pallas kernels, per_device(): pl.pallas_call(functools.partial(edge_kernel, planes=planes), out_shape=s...  4.86 us
  transfers between devices with their start and end apart: 19, of which 14 were waited for; matrix products, arithmetic and copies ran while one was open for 1% of the time, Pallas kernels for 5%

profile of v3, /device:TPU:1, one launch (start us, length us, event | category | flops | bytes accessed | tf_op | source)
XLA Modules:
  0.0 80.5 jit_solution(4149411509265792759)
XLA Ops:
  1.4 8.1 %forward.1 = (f32[8,128,128]{2,1,0:T(8,128)S(1)}, bf16[8,128,128]{2,1,0:T(8,128)(2,1)S(1)}, f32[8,128,128]{2,1,0:T(8,128)S(1)}, bf16[8,128,128]{2,1,0:T(8,128)(2,1)S(1)}, bf16[96,256,256]{2,1,0:T(8,128)(2,1)S(1)}) custom-call(s32[96]{0:T(128)} %tile_ids.3, s32[96]{0:T(128)} %blocks.3, s32[16]{0:T(128)} %owner.3, s32[1]{0:T(128)S(6)} %copy.9.count, ...), custom_call_target="tpu_custom_call" | custom-call | tf_op jit(solution)/shard_map/forward/pallas_call | solution.py:309
  9.5 2.1 %collective-permute-start.8 = (bf16[8,128,128]{2,1,0:T(8,128)(2,1)S(1)}, bf16[8,128,128]{2,1,0:T(8,128)(2,1)S(1)}, u32[]{:S(2)}, u32[]{:S(2)}) collective-permute-start(bf16[8,128,128]{2,1,0:T(8,128)(2,1)S(1)} %get-tuple-element.18), channel_id=1, source_target_pairs={{0,4},{2,6},{4,0},{6,2},{8,12},{10,14},{12,8},{14,10},{16,20},{18,... | collective-permute-start | bytes 786440 | tf_op jit(solution)/shard_map/ppermute | solution.py:258
  11.6 1.3 %collective-permute-start = (bf16[8,128,128]{2,1,0:T(8,128)(2,1)S(1)}, bf16[8,128,128]{2,1,0:T(8,128)(2,1)S(1)}, u32[]{:S(2)}, u32[]{:S(2)}) collective-permute-start(bf16[8,128,128]{2,1,0:T(8,128)(2,1)S(1)} %get-tuple-element.16), channel_id=1, source_target_pairs={{0,2},{2,0},{4,6},{6,4},{8,10},{10,8},{12,14},{14,12},{16,18},{18,... | collective-permute-start | bytes 786440 | tf_op jit(solution)/shard_map/ppermute | solution.py:258
  12.9 4.7 %collective-permute-done.8 = bf16[8,128,128]{2,1,0:T(8,128)(2,1)S(1)} collective-permute-done((bf16[8,128,128]{2,1,0:T(8,128)(2,1)S(1)}, bf16[8,128,128]{2,1,0:T(8,128)(2,1)S(1)}, u32[]{:S(2)}, u32[]{:S(2)}) %collective-permute-start.8) | collective-permute-done | bytes 262176 | tf_op jit(solution)/shard_map/ppermute | solution.py:258
  17.7 1.3 %collective-permute-start.9 = (bf16[4,128,128]{2,1,0:T(8,128)(2,1)S(1)}, bf16[4,128,128]{2,1,0:T(8,128)(2,1)S(1)}, u32[]{:S(2)}, u32[]{:S(2)}) collective-permute-start(bf16[4,128,128]{2,1,0:T(8,128)(2,1)S(1)} %slice.90), channel_id=1, source_target_pairs={{0,2},{2,0},{4,6},{6,4},{8,10},{10,8},{12,14},{14,12},{16,18},{18,... | collective-permute-start | bytes 393224 | tf_op jit(solution)/shard_map/ppermute | solution.py:258
  19.0 1.3 %collective-permute-start.1 = (bf16[4,128,128]{2,1,0:T(8,128)(2,1)S(1)}, bf16[4,128,128]{2,1,0:T(8,128)(2,1)S(1)}, u32[]{:S(2)}, u32[]{:S(2)}) collective-permute-start(bf16[4,128,128]{2,1,0:T(8,128)(2,1)S(1)} %slice.91), channel_id=1, source_target_pairs={{0,4},{2,6},{4,0},{6,2},{8,12},{10,14},{12,8},{14,10},{16,20},{18,... | collective-permute-start | bytes 393224 | tf_op jit(solution)/shard_map/ppermute | solution.py:258
  21.6 1.4 %collective-permute-start.10 = (bf16[2,128,128]{2,1,0:T(8,128)(2,1)S(1)}, bf16[2,128,128]{2,1,0:T(8,128)(2,1)S(1)}, u32[]{:S(2)}, u32[]{:S(2)}) collective-permute-start(bf16[2,128,128]{2,1,0:T(8,128)(2,1)S(1)} %slice.92), channel_id=1, source_target_pairs={{0,8},{2,10},{4,12},{6,14},{8,0},{10,2},{12,4},{14,6},{16,24},{18,... | collective-permute-start | bytes 196616 | tf_op jit(solution)/shard_map/ppermute | solution.py:258
  23.3 1.3 %collective-permute-start.2 = (bf16[2,128,128]{2,1,0:T(8,128)(2,1)S(1)}, bf16[2,128,128]{2,1,0:T(8,128)(2,1)S(1)}, u32[]{:S(2)}, u32[]{:S(2)}) collective-permute-start(bf16[2,128,128]{2,1,0:T(8,128)(2,1)S(1)} %slice.93), channel_id=1, source_target_pairs={{0,8},{2,10},{4,12},{6,14},{8,0},{10,2},{12,4},{14,6},{16,24},{18,... | collective-permute-start | bytes 196616 | tf_op jit(solution)/shard_map/ppermute | solution.py:258
  25.1 2.4 %collective-permute-start.11 = (bf16[1,128,128]{2,1,0:T(8,128)(2,1)S(1)}, bf16[1,128,128]{2,1,0:T(8,128)(2,1)S(1)}, u32[]{:S(2)}, u32[]{:S(2)}) collective-permute-start(bf16[1,128,128]{2,1,0:T(8,128)(2,1)S(1)} %slice.94), channel_id=1, source_target_pairs={{0,16},{2,18},{4,20},{6,22},{8,24},{10,26},{12,28},{14,30},{16,0},... | collective-permute-start | bytes 98312 | tf_op jit(solution)/shard_map/ppermute | solution.py:258
  29.0 2.5 %collective-permute-start.12 = (bf16[1,128,128]{2,1,0:T(8,128)(2,1)S(1)}, bf16[1,128,128]{2,1,0:T(8,128)(2,1)S(1)}, u32[]{:S(2)}, u32[]{:S(2)}) collective-permute-start(bf16[1,128,128]{2,1,0:T(8,128)(2,1)S(1)} %residual.3), channel_id=1, source_target_pairs={{0,16},{2,18},{4,20},{6,22},{8,24},{10,26},{12,28},{14,30},{16,0},... | collective-permute-start | bytes 98312 | tf_op jit(solution)/shard_map/ppermute | solution.py:268
  33.3 1.3 %collective-permute-start.13 = (bf16[2,128,128]{2,1,0:T(8,128)(2,1)S(1)}, bf16[2,128,128]{2,1,0:T(8,128)(2,1)S(1)}, u32[]{:S(2)}, u32[]{:S(2)}) collective-permute-start(bf16[2,128,128]{2,1,0:T(8,128)(2,1)S(1)} %pad_maximum_fusion.7), channel_id=1, source_target_pairs={{0,8},{2,10},{4,12},{6,14},{8,0},{10,2},{12,4},{14,6},{16,24},{18,... | collective-permute-start | bytes 196616 | tf_op jit(solution)/shard_map/ppermute | solution.py:268
  35.3 2.1 %collective-permute-start.5 = (bf16[2,128,128]{2,1,0:T(8,128)(2,1)S(1)}, bf16[2,128,128]{2,1,0:T(8,128)(2,1)S(1)}, u32[]{:S(2)}, u32[]{:S(2)}) collective-permute-start(bf16[2,128,128]{2,1,0:T(8,128)(2,1)S(1)} %pad_maximum_fusion.6), channel_id=1, source_target_pairs={{0,8},{2,10},{4,12},{6,14},{8,0},{10,2},{12,4},{14,6},{16,24},{18,... | collective-permute-start | bytes 196616 | tf_op jit(solution)/shard_map/ppermute | solution.py:268
  37.4 1.4 %collective-permute-start.14 = (bf16[4,128,128]{2,1,0:T(8,128)(2,1)S(1)}, bf16[4,128,128]{2,1,0:T(8,128)(2,1)S(1)}, u32[]{:S(2)}, u32[]{:S(2)}) collective-permute-start(bf16[4,128,128]{2,1,0:T(8,128)(2,1)S(1)} %pad_maximum_fusion.5), channel_id=1, source_target_pairs={{0,2},{2,0},{4,6},{6,4},{8,10},{10,8},{12,14},{14,12},{16,18},{18,... | collective-permute-start | bytes 393224 | tf_op jit(solution)/shard_map/ppermute | solution.py:268
  39.1 1.4 %collective-permute-start.6 = (bf16[4,128,128]{2,1,0:T(8,128)(2,1)S(1)}, bf16[4,128,128]{2,1,0:T(8,128)(2,1)S(1)}, u32[]{:S(2)}, u32[]{:S(2)}) collective-permute-start(bf16[4,128,128]{2,1,0:T(8,128)(2,1)S(1)} %pad_maximum_fusion.4), channel_id=1, source_target_pairs={{0,4},{2,6},{4,0},{6,2},{8,12},{10,14},{12,8},{14,10},{16,20},{18,... | collective-permute-start | bytes 393224 | tf_op jit(solution)/shard_map/ppermute | solution.py:268
  41.4 1.4 %collective-permute-start.15 = (bf16[8,128,128]{2,1,0:T(8,128)(2,1)S(1)}, bf16[8,128,128]{2,1,0:T(8,128)(2,1)S(1)}, u32[]{:S(2)}, u32[]{:S(2)}) collective-permute-start(bf16[8,128,128]{2,1,0:T(8,128)(2,1)S(1)} %pad_maximum_fusion.1.b_low), channel_id=1, source_target_pairs={{0,4},{2,6},{4,0},{6,2},{8,12},{10,14},{12,8},{14,10},{16,20},{18,... | collective-permute-start | bytes 786440 | tf_op jit(solution)/shard_map/ppermute | solution.py:268
  43.1 1.6 %collective-permute-start.7 = (bf16[8,128,128]{2,1,0:T(8,128)(2,1)S(1)}, bf16[8,128,128]{2,1,0:T(8,128)(2,1)S(1)}, u32[]{:S(2)}, u32[]{:S(2)}) collective-permute-start(bf16[8,128,128]{2,1,0:T(8,128)(2,1)S(1)} %pad_maximum_fusion.a_low), channel_id=1, source_target_pairs={{0,2},{2,0},{4,6},{6,4},{8,10},{10,8},{12,14},{14,12},{16,18},{18,... | collective-permute-start | bytes 786440 | tf_op jit(solution)/shard_map/ppermute | solution.py:268
  44.7 2.0 %collective-permute-done.15.b_high = bf16[8,128,128]{2,1,0:T(8,128)(2,1)S(1)} collective-permute-done((bf16[8,128,128]{2,1,0:T(8,128)(2,1)S(1)}, bf16[8,128,128]{2,1,0:T(8,128)(2,1)S(1)}, u32[]{:S(2)}, u32[]{:S(2)}) %collective-permute-start.15) | collective-permute-done | bytes 262176 | tf_op jit(solution)/shard_map/ppermute | solution.py:268
  46.7 3.3 %collective-permute-done.7.a_high = bf16[8,128,128]{2,1,0:T(8,128)(2,1)S(1)} collective-permute-done((bf16[8,128,128]{2,1,0:T(8,128)(2,1)S(1)}, bf16[8,128,128]{2,1,0:T(8,128)(2,1)S(1)}, u32[]{:S(2)}, u32[]{:S(2)}) %collective-permute-start.7) | collective-permute-done | bytes 262176 | tf_op jit(solution)/shard_map/ppermute | solution.py:268
  50.0 5.0 %backward.1 = (f32[16,128,128]{2,1,0:T(8,128)S(1)}, bf16[512,128]{1,0:T(8,128)(2,1)S(1)}, bf16[512,128]{1,0:T(8,128)(2,1)S(1)}, f32[16,8,128]{2,1,0:T(8,128)S(1)}) custom-call(s32[96]{0:T(128)} %tile_ids.3, s32[96]{0:T(128)} %blocks.3, s32[16]{0:T(128)} %owner.3, s32[1]{0:T(128)S(6)} %copy.9.count, bf16[8,128,128]{2,1,0:T(8,128)(2,1)S(1)} %pad_maximum_fusion.a_low, ...), custom_call_target="tpu_custom_call" | custom-call | tf_op jit(solution)/shard_map/backward/pallas_call | solution.py:343
  55.0 9.0 %collective-permute-start.16 = (f32[16,8,128]{2,1,0:T(8,128)S(1)}, f32[16,8,128]{2,1,0:T(8,128)S(1)}, u32[]{:S(2)}, u32[]{:S(2)}) collective-permute-start(f32[16,8,128]{2,1,0:T(8,128)S(1)} %get-tuple-element.21), channel_id=1, source_target_pairs={{0,1},{1,0},{2,3},{3,2},{4,5},{5,4},{6,7},{7,6},{8,9},{9,8},{10,11... | collective-permute-start | bytes 196616 | tf_op jit(solution)/shard_map/ppermute | solution.py:362
  65.6 3.2 %collective-permute-start.17 = (bf16[576,128]{1,0:T(8,128)(2,1)S(1)}, bf16[576,128]{1,0:T(8,128)(2,1)S(1)}, u32[]{:S(2)}, u32[]{:S(2)}) collective-permute-start(bf16[576,128]{1,0:T(8,128)(2,1)S(1)} %pad_maximum_fusion.2), channel_id=1, source_target_pairs={{0,2},{2,0},{4,6},{6,4},{8,10},{10,8},{12,14},{14,12},{16,18},{18,... | collective-permute-start | bytes 442376 | tf_op jit(solution)/shard_map/ppermute | solution.py:372
  69.5 4.0 %inner_sweeps.1 = (f32[8,128,128]{2,1,0:T(8,128)S(1)}, f32[8,16,128]{2,1,0:T(8,128)S(1)}, f32[4,4,128,128]{3,2,1,0:T(8,128)S(1)}, f32[4,4,16,128]{3,2,1,0:T(8,128)S(1)}) custom-call(f32[16,128,128]{2,1,0:T(8,128)S(1)} %get-tuple-element.20.relaxed, f32[16,16,128]{2,1,0:T(8,128)S(1)} %maximum_select_fusion.strip), custom_call_target="tpu_custom_call" | custom-call | tf_op jit(solution)/shard_map/inner_sweeps/pallas_call | solution.py:380
  73.5 2.1 %collective-permute-done.17.from_near = bf16[576,128]{1,0:T(8,128)(2,1)S(1)} collective-permute-done((bf16[576,128]{1,0:T(8,128)(2,1)S(1)}, bf16[576,128]{1,0:T(8,128)(2,1)S(1)}, u32[]{:S(2)}, u32[]{:S(2)}) %collective-permute-start.17) | collective-permute-done | bytes 147488 | tf_op jit(solution)/shard_map/ppermute | solution.py:372
  75.6 4.9 %edge_sweeps.1 = f32[16,128,128]{2,1,0:T(8,128)} custom-call(f32[8,128,128]{2,1,0:T(8,128)S(1)} %get-tuple-element.22.inner, f32[8,16,128]{2,1,0:T(8,128)S(1)} %get-tuple-element.23.inner_strip, f32[4,4,128,128]{3,2,1,0:T(8,128)S(1)} %get-tuple-element.24.saved, f32[4,4,16,128]{3,2,1,0:T(8,128)S(1)} %get-tuple-element.25.saved_strip, ...), custom_call_target="tpu_custom_call" | custom-call | tf_op jit(solution)/shard_map/edge_sweeps/pallas_call | solution.py:392
  (49 shorter events, 9.8 us)
Async XLA Ops:
  0.6 49.3 %copy-start = (f32[16,128,128]{2,1,0:T(8,128)S(1)}, f32[16,128,128]{2,1,0:T(8,128)}, u32[]{:S(2)}) copy-start(f32[16,128,128]{2,1,0:T(8,128)} %image.3) | copy-start | bytes 3145732
  0.6 28.2 %copy-start.1 = (f32[1,256,128]{2,1,0:T(8,128)S(1)}, f32[1,256,128]{2,1,0:T(8,128)}, u32[]{:S(2)}) copy-start(f32[1,256,128]{2,1,0:T(8,128)} %measured.3) | copy-start | bytes 393220
  9.5 8.1 %collective-permute-start.8 = (bf16[8,128,128]{2,1,0:T(8,128)(2,1)S(1)}, bf16[8,128,128]{2,1,0:T(8,128)(2,1)S(1)}, u32[]{:S(2)}, u32[]{:S(2)}) collective-permute-start(bf16[8,128,128]{2,1,0:T(8,128)(2,1)S(1)} %get-tuple-element.18), channel_id=1, source_target_pairs={{0,4},{2,6},{4,0},{6,2},{8,12},{10,14},{12,8},{14,10},{16,20},{18,... | collective-permute-start | bytes 786440 | tf_op jit(solution)/shard_map/ppermute | solution.py:258
  11.6 7.3 %collective-permute-start = (bf16[8,128,128]{2,1,0:T(8,128)(2,1)S(1)}, bf16[8,128,128]{2,1,0:T(8,128)(2,1)S(1)}, u32[]{:S(2)}, u32[]{:S(2)}) collective-permute-start(bf16[8,128,128]{2,1,0:T(8,128)(2,1)S(1)} %get-tuple-element.16), channel_id=1, source_target_pairs={{0,2},{2,0},{4,6},{6,4},{8,10},{10,8},{12,14},{14,12},{16,18},{18,... | collective-permute-start | bytes 786440 | tf_op jit(solution)/shard_map/ppermute | solution.py:258
  17.7 3.9 %collective-permute-start.9 = (bf16[4,128,128]{2,1,0:T(8,128)(2,1)S(1)}, bf16[4,128,128]{2,1,0:T(8,128)(2,1)S(1)}, u32[]{:S(2)}, u32[]{:S(2)}) collective-permute-start(bf16[4,128,128]{2,1,0:T(8,128)(2,1)S(1)} %slice.90), channel_id=1, source_target_pairs={{0,2},{2,0},{4,6},{6,4},{8,10},{10,8},{12,14},{14,12},{16,18},{18,... | collective-permute-start | bytes 393224 | tf_op jit(solution)/shard_map/ppermute | solution.py:258
  19.0 4.2 %collective-permute-start.1 = (bf16[4,128,128]{2,1,0:T(8,128)(2,1)S(1)}, bf16[4,128,128]{2,1,0:T(8,128)(2,1)S(1)}, u32[]{:S(2)}, u32[]{:S(2)}) collective-permute-start(bf16[4,128,128]{2,1,0:T(8,128)(2,1)S(1)} %slice.91), channel_id=1, source_target_pairs={{0,4},{2,6},{4,0},{6,2},{8,12},{10,14},{12,8},{14,10},{16,20},{18,... | collective-permute-start | bytes 393224 | tf_op jit(solution)/shard_map/ppermute | solution.py:258
  21.6 3.5 %collective-permute-start.10 = (bf16[2,128,128]{2,1,0:T(8,128)(2,1)S(1)}, bf16[2,128,128]{2,1,0:T(8,128)(2,1)S(1)}, u32[]{:S(2)}, u32[]{:S(2)}) collective-permute-start(bf16[2,128,128]{2,1,0:T(8,128)(2,1)S(1)} %slice.92), channel_id=1, source_target_pairs={{0,8},{2,10},{4,12},{6,14},{8,0},{10,2},{12,4},{14,6},{16,24},{18,... | collective-permute-start | bytes 196616 | tf_op jit(solution)/shard_map/ppermute | solution.py:258
  23.3 4.2 %collective-permute-start.2 = (bf16[2,128,128]{2,1,0:T(8,128)(2,1)S(1)}, bf16[2,128,128]{2,1,0:T(8,128)(2,1)S(1)}, u32[]{:S(2)}, u32[]{:S(2)}) collective-permute-start(bf16[2,128,128]{2,1,0:T(8,128)(2,1)S(1)} %slice.93), channel_id=1, source_target_pairs={{0,8},{2,10},{4,12},{6,14},{8,0},{10,2},{12,4},{14,6},{16,24},{18,... | collective-permute-start | bytes 196616 | tf_op jit(solution)/shard_map/ppermute | solution.py:258
  25.1 3.7 %collective-permute-start.11 = (bf16[1,128,128]{2,1,0:T(8,128)(2,1)S(1)}, bf16[1,128,128]{2,1,0:T(8,128)(2,1)S(1)}, u32[]{:S(2)}, u32[]{:S(2)}) collective-permute-start(bf16[1,128,128]{2,1,0:T(8,128)(2,1)S(1)} %slice.94), channel_id=1, source_target_pairs={{0,16},{2,18},{4,20},{6,22},{8,24},{10,26},{12,28},{14,30},{16,0},... | collective-permute-start | bytes 98312 | tf_op jit(solution)/shard_map/ppermute | solution.py:258
  27.5 3.9 %collective-permute-start.3 = (bf16[1,128,128]{2,1,0:T(8,128)(2,1)S(1)}, bf16[1,128,128]{2,1,0:T(8,128)(2,1)S(1)}, u32[]{:S(2)}, u32[]{:S(2)}) collective-permute-start(bf16[1,128,128]{2,1,0:T(8,128)(2,1)S(1)} %slice.95), channel_id=1, source_target_pairs={{0,16},{2,18},{4,20},{6,22},{8,24},{10,26},{12,28},{14,30},{16,0},... | collective-permute-start | bytes 98312 | tf_op jit(solution)/shard_map/ppermute | solution.py:258
  29.0 4.3 %collective-permute-start.12 = (bf16[1,128,128]{2,1,0:T(8,128)(2,1)S(1)}, bf16[1,128,128]{2,1,0:T(8,128)(2,1)S(1)}, u32[]{:S(2)}, u32[]{:S(2)}) collective-permute-start(bf16[1,128,128]{2,1,0:T(8,128)(2,1)S(1)} %residual.3), channel_id=1, source_target_pairs={{0,16},{2,18},{4,20},{6,22},{8,24},{10,26},{12,28},{14,30},{16,0},... | collective-permute-start | bytes 98312 | tf_op jit(solution)/shard_map/ppermute | solution.py:268
  31.6 3.7 %collective-permute-start.4 = (bf16[1,128,128]{2,1,0:T(8,128)(2,1)S(1)}, bf16[1,128,128]{2,1,0:T(8,128)(2,1)S(1)}, u32[]{:S(2)}, u32[]{:S(2)}) collective-permute-start(bf16[1,128,128]{2,1,0:T(8,128)(2,1)S(1)} %residual.2), channel_id=1, source_target_pairs={{0,16},{2,18},{4,20},{6,22},{8,24},{10,26},{12,28},{14,30},{16,0},... | collective-permute-start | bytes 98312 | tf_op jit(solution)/shard_map/ppermute | solution.py:268
  33.3 4.1 %collective-permute-start.13 = (bf16[2,128,128]{2,1,0:T(8,128)(2,1)S(1)}, bf16[2,128,128]{2,1,0:T(8,128)(2,1)S(1)}, u32[]{:S(2)}, u32[]{:S(2)}) collective-permute-start(bf16[2,128,128]{2,1,0:T(8,128)(2,1)S(1)} %pad_maximum_fusion.7), channel_id=1, source_target_pairs={{0,8},{2,10},{4,12},{6,14},{8,0},{10,2},{12,4},{14,6},{16,24},{18,... | collective-permute-start | bytes 196616 | tf_op jit(solution)/shard_map/ppermute | solution.py:268
  35.3 3.7 %collective-permute-start.5 = (bf16[2,128,128]{2,1,0:T(8,128)(2,1)S(1)}, bf16[2,128,128]{2,1,0:T(8,128)(2,1)S(1)}, u32[]{:S(2)}, u32[]{:S(2)}) collective-permute-start(bf16[2,128,128]{2,1,0:T(8,128)(2,1)S(1)} %pad_maximum_fusion.6), channel_id=1, source_target_pairs={{0,8},{2,10},{4,12},{6,14},{8,0},{10,2},{12,4},{14,6},{16,24},{18,... | collective-permute-start | bytes 196616 | tf_op jit(solution)/shard_map/ppermute | solution.py:268
  37.4 3.9 %collective-permute-start.14 = (bf16[4,128,128]{2,1,0:T(8,128)(2,1)S(1)}, bf16[4,128,128]{2,1,0:T(8,128)(2,1)S(1)}, u32[]{:S(2)}, u32[]{:S(2)}) collective-permute-start(bf16[4,128,128]{2,1,0:T(8,128)(2,1)S(1)} %pad_maximum_fusion.5), channel_id=1, source_target_pairs={{0,2},{2,0},{4,6},{6,4},{8,10},{10,8},{12,14},{14,12},{16,18},{18,... | collective-permute-start | bytes 393224 | tf_op jit(solution)/shard_map/ppermute | solution.py:268
  39.1 4.0 %collective-permute-start.6 = (bf16[4,128,128]{2,1,0:T(8,128)(2,1)S(1)}, bf16[4,128,128]{2,1,0:T(8,128)(2,1)S(1)}, u32[]{:S(2)}, u32[]{:S(2)}) collective-permute-start(bf16[4,128,128]{2,1,0:T(8,128)(2,1)S(1)} %pad_maximum_fusion.4), channel_id=1, source_target_pairs={{0,4},{2,6},{4,0},{6,2},{8,12},{10,14},{12,8},{14,10},{16,20},{18,... | collective-permute-start | bytes 393224 | tf_op jit(solution)/shard_map/ppermute | solution.py:268
  41.4 5.3 %collective-permute-start.15 = (bf16[8,128,128]{2,1,0:T(8,128)(2,1)S(1)}, bf16[8,128,128]{2,1,0:T(8,128)(2,1)S(1)}, u32[]{:S(2)}, u32[]{:S(2)}) collective-permute-start(bf16[8,128,128]{2,1,0:T(8,128)(2,1)S(1)} %pad_maximum_fusion.1.b_low), channel_id=1, source_target_pairs={{0,4},{2,6},{4,0},{6,2},{8,12},{10,14},{12,8},{14,10},{16,20},{18,... | collective-permute-start | bytes 786440 | tf_op jit(solution)/shard_map/ppermute | solution.py:268
  43.1 6.9 %collective-permute-start.7 = (bf16[8,128,128]{2,1,0:T(8,128)(2,1)S(1)}, bf16[8,128,128]{2,1,0:T(8,128)(2,1)S(1)}, u32[]{:S(2)}, u32[]{:S(2)}) collective-permute-start(bf16[8,128,128]{2,1,0:T(8,128)(2,1)S(1)} %pad_maximum_fusion.a_low), channel_id=1, source_target_pairs={{0,2},{2,0},{4,6},{6,4},{8,10},{10,8},{12,14},{14,12},{16,18},{18,... | collective-permute-start | bytes 786440 | tf_op jit(solution)/shard_map/ppermute | solution.py:268
  55.0 9.9 %collective-permute-start.16 = (f32[16,8,128]{2,1,0:T(8,128)S(1)}, f32[16,8,128]{2,1,0:T(8,128)S(1)}, u32[]{:S(2)}, u32[]{:S(2)}) collective-permute-start(f32[16,8,128]{2,1,0:T(8,128)S(1)} %get-tuple-element.21), channel_id=1, source_target_pairs={{0,1},{1,0},{2,3},{3,2},{4,5},{5,4},{6,7},{7,6},{8,9},{9,8},{10,11... | collective-permute-start | bytes 196616 | tf_op jit(solution)/shard_map/ppermute | solution.py:362
  64.9 8.6 %collective-permute-start.18 = (bf16[576,128]{1,0:T(8,128)(2,1)S(1)}, bf16[576,128]{1,0:T(8,128)(2,1)S(1)}, u32[]{:S(2)}, u32[]{:S(2)}) collective-permute-start(bf16[576,128]{1,0:T(8,128)(2,1)S(1)} %pad_maximum_fusion.3), channel_id=1, source_target_pairs={{2,4},{4,2},{6,8},{8,6},{10,12},{12,10},{14,16},{16,14},{18,20},{2... | collective-permute-start | bytes 442376 | tf_op jit(solution)/shard_map/ppermute | solution.py:372
  65.6 10.0 %collective-permute-start.17 = (bf16[576,128]{1,0:T(8,128)(2,1)S(1)}, bf16[576,128]{1,0:T(8,128)(2,1)S(1)}, u32[]{:S(2)}, u32[]{:S(2)}) collective-permute-start(bf16[576,128]{1,0:T(8,128)(2,1)S(1)} %pad_maximum_fusion.2), channel_id=1, source_target_pairs={{0,2},{2,0},{4,6},{6,4},{8,10},{10,8},{12,14},{14,12},{16,18},{18,... | collective-permute-start | bytes 442376 | tf_op jit(solution)/shard_map/ppermute | solution.py:372

commit v4 on v3

--- a/solution.py
+++ b/solution.py
@@ -10,8 +10,9 @@
 TILE = 16
 SWEEPS = 4
 EDGE = 8
-GROUP = 16
-BACK_GROUP = 32
+FETCH = 8
+FORWARD_GROUP = 16
+BACKWARD_GROUP = 48
 
 smooth_square = 0.09
 flow_step = 0.04
@@ -30,7 +31,7 @@
 
 
 def weight_copy(weights, held, sems, group):
-    span = pl.ds(group * GROUP, GROUP)
+    span = pl.ds(group * FETCH, FETCH)
     return pltpu.make_async_copy(weights.at[span], held.at[span], sems.at[group])
 
 
@@ -44,37 +45,45 @@
 
 def forward_kernel(
     orders, tile_ids, blocks, owner, count, image, weights,
-    a_keep, a_send, b_keep, b_send, held, pixels, turned, total, image_sem, sems, *scalars,
+    a_keep, a_send, b_keep, b_send, held, pixels, turned, total, image_sems, sems, *scalars,
 ):
     me = lax.axis_index("plane")
     lists, (tile_ids, blocks, owner, count) = list_copies((tile_ids, blocks, owner, count), scalars)
     slots, voxels, rays = held.shape
     parts = total.shape[0] - 1
     half = rays // 2
-    image_copy = pltpu.make_async_copy(image, pixels, image_sem)
-    image_copy.start()
-    for group in range(slots // GROUP):
-        weight_copy(weights, held, sems, group).start()
+    tiles = turned.shape[0]
+    image_copies = []
+    for t in range(tiles):
+        part = (slice(None), pl.ds(t * TILE, TILE))
+        copy = pltpu.make_async_copy(image.at[part], pixels.at[part], image_sems.at[t])
+        copy.start()
+        image_copies.append(copy)
+    for fetch in range(1):
+        weight_copy(weights, held, sems, fetch).start()
     total[...] = jnp.zeros_like(total)
-    image_copy.wait()
-    for t in range(turned.shape[0]):
+    for copy in image_copies:
+        copy.wait()
+    for fetch in range(1, slots // FETCH):
+        weight_copy(weights, held, sems, fetch).start()
+    for t in range(tiles):
         tile = pixels[:, t * TILE : (t + 1) * TILE, :].reshape(voxels, pixels.shape[2])
         turned[t] = tile.T.astype(jnp.bfloat16)
-
     for copy in lists:
         copy.wait()
 
     def step(group, carry):
-        weight_copy(weights, held, sems, group).wait()
-        for k in range(GROUP):
-            s = group * GROUP + k
+        for fetch in range(FORWARD_GROUP // FETCH):
+            weight_copy(weights, held, sems, group * (FORWARD_GROUP // FETCH) + fetch).wait()
+        for k in range(FORWARD_GROUP):
+            s = group * FORWARD_GROUP + k
             to = jnp.where(s < count[0], owner[blocks[s]] ^ me, parts)
             total[to] += jnp.dot(
                 turned[tile_ids[s]], held[s], preferred_element_type=jnp.float32
             )
         return carry
 
-    lax.fori_loop(0, slots // GROUP, step, 0)
+    lax.fori_loop(0, slots // FORWARD_GROUP, step, 0)
     for keep, send, order, low in ((a_keep, a_send, orders[0], 0), (b_keep, b_send, orders[1], half)):
         for p in range(parts // 2):
             keep[p] = total[relative_block(order, p), :, low : low + half]
@@ -111,15 +120,15 @@
         copy.wait()
 
     def step(group, carry):
-        for k in range(BACK_GROUP):
-            s = group * BACK_GROUP + k
+        for k in range(BACKWARD_GROUP):
+            s = group * BACKWARD_GROUP + k
             to = jnp.where(s < count[0], tile_ids[s], tiles)
             total[to] += jnp.dot(
                 weights[s], spread[owner[blocks[s]] ^ me], preferred_element_type=jnp.float32
             )
         return carry
 
-    lax.fori_loop(0, slots // BACK_GROUP, step, 0)
+    lax.fori_loop(0, slots // BACKWARD_GROUP, step, 0)
     for t in range(tiles):
         span = slice(t * TILE, (t + 1) * TILE)
         update = total[t].reshape(rows, TILE, slices)
@@ -166,9 +175,25 @@
     return cell + flow_step * diverge, flow_rows
 
 
+def patched(rows, strips, cut):
+    count, _, cols = strips.shape
+    slices = rows[0].shape[1]
+    low_side = cut == 0
+    mine = jnp.where(low_side, strips[:, :EDGE], strips[:, EDGE:]).reshape(count * EDGE, cols)
+    turned = jnp.concatenate([mine] * (slices // (count * EDGE)), axis=0).T
+    lane = lax.broadcasted_iota(jnp.int32, (cols, slices), 1)
+    start = jnp.where(low_side, slices - EDGE, 0)
+    first = jnp.where(low_side, slices - SWEEPS, 0)
+    patch = (lane >= first) & (lane < first + SWEEPS)
+    return [
+        jnp.where(patch, pltpu.roll(turned, (start - i * EDGE + slices) % slices, 1), row)
+        for i, row in enumerate(rows)
+    ]
+
+
 def inner_kernel(relaxed, strip, *refs):
     rows = relaxed.shape[0]
-    fields, results, saves = refs[4:6], refs[0:2], refs[2:4]
+    result, saves, fields = refs[0], refs[1:3], refs[3:5]
     for field, start in zip(fields, (relaxed, strip)):
         field[...] = start[...]
     for k in range(SWEEPS):
@@ -185,16 +210,20 @@
 
         before = tuple(flows(field[k], field[k + 1])[0] for field in fields)
         lax.fori_loop(k + 1, rows - 1 - k, body, before, unroll=3)
-    for field, result in zip(fields, results):
-        result[...] = field[SWEEPS : rows - SWEEPS]
+    inner = [fields[0][i] for i in range(SWEEPS, rows - SWEEPS)]
+    strips = fields[1][SWEEPS : rows - SWEEPS]
+    for i, row in enumerate(patched(inner, strips, lax.axis_index("cuts"))):
+        result[i] = row
 
 
 def edge_kernel(
-    inner, inner_strip, saved, saved_strip, from_near, from_far, volume,
-    low_field, low_strip, high_field, high_strip, *, planes,
+    inner, saved, saved_strip, from_near, from_far, volume,
+    low_field, low_strip, high_field, high_strip, ends, sems, *, planes,
 ):
     rows, cols, slices = volume.shape
     me, cut = lax.axis_index("plane"), lax.axis_index("cuts")
+    inner_copy = pltpu.make_async_copy(inner, volume.at[pl.ds(SWEEPS, rows - 2 * SWEEPS)], sems.at[0])
+    inner_copy.start()
     body_rows = SWEEPS * cols
     even = lax.rem(me, 2) == 0
     for other, this, field, strip, at in (
@@ -234,23 +263,19 @@
         )
         lax.fori_loop(1, SWEEPS + 1, body, before, unroll=2)
     last = SWEEPS % 2
-    low_side = cut == 0
-    mine = jnp.concatenate([low_strip[0:4], inner_strip[...], high_strip[last, 2:6]], axis=0)
-    mine = jnp.where(low_side, mine[:, :EDGE], mine[:, EDGE:])
-    turned = mine.reshape(rows * EDGE, cols).T
-    lane = lax.broadcasted_iota(jnp.int32, (cols, slices), 1)
-    start = jnp.where(low_side, slices - EDGE, 0)
-    first = jnp.where(low_side, slices - SWEEPS, 0)
-    patch = (lane >= first) & (lane < first + SWEEPS)
-    for i in range(rows):
-        if i < SWEEPS:
-            row = low_field[i]
-        elif i < rows - SWEEPS:
-            row = inner[i - SWEEPS]
-        else:
-            row = high_field[last, i - (rows - SWEEPS) + 2]
-        moved = pltpu.roll(turned, (start - i * EDGE + slices) % slices, 1)
-        volume[i] = jnp.where(patch, moved, row)
+    outer = [low_field[i] for i in range(SWEEPS)] + [high_field[last, 2 + i] for i in range(SWEEPS)]
+    strips = jnp.concatenate([low_strip[0:4], high_strip[last, 2:6]], axis=0)
+    for i, row in enumerate(patched(outer, strips, cut)):
+        ends[i] = row
+    copies = [
+        inner_copy,
+        pltpu.make_async_copy(ends.at[pl.ds(0, SWEEPS)], volume.at[pl.ds(0, SWEEPS)], sems.at[1]),
+        pltpu.make_async_copy(ends.at[pl.ds(SWEEPS, SWEEPS)], volume.at[pl.ds(rows - SWEEPS, SWEEPS)], sems.at[2]),
+    ]
+    for copy in copies[1:]:
+        copy.start()
+    for copy in copies:
+        copy.wait()
 
 
 def sum_chain(keep, send, order, planes):
@@ -301,22 +326,21 @@
     ] + [active_pair_count]
     far_image = pltpu.with_memory_space_constraint(image, pltpu.HBM)
     scalars = [
-        *(pltpu.SMEM(a.shape, jnp.int32) for a in (pair_tile_index, pair_ray_block, ray_owner, active_pair_count)),
+        *(pltpu.SMEM(a.shape, jnp.int32) for a in lists),
         pltpu.SemaphoreType.DMA((4,)),
     ]
 
     kept, sent = shape((parts // 2, slices, half), f32), shape((parts // 2, slices, half), bf16)
-    a_keep, a_send, b_keep, b_send, held = pl.pallas_call(
+    a_keep, a_send, b_keep, b_send, held, pixels = pl.pallas_call(
         functools.partial(forward_kernel, orders),
-        out_shape=(kept, sent, kept, sent, shape(weights.shape, bf16)),
+        out_shape=(kept, sent, kept, sent, shape(weights.shape, bf16), shape(image.shape, f32)),
         in_specs=[HBM] * 6,
-        out_specs=(VMEM,) * 5,
+        out_specs=(VMEM,) * 6,
         scratch_shapes=[
-            pltpu.VMEM((rows, cols, slices), f32),
             pltpu.VMEM((tiles, slices, voxels), bf16),
             pltpu.VMEM((parts + 1, slices, rays), f32),
-            pltpu.SemaphoreType.DMA,
-            pltpu.SemaphoreType.DMA((slots // GROUP,)),
+            pltpu.SemaphoreType.DMA((tiles,)),
+            pltpu.SemaphoreType.DMA((slots // FETCH,)),
             *scalars,
         ],
         compiler_params=PARAMS,
@@ -357,7 +381,7 @@
         ],
         compiler_params=PARAMS,
         name="backward",
-    )(*lists, a_low, a_high, b_low, b_high, image, held)
+    )(*lists, a_low, a_high, b_low, b_high, pixels, held)
 
     other = lax.ppermute(strip, "cuts", [(0, 1), (1, 0)])
     both = jnp.where(
@@ -377,14 +401,14 @@
     from_near = trade(to_near, ends[0], ends[1], near)
 
     spans = (cols, slices), (2 * EDGE, cols)
-    *inner, saved, saved_strip = pl.pallas_call(
+    inner, saved, saved_strip = pl.pallas_call(
         inner_kernel,
         out_shape=[
-            *(shape((rows - 2 * SWEEPS, *span), f32) for span in spans),
+            shape((rows - 2 * SWEEPS, cols, slices), f32),
             *(shape((SWEEPS, 4, *span), f32) for span in spans),
         ],
         in_specs=[VMEM] * 2,
-        out_specs=[VMEM] * 4,
+        out_specs=[VMEM] * 3,
         scratch_shapes=[pltpu.VMEM((rows, *span), f32) for span in spans],
         compiler_params=PARAMS,
         name="inner_sweeps",
@@ -392,15 +416,17 @@
     volume = pl.pallas_call(
         functools.partial(edge_kernel, planes=planes),
         out_shape=shape((rows, cols, slices), f32),
-        in_specs=[VMEM] * 6,
-        out_specs=VMEM,
+        in_specs=[VMEM] * 5,
+        out_specs=HBM,
         scratch_shapes=[
             *(pltpu.VMEM((6, *span), f32) for span in spans),
             *(pltpu.VMEM((2, 6, *span), f32) for span in spans),
+            pltpu.VMEM((2 * SWEEPS, cols, slices), f32),
+            pltpu.SemaphoreType.DMA((3,)),
         ],
         compiler_params=PARAMS,
         name="edge_sweeps",
-    )(*inner, saved, saved_strip, from_near, from_far)
+    )(inner, saved, saved_strip, from_near, from_far)
     return (volume, residual)
 
 

time: 81.7 us -> 78.8 us (0.965)
  Pallas kernels: 22.2 us -> 20.4 us
  starting transfers between devices: 38 us -> 36.6 us
    pallas_call x1, Pallas kernels: 8.11 us -> 6.49 us  [per_device(): pl.pallas_call(functools.partial(forward_kernel, orders), out_shape=(kept...]
  transfers between devices with their start and end apart: 19 -> 19, of which waited for: 14 -> 14; matrix products, arithmetic and copies ran while one was open for 1% -> 1% of each run, Pallas kernels for 5% -> 6%
where the time goes in v4:
time: 78.8 us; the launch traced here: 77.5 us
  starting transfers between devices  36.6 us (46%)
  Pallas kernels  20.4 us (26%)
  waiting for transfers between devices  17.8 us (23%)
  between operations  1.52 us (2%)
  other arithmetic  0.99 us (1%)
    ppermute x8, starting transfers between devices, spread_chain(): lax.ppermute(piece, 'plane', [(i, i ^ 1 << bit) for i in range(planes)])  12.6 us
    ppermute x8, starting transfers between devices, sum_chain(): lax.ppermute(send, 'plane', [(i, i ^ 1 << bit) for i in range(planes)])  12.1 us
    ppermute x1, starting transfers between devices, per_device(): other = lax.ppermute(strip, 'cuts', [(0, 1), (1, 0)])  8.44 us
    ppermute x8, waiting for transfers between devices, spread_chain(): lax.ppermute(piece, 'plane', [(i, i ^ 1 << bit) for i in range(planes)])  8.16 us
    ppermute x8, waiting for transfers between devices, sum_chain(): lax.ppermute(send, 'plane', [(i, i ^ 1 << bit) for i in range(planes)])  7.01 us
    pallas_call x1, Pallas kernels, per_device(): pl.pallas_call(functools.partial(forward_kernel, orders), out_shape=(kept...  6.49 us
    pallas_call x1, Pallas kernels, per_device(): pl.pallas_call(functools.partial(backward_kernel, orders), out_shape=(sha...  4.86 us
    pallas_call x1, Pallas kernels, per_device(): pl.pallas_call(functools.partial(edge_kernel, planes=planes), out_shape=s...  4.57 us
  transfers between devices with their start and end apart: 19, of which 14 were waited for; matrix products, arithmetic and copies ran while one was open for 1% of the time, Pallas kernels for 6%

profile of v4, /device:TPU:1, one launch (start us, length us, event | category | flops | bytes accessed | tf_op | source)
XLA Modules:
  0.0 77.5 jit_solution(9493470802680369433)
XLA Ops:
  1.3 6.5 %forward.1 = (f32[8,128,128]{2,1,0:T(8,128)S(1)}, bf16[8,128,128]{2,1,0:T(8,128)(2,1)S(1)}, f32[8,128,128]{2,1,0:T(8,128)S(1)}, bf16[8,128,128]{2,1,0:T(8,128)(2...) custom-call(s32[96]{0:T(128)} %tile_ids.3, s32[96]{0:T(128)} %blocks.3, s32[16]{0:T(128)} %owner.3, ...), custom_call_target="tpu_custom_call" | custom-call | tf_op jit(solution)/shard_map/forward/pallas_call | solution.py:334
  7.8 2.1 %collective-permute-start.8 = (bf16[8,128,128]{2,1,0:T(8,128)(2,1)S(1)}, bf16[8,128,128]{2,1,0:T(8,128)(2,1)S(1)}, u32[]{:S(2)}, u32[]{:S(2)}) collective-permute-start(bf16[8,128,128]{2,1,0:T(8,128)(2,1)S(1)} %get-tuple-element.18), channel_id=1, source_target_pairs={{0,4},{2,6},{4,0},{6,2},{8,12},{10,14},{12,8},{14,10},{16,20},{18,... | collective-permute-start | bytes 786440 | tf_op jit(solution)/shard_map/ppermute | solution.py:283
  11.2 4.8 %collective-permute-done.8 = bf16[8,128,128]{2,1,0:T(8,128)(2,1)S(1)} collective-permute-done((bf16[8,128,128]{2,1,0:T(8,128)(2,1)S(1)}, bf16[8,128,128]{2,1,0:T(8,128)(2,1)S(1)}, u32[]{:S(2)}, u32[]{:S(2)}) %collective-permute-start.8) | collective-permute-done | bytes 262176 | tf_op jit(solution)/shard_map/ppermute | solution.py:283
  17.3 1.3 %collective-permute-start.1 = (bf16[4,128,128]{2,1,0:T(8,128)(2,1)S(1)}, bf16[4,128,128]{2,1,0:T(8,128)(2,1)S(1)}, u32[]{:S(2)}, u32[]{:S(2)}) collective-permute-start(bf16[4,128,128]{2,1,0:T(8,128)(2,1)S(1)} %slice.91), channel_id=1, source_target_pairs={{0,4},{2,6},{4,0},{6,2},{8,12},{10,14},{12,8},{14,10},{16,20},{18,... | collective-permute-start | bytes 393224 | tf_op jit(solution)/shard_map/ppermute | solution.py:283
  18.7 1.3 %collective-permute-done.9 = bf16[4,128,128]{2,1,0:T(8,128)(2,1)S(1)} collective-permute-done((bf16[4,128,128]{2,1,0:T(8,128)(2,1)S(1)}, bf16[4,128,128]{2,1,0:T(8,128)(2,1)S(1)}, u32[]{:S(2)}, u32[]{:S(2)}) %collective-permute-start.9) | collective-permute-done | bytes 131104 | tf_op jit(solution)/shard_map/ppermute | solution.py:283
  20.0 1.3 %collective-permute-start.10 = (bf16[2,128,128]{2,1,0:T(8,128)(2,1)S(1)}, bf16[2,128,128]{2,1,0:T(8,128)(2,1)S(1)}, u32[]{:S(2)}, u32[]{:S(2)}) collective-permute-start(bf16[2,128,128]{2,1,0:T(8,128)(2,1)S(1)} %slice.92), channel_id=1, source_target_pairs={{0,8},{2,10},{4,12},{6,14},{8,0},{10,2},{12,4},{14,6},{16,24},{18,... | collective-permute-start | bytes 196616 | tf_op jit(solution)/shard_map/ppermute | solution.py:283
  21.6 1.4 %collective-permute-start.2 = (bf16[2,128,128]{2,1,0:T(8,128)(2,1)S(1)}, bf16[2,128,128]{2,1,0:T(8,128)(2,1)S(1)}, u32[]{:S(2)}, u32[]{:S(2)}) collective-permute-start(bf16[2,128,128]{2,1,0:T(8,128)(2,1)S(1)} %slice.93), channel_id=1, source_target_pairs={{0,8},{2,10},{4,12},{6,14},{8,0},{10,2},{12,4},{14,6},{16,24},{18,... | collective-permute-start | bytes 196616 | tf_op jit(solution)/shard_map/ppermute | solution.py:283
  23.5 2.3 %collective-permute-start.11 = (bf16[1,128,128]{2,1,0:T(8,128)(2,1)S(1)}, bf16[1,128,128]{2,1,0:T(8,128)(2,1)S(1)}, u32[]{:S(2)}, u32[]{:S(2)}) collective-permute-start(bf16[1,128,128]{2,1,0:T(8,128)(2,1)S(1)} %slice.94), channel_id=1, source_target_pairs={{0,16},{2,18},{4,20},{6,22},{8,24},{10,26},{12,28},{14,30},{16,0},... | collective-permute-start | bytes 98312 | tf_op jit(solution)/shard_map/ppermute | solution.py:283
  25.9 1.3 %collective-permute-start.3 = (bf16[1,128,128]{2,1,0:T(8,128)(2,1)S(1)}, bf16[1,128,128]{2,1,0:T(8,128)(2,1)S(1)}, u32[]{:S(2)}, u32[]{:S(2)}) collective-permute-start(bf16[1,128,128]{2,1,0:T(8,128)(2,1)S(1)} %slice.95), channel_id=1, source_target_pairs={{0,16},{2,18},{4,20},{6,22},{8,24},{10,26},{12,28},{14,30},{16,0},... | collective-permute-start | bytes 98312 | tf_op jit(solution)/shard_map/ppermute | solution.py:283
  27.4 2.3 %collective-permute-start.12 = (bf16[1,128,128]{2,1,0:T(8,128)(2,1)S(1)}, bf16[1,128,128]{2,1,0:T(8,128)(2,1)S(1)}, u32[]{:S(2)}, u32[]{:S(2)}) collective-permute-start(bf16[1,128,128]{2,1,0:T(8,128)(2,1)S(1)} %residual.3), channel_id=1, source_target_pairs={{0,16},{2,18},{4,20},{6,22},{8,24},{10,26},{12,28},{14,30},{16,0},... | collective-permute-start | bytes 98312 | tf_op jit(solution)/shard_map/ppermute | solution.py:293
  31.7 1.3 %collective-permute-start.13 = (bf16[2,128,128]{2,1,0:T(8,128)(2,1)S(1)}, bf16[2,128,128]{2,1,0:T(8,128)(2,1)S(1)}, u32[]{:S(2)}, u32[]{:S(2)}) collective-permute-start(bf16[2,128,128]{2,1,0:T(8,128)(2,1)S(1)} %pad_maximum_fusion.7), channel_id=1, source_target_pairs={{0,8},{2,10},{4,12},{6,14},{8,0},{10,2},{12,4},{14,6},{16,24},{18,... | collective-permute-start | bytes 196616 | tf_op jit(solution)/shard_map/ppermute | solution.py:293
  33.6 2.1 %collective-permute-start.5 = (bf16[2,128,128]{2,1,0:T(8,128)(2,1)S(1)}, bf16[2,128,128]{2,1,0:T(8,128)(2,1)S(1)}, u32[]{:S(2)}, u32[]{:S(2)}) collective-permute-start(bf16[2,128,128]{2,1,0:T(8,128)(2,1)S(1)} %pad_maximum_fusion.6), channel_id=1, source_target_pairs={{0,8},{2,10},{4,12},{6,14},{8,0},{10,2},{12,4},{14,6},{16,24},{18,... | collective-permute-start | bytes 196616 | tf_op jit(solution)/shard_map/ppermute | solution.py:293
  35.7 1.4 %collective-permute-start.14 = (bf16[4,128,128]{2,1,0:T(8,128)(2,1)S(1)}, bf16[4,128,128]{2,1,0:T(8,128)(2,1)S(1)}, u32[]{:S(2)}, u32[]{:S(2)}) collective-permute-start(bf16[4,128,128]{2,1,0:T(8,128)(2,1)S(1)} %pad_maximum_fusion.5), channel_id=1, source_target_pairs={{0,2},{2,0},{4,6},{6,4},{8,10},{10,8},{12,14},{14,12},{16,18},{18,... | collective-permute-start | bytes 393224 | tf_op jit(solution)/shard_map/ppermute | solution.py:293
  37.4 1.3 %collective-permute-start.6 = (bf16[4,128,128]{2,1,0:T(8,128)(2,1)S(1)}, bf16[4,128,128]{2,1,0:T(8,128)(2,1)S(1)}, u32[]{:S(2)}, u32[]{:S(2)}) collective-permute-start(bf16[4,128,128]{2,1,0:T(8,128)(2,1)S(1)} %pad_maximum_fusion.4), channel_id=1, source_target_pairs={{0,4},{2,6},{4,0},{6,2},{8,12},{10,14},{12,8},{14,10},{16,20},{18,... | collective-permute-start | bytes 393224 | tf_op jit(solution)/shard_map/ppermute | solution.py:293
  39.7 1.3 %collective-permute-start.15 = (bf16[8,128,128]{2,1,0:T(8,128)(2,1)S(1)}, bf16[8,128,128]{2,1,0:T(8,128)(2,1)S(1)}, u32[]{:S(2)}, u32[]{:S(2)}) collective-permute-start(bf16[8,128,128]{2,1,0:T(8,128)(2,1)S(1)} %pad_maximum_fusion.1.b_low), channel_id=1, source_target_pairs={{0,4},{2,6},{4,0},{6,2},{8,12},{10,14},{12,8},{14,10},{16,20},{18,... | collective-permute-start | bytes 786440 | tf_op jit(solution)/shard_map/ppermute | solution.py:293
  41.3 1.6 %collective-permute-start.7 = (bf16[8,128,128]{2,1,0:T(8,128)(2,1)S(1)}, bf16[8,128,128]{2,1,0:T(8,128)(2,1)S(1)}, u32[]{:S(2)}, u32[]{:S(2)}) collective-permute-start(bf16[8,128,128]{2,1,0:T(8,128)(2,1)S(1)} %pad_maximum_fusion.a_low), channel_id=1, source_target_pairs={{0,2},{2,0},{4,6},{6,4},{8,10},{10,8},{12,14},{14,12},{16,18},{18,... | collective-permute-start | bytes 786440 | tf_op jit(solution)/shard_map/ppermute | solution.py:293
  42.9 2.0 %collective-permute-done.15.b_high = bf16[8,128,128]{2,1,0:T(8,128)(2,1)S(1)} collective-permute-done((bf16[8,128,128]{2,1,0:T(8,128)(2,1)S(1)}, bf16[8,128,128]{2,1,0:T(8,128)(2,1)S(1)}, u32[]{:S(2)}, u32[]{:S(2)}) %collective-permute-start.15) | collective-permute-done | bytes 262176 | tf_op jit(solution)/shard_map/ppermute | solution.py:293
  44.9 3.4 %collective-permute-done.7.a_high = bf16[8,128,128]{2,1,0:T(8,128)(2,1)S(1)} collective-permute-done((bf16[8,128,128]{2,1,0:T(8,128)(2,1)S(1)}, bf16[8,128,128]{2,1,0:T(8,128)(2,1)S(1)}, u32[]{:S(2)}, u32[]{:S(2)}) %collective-permute-start.7) | collective-permute-done | bytes 262176 | tf_op jit(solution)/shard_map/ppermute | solution.py:293
  48.4 4.9 %backward.1 = (f32[16,128,128]{2,1,0:T(8,128)S(1)}, bf16[512,128]{1,0:T(8,128)(2,1)S(1)}, bf16[512,128]{1,0:T(8,128)(2,1)S(1)}, f32[16,8,128]{2,1,0:T(8,128)S(1)}) custom-call(s32[96]{0:T(128)} %tile_ids.3, s32[96]{0:T(128)} %blocks.3, s32[16]{0:T(128)} %owner.3, s32[1]{0:T(128)S(6)} %copy.9.count, bf16[8,128,128]{2,1,0:T(8,128)(2,1)S(1)} %pad_maximum_fusion.a_low, ...), custom_call_target="tpu_custom_call" | custom-call | tf_op jit(solution)/shard_map/backward/pallas_call | solution.py:367
  53.2 8.4 %collective-permute-start.16 = (f32[16,8,128]{2,1,0:T(8,128)S(1)}, f32[16,8,128]{2,1,0:T(8,128)S(1)}, u32[]{:S(2)}, u32[]{:S(2)}) collective-permute-start(f32[16,8,128]{2,1,0:T(8,128)S(1)} %get-tuple-element.22), channel_id=1, source_target_pairs={{0,1},{1,0},{2,3},{3,2},{4,5},{5,4},{6,7},{7,6},{8,9},{9,8},{10,11... | collective-permute-start | bytes 196616 | tf_op jit(solution)/shard_map/ppermute | solution.py:386
  63.3 2.9 %collective-permute-start.17 = (bf16[576,128]{1,0:T(8,128)(2,1)S(1)}, bf16[576,128]{1,0:T(8,128)(2,1)S(1)}, u32[]{:S(2)}, u32[]{:S(2)}) collective-permute-start(bf16[576,128]{1,0:T(8,128)(2,1)S(1)} %pad_maximum_fusion.2), channel_id=1, source_target_pairs={{0,2},{2,0},{4,6},{6,4},{8,10},{10,8},{12,14},{14,12},{16,18},{18,... | collective-permute-start | bytes 442376 | tf_op jit(solution)/shard_map/ppermute | solution.py:396
  66.9 4.2 %inner_sweeps.1 = (f32[8,128,128]{2,1,0:T(8,128)S(1)}, f32[4,4,128,128]{3,2,1,0:T(8,128)S(1)}, f32[4,4,16,128]{3,2,1,0:T(8,128)S(1)}) custom-call(f32[16,128,128]{2,1,0:T(8,128)S(1)} %get-tuple-element.21.relaxed, f32[16,16,128]{2,1,0:T(8,128)S(1)} %maximum_select_fusion.strip), custom_call_target="tpu_custom_call" | custom-call | tf_op jit(solution)/shard_map/inner_sweeps/pallas_call | solution.py:404
  71.1 1.8 %collective-permute-done.17.from_near = bf16[576,128]{1,0:T(8,128)(2,1)S(1)} collective-permute-done((bf16[576,128]{1,0:T(8,128)(2,1)S(1)}, bf16[576,128]{1,0:T(8,128)(2,1)S(1)}, u32[]{:S(2)}, u32[]{:S(2)}) %collective-permute-start.17) | collective-permute-done | bytes 147488 | tf_op jit(solution)/shard_map/ppermute | solution.py:396
  72.9 4.6 %edge_sweeps.1 = f32[16,128,128]{2,1,0:T(8,128)} custom-call(f32[8,128,128]{2,1,0:T(8,128)S(1)} %get-tuple-element.23.inner, f32[4,4,128,128]{3,2,1,0:T(8,128)S(1)} %get-tuple-element.24.saved, f32[4,4,16,128]{3,2,1,0:T(8,128)S(1)} %get-tuple-element.25.saved_strip, bf16[576,128]{1,0:T(8,128)(2,1)S(1)} %collective-permute-done.17.from_near, ...), custom_call_target="tpu_custom_call" | custom-call | tf_op jit(solution)/shard_map/edge_sweeps/pallas_call | solution.py:416
  (47 shorter events, 10.0 us)
Async XLA Ops:
  0.6 26.6 %copy-start = (f32[1,256,128]{2,1,0:T(8,128)S(1)}, f32[1,256,128]{2,1,0:T(8,128)}, u32[]{:S(2)}) copy-start(f32[1,256,128]{2,1,0:T(8,128)} %measured.3) | copy-start | bytes 393220
  7.8 8.2 %collective-permute-start.8 = (bf16[8,128,128]{2,1,0:T(8,128)(2,1)S(1)}, bf16[8,128,128]{2,1,0:T(8,128)(2,1)S(1)}, u32[]{:S(2)}, u32[]{:S(2)}) collective-permute-start(bf16[8,128,128]{2,1,0:T(8,128)(2,1)S(1)} %get-tuple-element.18), channel_id=1, source_target_pairs={{0,4},{2,6},{4,0},{6,2},{8,12},{10,14},{12,8},{14,10},{16,20},{18,... | collective-permute-start | bytes 786440 | tf_op jit(solution)/shard_map/ppermute | solution.py:283
  9.9 7.3 %collective-permute-start = (bf16[8,128,128]{2,1,0:T(8,128)(2,1)S(1)}, bf16[8,128,128]{2,1,0:T(8,128)(2,1)S(1)}, u32[]{:S(2)}, u32[]{:S(2)}) collective-permute-start(bf16[8,128,128]{2,1,0:T(8,128)(2,1)S(1)} %get-tuple-element.16), channel_id=1, source_target_pairs={{0,2},{2,0},{4,6},{6,4},{8,10},{10,8},{12,14},{14,12},{16,18},{18,... | collective-permute-start | bytes 786440 | tf_op jit(solution)/shard_map/ppermute | solution.py:283
  16.1 3.9 %collective-permute-start.9 = (bf16[4,128,128]{2,1,0:T(8,128)(2,1)S(1)}, bf16[4,128,128]{2,1,0:T(8,128)(2,1)S(1)}, u32[]{:S(2)}, u32[]{:S(2)}) collective-permute-start(bf16[4,128,128]{2,1,0:T(8,128)(2,1)S(1)} %slice.90), channel_id=1, source_target_pairs={{0,2},{2,0},{4,6},{6,4},{8,10},{10,8},{12,14},{14,12},{16,18},{18,... | collective-permute-start | bytes 393224 | tf_op jit(solution)/shard_map/ppermute | solution.py:283
  17.3 4.2 %collective-permute-start.1 = (bf16[4,128,128]{2,1,0:T(8,128)(2,1)S(1)}, bf16[4,128,128]{2,1,0:T(8,128)(2,1)S(1)}, u32[]{:S(2)}, u32[]{:S(2)}) collective-permute-start(bf16[4,128,128]{2,1,0:T(8,128)(2,1)S(1)} %slice.91), channel_id=1, source_target_pairs={{0,4},{2,6},{4,0},{6,2},{8,12},{10,14},{12,8},{14,10},{16,20},{18,... | collective-permute-start | bytes 393224 | tf_op jit(solution)/shard_map/ppermute | solution.py:283
  20.0 3.5 %collective-permute-start.10 = (bf16[2,128,128]{2,1,0:T(8,128)(2,1)S(1)}, bf16[2,128,128]{2,1,0:T(8,128)(2,1)S(1)}, u32[]{:S(2)}, u32[]{:S(2)}) collective-permute-start(bf16[2,128,128]{2,1,0:T(8,128)(2,1)S(1)} %slice.92), channel_id=1, source_target_pairs={{0,8},{2,10},{4,12},{6,14},{8,0},{10,2},{12,4},{14,6},{16,24},{18,... | collective-permute-start | bytes 196616 | tf_op jit(solution)/shard_map/ppermute | solution.py:283
  21.6 4.2 %collective-permute-start.2 = (bf16[2,128,128]{2,1,0:T(8,128)(2,1)S(1)}, bf16[2,128,128]{2,1,0:T(8,128)(2,1)S(1)}, u32[]{:S(2)}, u32[]{:S(2)}) collective-permute-start(bf16[2,128,128]{2,1,0:T(8,128)(2,1)S(1)} %slice.93), channel_id=1, source_target_pairs={{0,8},{2,10},{4,12},{6,14},{8,0},{10,2},{12,4},{14,6},{16,24},{18,... | collective-permute-start | bytes 196616 | tf_op jit(solution)/shard_map/ppermute | solution.py:283
  23.5 3.7 %collective-permute-start.11 = (bf16[1,128,128]{2,1,0:T(8,128)(2,1)S(1)}, bf16[1,128,128]{2,1,0:T(8,128)(2,1)S(1)}, u32[]{:S(2)}, u32[]{:S(2)}) collective-permute-start(bf16[1,128,128]{2,1,0:T(8,128)(2,1)S(1)} %slice.94), channel_id=1, source_target_pairs={{0,16},{2,18},{4,20},{6,22},{8,24},{10,26},{12,28},{14,30},{16,0},... | collective-permute-start | bytes 98312 | tf_op jit(solution)/shard_map/ppermute | solution.py:283
  25.9 3.9 %collective-permute-start.3 = (bf16[1,128,128]{2,1,0:T(8,128)(2,1)S(1)}, bf16[1,128,128]{2,1,0:T(8,128)(2,1)S(1)}, u32[]{:S(2)}, u32[]{:S(2)}) collective-permute-start(bf16[1,128,128]{2,1,0:T(8,128)(2,1)S(1)} %slice.95), channel_id=1, source_target_pairs={{0,16},{2,18},{4,20},{6,22},{8,24},{10,26},{12,28},{14,30},{16,0},... | collective-permute-start | bytes 98312 | tf_op jit(solution)/shard_map/ppermute | solution.py:283
  27.4 4.3 %collective-permute-start.12 = (bf16[1,128,128]{2,1,0:T(8,128)(2,1)S(1)}, bf16[1,128,128]{2,1,0:T(8,128)(2,1)S(1)}, u32[]{:S(2)}, u32[]{:S(2)}) collective-permute-start(bf16[1,128,128]{2,1,0:T(8,128)(2,1)S(1)} %residual.3), channel_id=1, source_target_pairs={{0,16},{2,18},{4,20},{6,22},{8,24},{10,26},{12,28},{14,30},{16,0},... | collective-permute-start | bytes 98312 | tf_op jit(solution)/shard_map/ppermute | solution.py:293
  29.9 3.7 %collective-permute-start.4 = (bf16[1,128,128]{2,1,0:T(8,128)(2,1)S(1)}, bf16[1,128,128]{2,1,0:T(8,128)(2,1)S(1)}, u32[]{:S(2)}, u32[]{:S(2)}) collective-permute-start(bf16[1,128,128]{2,1,0:T(8,128)(2,1)S(1)} %residual.2), channel_id=1, source_target_pairs={{0,16},{2,18},{4,20},{6,22},{8,24},{10,26},{12,28},{14,30},{16,0},... | collective-permute-start | bytes 98312 | tf_op jit(solution)/shard_map/ppermute | solution.py:293
  31.7 4.0 %collective-permute-start.13 = (bf16[2,128,128]{2,1,0:T(8,128)(2,1)S(1)}, bf16[2,128,128]{2,1,0:T(8,128)(2,1)S(1)}, u32[]{:S(2)}, u32[]{:S(2)}) collective-permute-start(bf16[2,128,128]{2,1,0:T(8,128)(2,1)S(1)} %pad_maximum_fusion.7), channel_id=1, source_target_pairs={{0,8},{2,10},{4,12},{6,14},{8,0},{10,2},{12,4},{14,6},{16,24},{18,... | collective-permute-start | bytes 196616 | tf_op jit(solution)/shard_map/ppermute | solution.py:293
  33.6 3.7 %collective-permute-start.5 = (bf16[2,128,128]{2,1,0:T(8,128)(2,1)S(1)}, bf16[2,128,128]{2,1,0:T(8,128)(2,1)S(1)}, u32[]{:S(2)}, u32[]{:S(2)}) collective-permute-start(bf16[2,128,128]{2,1,0:T(8,128)(2,1)S(1)} %pad_maximum_fusion.6), channel_id=1, source_target_pairs={{0,8},{2,10},{4,12},{6,14},{8,0},{10,2},{12,4},{14,6},{16,24},{18,... | collective-permute-start | bytes 196616 | tf_op jit(solution)/shard_map/ppermute | solution.py:293
  35.7 3.9 %collective-permute-start.14 = (bf16[4,128,128]{2,1,0:T(8,128)(2,1)S(1)}, bf16[4,128,128]{2,1,0:T(8,128)(2,1)S(1)}, u32[]{:S(2)}, u32[]{:S(2)}) collective-permute-start(bf16[4,128,128]{2,1,0:T(8,128)(2,1)S(1)} %pad_maximum_fusion.5), channel_id=1, source_target_pairs={{0,2},{2,0},{4,6},{6,4},{8,10},{10,8},{12,14},{14,12},{16,18},{18,... | collective-permute-start | bytes 393224 | tf_op jit(solution)/shard_map/ppermute | solution.py:293
  37.4 3.9 %collective-permute-start.6 = (bf16[4,128,128]{2,1,0:T(8,128)(2,1)S(1)}, bf16[4,128,128]{2,1,0:T(8,128)(2,1)S(1)}, u32[]{:S(2)}, u32[]{:S(2)}) collective-permute-start(bf16[4,128,128]{2,1,0:T(8,128)(2,1)S(1)} %pad_maximum_fusion.4), channel_id=1, source_target_pairs={{0,4},{2,6},{4,0},{6,2},{8,12},{10,14},{12,8},{14,10},{16,20},{18,... | collective-permute-start | bytes 393224 | tf_op jit(solution)/shard_map/ppermute | solution.py:293
  39.7 5.3 %collective-permute-start.15 = (bf16[8,128,128]{2,1,0:T(8,128)(2,1)S(1)}, bf16[8,128,128]{2,1,0:T(8,128)(2,1)S(1)}, u32[]{:S(2)}, u32[]{:S(2)}) collective-permute-start(bf16[8,128,128]{2,1,0:T(8,128)(2,1)S(1)} %pad_maximum_fusion.1.b_low), channel_id=1, source_target_pairs={{0,4},{2,6},{4,0},{6,2},{8,12},{10,14},{12,8},{14,10},{16,20},{18,... | collective-permute-start | bytes 786440 | tf_op jit(solution)/shard_map/ppermute | solution.py:293
  41.3 7.1 %collective-permute-start.7 = (bf16[8,128,128]{2,1,0:T(8,128)(2,1)S(1)}, bf16[8,128,128]{2,1,0:T(8,128)(2,1)S(1)}, u32[]{:S(2)}, u32[]{:S(2)}) collective-permute-start(bf16[8,128,128]{2,1,0:T(8,128)(2,1)S(1)} %pad_maximum_fusion.a_low), channel_id=1, source_target_pairs={{0,2},{2,0},{4,6},{6,4},{8,10},{10,8},{12,14},{14,12},{16,18},{18,... | collective-permute-start | bytes 786440 | tf_op jit(solution)/shard_map/ppermute | solution.py:293
  53.2 9.3 %collective-permute-start.16 = (f32[16,8,128]{2,1,0:T(8,128)S(1)}, f32[16,8,128]{2,1,0:T(8,128)S(1)}, u32[]{:S(2)}, u32[]{:S(2)}) collective-permute-start(f32[16,8,128]{2,1,0:T(8,128)S(1)} %get-tuple-element.22), channel_id=1, source_target_pairs={{0,1},{1,0},{2,3},{3,2},{4,5},{5,4},{6,7},{7,6},{8,9},{9,8},{10,11... | collective-permute-start | bytes 196616 | tf_op jit(solution)/shard_map/ppermute | solution.py:386
  62.6 8.5 %collective-permute-start.18 = (bf16[576,128]{1,0:T(8,128)(2,1)S(1)}, bf16[576,128]{1,0:T(8,128)(2,1)S(1)}, u32[]{:S(2)}, u32[]{:S(2)}) collective-permute-start(bf16[576,128]{1,0:T(8,128)(2,1)S(1)} %pad_maximum_fusion.3), channel_id=1, source_target_pairs={{2,4},{4,2},{6,8},{8,6},{10,12},{12,10},{14,16},{16,14},{18,20},{2... | collective-permute-start | bytes 442376 | tf_op jit(solution)/shard_map/ppermute | solution.py:396
  63.3 9.6 %collective-permute-start.17 = (bf16[576,128]{1,0:T(8,128)(2,1)S(1)}, bf16[576,128]{1,0:T(8,128)(2,1)S(1)}, u32[]{:S(2)}, u32[]{:S(2)}) collective-permute-start(bf16[576,128]{1,0:T(8,128)(2,1)S(1)} %pad_maximum_fusion.2), channel_id=1, source_target_pairs={{0,2},{2,0},{4,6},{6,4},{8,10},{10,8},{12,14},{14,12},{16,18},{18,... | collective-permute-start | bytes 442376 | tf_op jit(solution)/shard_map/ppermute | solution.py:396

commit v5 on v4

--- a/solution.py
+++ b/solution.py
@@ -90,11 +90,12 @@
             send[p] = total[relative_block(order, p + parts // 2), :, low : low + half].astype(jnp.bfloat16)
 
 
-def residual_kernel(low, keep, got, measured, residual):
+def residual_kernel(low, total, got, measured, measured_other, residual):
     half = residual.shape[1]
-    projection = (keep[0] + got[0].astype(jnp.float32)).T
-    mismatch = measured[0, low : low + half, :] - projection
-    residual[0] = (mismatch / jnp.sqrt(1.0 + mismatch * mismatch)).astype(jnp.bfloat16)
+    for p, target in enumerate((measured[0, low : low + half, :], measured_other[0])):
+        projection = (total[p] + got[1 - p].astype(jnp.float32)).T
+        mismatch = target - projection
+        residual[p] = (mismatch / jnp.sqrt(1.0 + mismatch * mismatch)).astype(jnp.bfloat16)
 
 
 def backward_kernel(
@@ -278,22 +279,24 @@
         copy.wait()
 
 
+def partner(bit, planes):
+    return [(i, i ^ (1 << bit)) for i in range(planes)]
+
+
 def sum_chain(keep, send, order, planes):
-    for stage, bit in enumerate(order):
-        got = lax.ppermute(send, "plane", [(i, i ^ (1 << bit)) for i in range(planes)])
-        if stage == len(order) - 1:
-            return keep, got
+    for bit in order[:-1]:
+        got = lax.ppermute(send, "plane", partner(bit, planes))
         total = keep + got.astype(jnp.float32)
         left = total.shape[0] // 2
         keep, send = total[:left], total[left:].astype(jnp.bfloat16)
+    return total, lax.ppermute(total.astype(jnp.bfloat16), "plane", partner(order[-1], planes))
 
 
 def spread_chain(piece, order, planes):
-    for stage, bit in reversed(list(enumerate(order))):
-        got = lax.ppermute(piece, "plane", [(i, i ^ (1 << bit)) for i in range(planes)])
-        if stage == 0:
-            return piece, got
+    for bit in reversed(order[1:-1]):
+        got = lax.ppermute(piece, "plane", partner(bit, planes))
         piece = jnp.concatenate([piece, got], axis=0)
+    return piece, lax.ppermute(piece, "plane", partner(order[0], planes))
 
 
 def per_device(
@@ -347,20 +350,22 @@
         name="forward",
     )(*lists, far_image, weights)
 
+    b_keep, target = lax.optimization_barrier((b_keep, measured))
     pieces = []
     for low, keep, send, order in ((0, a_keep, a_send, plain), (half, b_keep, b_send, swapped)):
-        keep, got = sum_chain(keep, send, order, planes)
+        target_other = lax.ppermute(target[:, low : low + half], "plane", partner(order[-1], planes))
+        total, got = sum_chain(keep, send, order, planes)
         pieces.append(
             pl.pallas_call(
                 functools.partial(residual_kernel, low),
-                out_shape=shape((1, half, slices), bf16),
-                in_specs=[VMEM] * 3,
+                out_shape=shape((2, half, slices), bf16),
+                in_specs=[VMEM] * 4,
                 out_specs=VMEM,
                 compiler_params=PARAMS,
                 name="residual",
-            )(keep, got, measured)
+            )(total, got, measured, target_other)
         )
-    residual = jnp.concatenate(pieces, axis=1)
+    residual = jnp.concatenate([piece[:1] for piece in pieces], axis=1)
     a_low, a_high = spread_chain(pieces[0], plain, planes)
     b_low, b_high = spread_chain(pieces[1], swapped, planes)
 

time: 78.8 us -> 74.4 us (0.944)
  starting transfers between devices: 36.6 us -> 34.4 us
  waiting for transfers between devices: 17.8 us -> 15.6 us
    ppermute x16, waiting for transfers between devices: 15.2 us -> 13 us  [the longest x2 5.88 us: spread_chain(): return (piece, lax.ppermute(piece, 'plane', partner(order[0], planes)))]
    ppermute x16, starting transfers between devices: 24.6 us -> 22.8 us  [the longest x6 8.35 us: sum_chain(): got = lax.ppermute(send, 'plane', partner(bit, planes))]
    ppermute x1, starting transfers between devices: 8.44 us -> 7.44 us  [per_device(): other = lax.ppermute(strip, 'cuts', [(0, 1), (1, 0)])]
  transfers between devices with their start and end apart: 19 -> 19, of which waited for: 14 -> 12; matrix products, arithmetic and copies ran while one was open for 1% -> 1% of each run, Pallas kernels for 6% -> 6%
where the time goes in v5:
time: 74.4 us; the launch traced here: 73 us
  starting transfers between devices  34.4 us (46%)
  Pallas kernels  20.4 us (27%)
  waiting for transfers between devices  15.6 us (21%)
  between operations  1.49 us (2%)
  other arithmetic  1 us (1%)
    ppermute x6, starting transfers between devices, sum_chain(): got = lax.ppermute(send, 'plane', partner(bit, planes))  8.35 us
    ppermute x1, starting transfers between devices, per_device(): other = lax.ppermute(strip, 'cuts', [(0, 1), (1, 0)])  7.44 us
    pallas_call x1, Pallas kernels, per_device(): pl.pallas_call(functools.partial(forward_kernel, orders), out_shape=(kept...  6.49 us
    ppermute x2, waiting for transfers between devices, spread_chain(): return (piece, lax.ppermute(piece, 'plane', partner(order[0], planes)))  5.88 us
    ppermute x4, starting transfers between devices, spread_chain(): got = lax.ppermute(piece, 'plane', partner(bit, planes))  5.71 us
    pallas_call x1, Pallas kernels, per_device(): pl.pallas_call(functools.partial(backward_kernel, orders), out_shape=(sha...  4.86 us
    ppermute x6, waiting for transfers between devices, sum_chain(): got = lax.ppermute(send, 'plane', partner(bit, planes))  4.67 us
    pallas_call x1, Pallas kernels, per_device(): pl.pallas_call(functools.partial(edge_kernel, planes=planes), out_shape=s...  4.57 us
  transfers between devices with their start and end apart: 19, of which 12 were waited for; matrix products, arithmetic and copies ran while one was open for 1% of the time, Pallas kernels for 6%

profile of v5, /device:TPU:1, one launch (start us, length us, event | category | flops | bytes accessed | tf_op | source)
XLA Modules:
  0.0 73.0 jit_solution(9208622736040592724)
XLA Ops:
  1.3 6.5 %forward.1 = (f32[8,128,128]{2,1,0:T(8,128)S(1)}, bf16[8,128,128]{2,1,0:T(8,128)(2,1)S(1)}, f32[8,128,128]{2,1,0:T(8,128)S(1)}, bf16[8,128,128]{2,1,0:T(8,128)(2...) custom-call(s32[96]{0:T(128)} %tile_ids.3, s32[96]{0:T(128)} %blocks.3, s32[16]{0:T(128)} %owner.3, ...), custom_call_target="tpu_custom_call" | custom-call | tf_op jit(solution)/shard_map/forward/pallas_call | solution.py:337
  7.8 2.1 %collective-permute-start.8 = (bf16[8,128,128]{2,1,0:T(8,128)(2,1)S(1)}, bf16[8,128,128]{2,1,0:T(8,128)(2,1)S(1)}, u32[]{:S(2)}, u32[]{:S(2)}) collective-permute-start(bf16[8,128,128]{2,1,0:T(8,128)(2,1)S(1)} %get-tuple-element.22), channel_id=1, source_target_pairs={{0,4},{2,6},{4,0},{6,2},{8,12},{10,14},{12,8},{14,10},{16,20},{18,... | collective-permute-start | bytes 786440 | tf_op jit(solution)/shard_map/ppermute | solution.py:288
  9.9 1.2 %collective-permute-start = (bf16[8,128,128]{2,1,0:T(8,128)(2,1)S(1)}, bf16[8,128,128]{2,1,0:T(8,128)(2,1)S(1)}, u32[]{:S(2)}, u32[]{:S(2)}) collective-permute-start(bf16[8,128,128]{2,1,0:T(8,128)(2,1)S(1)} %get-tuple-element.18), channel_id=1, source_target_pairs={{0,2},{2,0},{4,6},{6,4},{8,10},{10,8},{12,14},{14,12},{16,18},{18,... | collective-permute-start | bytes 786440 | tf_op jit(solution)/shard_map/ppermute | solution.py:288
  11.2 2.4 %collective-permute-start.12 = (f32[1,128,128]{2,1,0:T(8,128)S(1)}, f32[1,128,128]{2,1,0:T(8,128)S(1)}, u32[]{:S(2)}, u32[]{:S(2)}) collective-permute-start(f32[1,128,128]{2,1,0:T(8,128)S(1)} %get-tuple-element.38), channel_id=1, source_target_pairs={{0,16},{2,18},{4,20},{6,22},{8,24},{10,26},{12,28},{14,30},{16,0},... | collective-permute-start | bytes 196616 | tf_op jit(solution)/shard_map/ppermute | solution.py:356
  13.6 2.4 %collective-permute-done.8 = bf16[8,128,128]{2,1,0:T(8,128)(2,1)S(1)} collective-permute-done((bf16[8,128,128]{2,1,0:T(8,128)(2,1)S(1)}, bf16[8,128,128]{2,1,0:T(8,128)(2,1)S(1)}, u32[]{:S(2)}, u32[]{:S(2)}) %collective-permute-start.8) | collective-permute-done | bytes 262176 | tf_op jit(solution)/shard_map/ppermute | solution.py:288
  16.1 1.2 %collective-permute-start.9 = (bf16[4,128,128]{2,1,0:T(8,128)(2,1)S(1)}, bf16[4,128,128]{2,1,0:T(8,128)(2,1)S(1)}, u32[]{:S(2)}, u32[]{:S(2)}) collective-permute-start(bf16[4,128,128]{2,1,0:T(8,128)(2,1)S(1)} %slice.84), channel_id=1, source_target_pairs={{0,2},{2,0},{4,6},{6,4},{8,10},{10,8},{12,14},{14,12},{16,18},{18,... | collective-permute-start | bytes 393224 | tf_op jit(solution)/shard_map/ppermute | solution.py:288
  17.3 1.3 %collective-permute-start.1 = (bf16[4,128,128]{2,1,0:T(8,128)(2,1)S(1)}, bf16[4,128,128]{2,1,0:T(8,128)(2,1)S(1)}, u32[]{:S(2)}, u32[]{:S(2)}) collective-permute-start(bf16[4,128,128]{2,1,0:T(8,128)(2,1)S(1)} %slice.85), channel_id=1, source_target_pairs={{0,4},{2,6},{4,0},{6,2},{8,12},{10,14},{12,8},{14,10},{16,20},{18,... | collective-permute-start | bytes 393224 | tf_op jit(solution)/shard_map/ppermute | solution.py:288
  18.7 1.4 %collective-permute-done.9 = bf16[4,128,128]{2,1,0:T(8,128)(2,1)S(1)} collective-permute-done((bf16[4,128,128]{2,1,0:T(8,128)(2,1)S(1)}, bf16[4,128,128]{2,1,0:T(8,128)(2,1)S(1)}, u32[]{:S(2)}, u32[]{:S(2)}) %collective-permute-start.9) | collective-permute-done | bytes 131104 | tf_op jit(solution)/shard_map/ppermute | solution.py:288
  20.1 1.2 %collective-permute-start.10 = (bf16[2,128,128]{2,1,0:T(8,128)(2,1)S(1)}, bf16[2,128,128]{2,1,0:T(8,128)(2,1)S(1)}, u32[]{:S(2)}, u32[]{:S(2)}) collective-permute-start(bf16[2,128,128]{2,1,0:T(8,128)(2,1)S(1)} %slice.86), channel_id=1, source_target_pairs={{0,8},{2,10},{4,12},{6,14},{8,0},{10,2},{12,4},{14,6},{16,24},{18,... | collective-permute-start | bytes 196616 | tf_op jit(solution)/shard_map/ppermute | solution.py:288
  21.6 1.4 %collective-permute-start.2 = (bf16[2,128,128]{2,1,0:T(8,128)(2,1)S(1)}, bf16[2,128,128]{2,1,0:T(8,128)(2,1)S(1)}, u32[]{:S(2)}, u32[]{:S(2)}) collective-permute-start(bf16[2,128,128]{2,1,0:T(8,128)(2,1)S(1)} %slice.87), channel_id=1, source_target_pairs={{0,8},{2,10},{4,12},{6,14},{8,0},{10,2},{12,4},{14,6},{16,24},{18,... | collective-permute-start | bytes 196616 | tf_op jit(solution)/shard_map/ppermute | solution.py:288
  23.6 2.3 %collective-permute-start.11 = (bf16[2,128,128]{2,1,0:T(8,128)(2,1)S(1)}, bf16[2,128,128]{2,1,0:T(8,128)(2,1)S(1)}, u32[]{:S(2)}, u32[]{:S(2)}) collective-permute-start(bf16[2,128,128]{2,1,0:T(8,128)(2,1)S(1)} %get-tuple-element.32), channel_id=1, source_target_pairs={{0,16},{2,18},{4,20},{6,22},{8,24},{10,26},{12,28},{14,30},{16,0},... | collective-permute-start | bytes 196616 | tf_op jit(solution)/shard_map/ppermute | solution.py:292
  26.0 1.3 %collective-permute-start.3 = (bf16[2,128,128]{2,1,0:T(8,128)(2,1)S(1)}, bf16[2,128,128]{2,1,0:T(8,128)(2,1)S(1)}, u32[]{:S(2)}, u32[]{:S(2)}) collective-permute-start(bf16[2,128,128]{2,1,0:T(8,128)(2,1)S(1)} %get-tuple-element.34), channel_id=1, source_target_pairs={{0,16},{2,18},{4,20},{6,22},{8,24},{10,26},{12,28},{14,30},{16,0},... | collective-permute-start | bytes 196616 | tf_op jit(solution)/shard_map/ppermute | solution.py:292
  27.9 1.6 %collective-permute-start.13 = (bf16[2,128,128]{2,1,0:T(8,128)(2,1)S(1)}, bf16[2,128,128]{2,1,0:T(8,128)(2,1)S(1)}, u32[]{:S(2)}, u32[]{:S(2)}) collective-permute-start(bf16[2,128,128]{2,1,0:T(8,128)(2,1)S(1)} %residual.3), channel_id=1, source_target_pairs={{0,8},{2,10},{4,12},{6,14},{8,0},{10,2},{12,4},{14,6},{16,24},{18,... | collective-permute-start | bytes 196616 | tf_op jit(solution)/shard_map/ppermute | solution.py:297
  30.2 1.6 %collective-permute-start.5 = (bf16[2,128,128]{2,1,0:T(8,128)(2,1)S(1)}, bf16[2,128,128]{2,1,0:T(8,128)(2,1)S(1)}, u32[]{:S(2)}, u32[]{:S(2)}) collective-permute-start(bf16[2,128,128]{2,1,0:T(8,128)(2,1)S(1)} %residual.2), channel_id=1, source_target_pairs={{0,8},{2,10},{4,12},{6,14},{8,0},{10,2},{12,4},{14,6},{16,24},{18,... | collective-permute-start | bytes 196616 | tf_op jit(solution)/shard_map/ppermute | solution.py:297
  31.8 1.5 %collective-permute-start.14 = (bf16[4,128,128]{2,1,0:T(8,128)(2,1)S(1)}, bf16[4,128,128]{2,1,0:T(8,128)(2,1)S(1)}, u32[]{:S(2)}, u32[]{:S(2)}) collective-permute-start(bf16[4,128,128]{2,1,0:T(8,128)(2,1)S(1)} %pad_maximum_fusion.5), channel_id=1, source_target_pairs={{0,2},{2,0},{4,6},{6,4},{8,10},{10,8},{12,14},{14,12},{16,18},{18,... | collective-permute-start | bytes 393224 | tf_op jit(solution)/shard_map/ppermute | solution.py:297
  35.7 1.8 %collective-permute-start.15 = (bf16[8,128,128]{2,1,0:T(8,128)(2,1)S(1)}, bf16[8,128,128]{2,1,0:T(8,128)(2,1)S(1)}, u32[]{:S(2)}, u32[]{:S(2)}) collective-permute-start(bf16[8,128,128]{2,1,0:T(8,128)(2,1)S(1)} %pad_maximum_fusion.1.b_low), channel_id=1, source_target_pairs={{0,4},{2,6},{4,0},{6,2},{8,12},{10,14},{12,8},{14,10},{16,20},{18,... | collective-permute-start | bytes 786440 | tf_op jit(solution)/shard_map/ppermute | solution.py:299
  38.4 3.1 %collective-permute-done.15.b_high = bf16[8,128,128]{2,1,0:T(8,128)(2,1)S(1)} collective-permute-done((bf16[8,128,128]{2,1,0:T(8,128)(2,1)S(1)}, bf16[8,128,128]{2,1,0:T(8,128)(2,1)S(1)}, u32[]{:S(2)}, u32[]{:S(2)}) %collective-permute-start.15) | collective-permute-done | bytes 262176 | tf_op jit(solution)/shard_map/ppermute | solution.py:299
  41.5 2.8 %collective-permute-done.7.a_high = bf16[8,128,128]{2,1,0:T(8,128)(2,1)S(1)} collective-permute-done((bf16[8,128,128]{2,1,0:T(8,128)(2,1)S(1)}, bf16[8,128,128]{2,1,0:T(8,128)(2,1)S(1)}, u32[]{:S(2)}, u32[]{:S(2)}) %collective-permute-start.7) | collective-permute-done | bytes 262176 | tf_op jit(solution)/shard_map/ppermute | solution.py:299
  44.3 4.9 %backward.1 = (f32[16,128,128]{2,1,0:T(8,128)S(1)}, bf16[512,128]{1,0:T(8,128)(2,1)S(1)}, bf16[512,128]{1,0:T(8,128)(2,1)S(1)}, f32[16,8,128]{2,1,0:T(8,128)S(1)}) custom-call(s32[96]{0:T(128)} %tile_ids.3, s32[96]{0:T(128)} %blocks.3, s32[16]{0:T(128)} %owner.3, s32[1]{0:T(128)S(6)} %copy.9.count, bf16[8,128,128]{2,1,0:T(8,128)(2,1)S(1)} %pad_maximum_fusion.a_low, ...), custom_call_target="tpu_custom_call" | custom-call | tf_op jit(solution)/shard_map/backward/pallas_call | solution.py:372
  49.2 7.4 %collective-permute-start.16 = (f32[16,8,128]{2,1,0:T(8,128)S(1)}, f32[16,8,128]{2,1,0:T(8,128)S(1)}, u32[]{:S(2)}, u32[]{:S(2)}) collective-permute-start(f32[16,8,128]{2,1,0:T(8,128)S(1)} %get-tuple-element.26), channel_id=1, source_target_pairs={{0,1},{1,0},{2,3},{3,2},{4,5},{5,4},{6,7},{7,6},{8,9},{9,8},{10,11... | collective-permute-start | bytes 196616 | tf_op jit(solution)/shard_map/ppermute | solution.py:391
  58.3 3.5 %collective-permute-start.17 = (bf16[576,128]{1,0:T(8,128)(2,1)S(1)}, bf16[576,128]{1,0:T(8,128)(2,1)S(1)}, u32[]{:S(2)}, u32[]{:S(2)}) collective-permute-start(bf16[576,128]{1,0:T(8,128)(2,1)S(1)} %pad_maximum_fusion.2), channel_id=1, source_target_pairs={{0,2},{2,0},{4,6},{6,4},{8,10},{10,8},{12,14},{14,12},{16,18},{18,... | collective-permute-start | bytes 442376 | tf_op jit(solution)/shard_map/ppermute | solution.py:401
  62.5 4.2 %inner_sweeps.1 = (f32[8,128,128]{2,1,0:T(8,128)S(1)}, f32[4,4,128,128]{3,2,1,0:T(8,128)S(1)}, f32[4,4,16,128]{3,2,1,0:T(8,128)S(1)}) custom-call(f32[16,128,128]{2,1,0:T(8,128)S(1)} %get-tuple-element.25.relaxed, f32[16,16,128]{2,1,0:T(8,128)S(1)} %maximum_select_fusion.strip), custom_call_target="tpu_custom_call" | custom-call | tf_op jit(solution)/shard_map/inner_sweeps/pallas_call | solution.py:409
  66.7 1.8 %collective-permute-done.17.from_near = bf16[576,128]{1,0:T(8,128)(2,1)S(1)} collective-permute-done((bf16[576,128]{1,0:T(8,128)(2,1)S(1)}, bf16[576,128]{1,0:T(8,128)(2,1)S(1)}, u32[]{:S(2)}, u32[]{:S(2)}) %collective-permute-start.17) | collective-permute-done | bytes 147488 | tf_op jit(solution)/shard_map/ppermute | solution.py:401
  68.5 4.6 %edge_sweeps.1 = f32[16,128,128]{2,1,0:T(8,128)} custom-call(f32[8,128,128]{2,1,0:T(8,128)S(1)} %get-tuple-element.27.inner, f32[4,4,128,128]{3,2,1,0:T(8,128)S(1)} %get-tuple-element.28.saved, f32[4,4,16,128]{3,2,1,0:T(8,128)S(1)} %get-tuple-element.29.saved_strip, bf16[576,128]{1,0:T(8,128)(2,1)S(1)} %collective-permute-done.17.from_near, ...), custom_call_target="tpu_custom_call" | custom-call | tf_op jit(solution)/shard_map/edge_sweeps/pallas_call | solution.py:421
  (44 shorter events, 8.3 us)
Async XLA Ops:
  0.6 10.5 %copy-start = (f32[1,256,128]{2,1,0:T(8,128)S(1)}, f32[1,256,128]{2,1,0:T(8,128)}, u32[]{:S(2)}) copy-start(f32[1,256,128]{2,1,0:T(8,128)} %measured.3) | copy-start | bytes 393220
  7.8 8.2 %collective-permute-start.8 = (bf16[8,128,128]{2,1,0:T(8,128)(2,1)S(1)}, bf16[8,128,128]{2,1,0:T(8,128)(2,1)S(1)}, u32[]{:S(2)}, u32[]{:S(2)}) collective-permute-start(bf16[8,128,128]{2,1,0:T(8,128)(2,1)S(1)} %get-tuple-element.22), channel_id=1, source_target_pairs={{0,4},{2,6},{4,0},{6,2},{8,12},{10,14},{12,8},{14,10},{16,20},{18,... | collective-permute-start | bytes 786440 | tf_op jit(solution)/shard_map/ppermute | solution.py:288
  9.9 7.3 %collective-permute-start = (bf16[8,128,128]{2,1,0:T(8,128)(2,1)S(1)}, bf16[8,128,128]{2,1,0:T(8,128)(2,1)S(1)}, u32[]{:S(2)}, u32[]{:S(2)}) collective-permute-start(bf16[8,128,128]{2,1,0:T(8,128)(2,1)S(1)} %get-tuple-element.18), channel_id=1, source_target_pairs={{0,2},{2,0},{4,6},{6,4},{8,10},{10,8},{12,14},{14,12},{16,18},{18,... | collective-permute-start | bytes 786440 | tf_op jit(solution)/shard_map/ppermute | solution.py:288
  11.2 16.0 %collective-permute-start.12 = (f32[1,128,128]{2,1,0:T(8,128)S(1)}, f32[1,128,128]{2,1,0:T(8,128)S(1)}, u32[]{:S(2)}, u32[]{:S(2)}) collective-permute-start(f32[1,128,128]{2,1,0:T(8,128)S(1)} %get-tuple-element.38), channel_id=1, source_target_pairs={{0,16},{2,18},{4,20},{6,22},{8,24},{10,26},{12,28},{14,30},{16,0},... | collective-permute-start | bytes 196616 | tf_op jit(solution)/shard_map/ppermute | solution.py:356
  13.5 15.9 %collective-permute-start.4 = (f32[1,128,128]{2,1,0:T(8,128)S(1)}, f32[1,128,128]{2,1,0:T(8,128)S(1)}, u32[]{:S(2)}, u32[]{:S(2)}) collective-permute-start(f32[1,128,128]{2,1,0:T(8,128)S(1)} %get-tuple-element.39), channel_id=1, source_target_pairs={{0,16},{2,18},{4,20},{6,22},{8,24},{10,26},{12,28},{14,30},{16,0},... | collective-permute-start | bytes 196616 | tf_op jit(solution)/shard_map/ppermute | solution.py:356
  16.1 4.0 %collective-permute-start.9 = (bf16[4,128,128]{2,1,0:T(8,128)(2,1)S(1)}, bf16[4,128,128]{2,1,0:T(8,128)(2,1)S(1)}, u32[]{:S(2)}, u32[]{:S(2)}) collective-permute-start(bf16[4,128,128]{2,1,0:T(8,128)(2,1)S(1)} %slice.84), channel_id=1, source_target_pairs={{0,2},{2,0},{4,6},{6,4},{8,10},{10,8},{12,14},{14,12},{16,18},{18,... | collective-permute-start | bytes 393224 | tf_op jit(solution)/shard_map/ppermute | solution.py:288
  17.3 4.2 %collective-permute-start.1 = (bf16[4,128,128]{2,1,0:T(8,128)(2,1)S(1)}, bf16[4,128,128]{2,1,0:T(8,128)(2,1)S(1)}, u32[]{:S(2)}, u32[]{:S(2)}) collective-permute-start(bf16[4,128,128]{2,1,0:T(8,128)(2,1)S(1)} %slice.85), channel_id=1, source_target_pairs={{0,4},{2,6},{4,0},{6,2},{8,12},{10,14},{12,8},{14,10},{16,20},{18,... | collective-permute-start | bytes 393224 | tf_op jit(solution)/shard_map/ppermute | solution.py:288
  20.1 3.5 %collective-permute-start.10 = (bf16[2,128,128]{2,1,0:T(8,128)(2,1)S(1)}, bf16[2,128,128]{2,1,0:T(8,128)(2,1)S(1)}, u32[]{:S(2)}, u32[]{:S(2)}) collective-permute-start(bf16[2,128,128]{2,1,0:T(8,128)(2,1)S(1)} %slice.86), channel_id=1, source_target_pairs={{0,8},{2,10},{4,12},{6,14},{8,0},{10,2},{12,4},{14,6},{16,24},{18,... | collective-permute-start | bytes 196616 | tf_op jit(solution)/shard_map/ppermute | solution.py:288
  21.6 4.4 %collective-permute-start.2 = (bf16[2,128,128]{2,1,0:T(8,128)(2,1)S(1)}, bf16[2,128,128]{2,1,0:T(8,128)(2,1)S(1)}, u32[]{:S(2)}, u32[]{:S(2)}) collective-permute-start(bf16[2,128,128]{2,1,0:T(8,128)(2,1)S(1)} %slice.87), channel_id=1, source_target_pairs={{0,8},{2,10},{4,12},{6,14},{8,0},{10,2},{12,4},{14,6},{16,24},{18,... | collective-permute-start | bytes 196616 | tf_op jit(solution)/shard_map/ppermute | solution.py:288
  23.6 4.1 %collective-permute-start.11 = (bf16[2,128,128]{2,1,0:T(8,128)(2,1)S(1)}, bf16[2,128,128]{2,1,0:T(8,128)(2,1)S(1)}, u32[]{:S(2)}, u32[]{:S(2)}) collective-permute-start(bf16[2,128,128]{2,1,0:T(8,128)(2,1)S(1)} %get-tuple-element.32), channel_id=1, source_target_pairs={{0,16},{2,18},{4,20},{6,22},{8,24},{10,26},{12,28},{14,30},{16,0},... | collective-permute-start | bytes 196616 | tf_op jit(solution)/shard_map/ppermute | solution.py:292
  26.0 4.1 %collective-permute-start.3 = (bf16[2,128,128]{2,1,0:T(8,128)(2,1)S(1)}, bf16[2,128,128]{2,1,0:T(8,128)(2,1)S(1)}, u32[]{:S(2)}, u32[]{:S(2)}) collective-permute-start(bf16[2,128,128]{2,1,0:T(8,128)(2,1)S(1)} %get-tuple-element.34), channel_id=1, source_target_pairs={{0,16},{2,18},{4,20},{6,22},{8,24},{10,26},{12,28},{14,30},{16,0},... | collective-permute-start | bytes 196616 | tf_op jit(solution)/shard_map/ppermute | solution.py:292
  27.9 3.9 %collective-permute-start.13 = (bf16[2,128,128]{2,1,0:T(8,128)(2,1)S(1)}, bf16[2,128,128]{2,1,0:T(8,128)(2,1)S(1)}, u32[]{:S(2)}, u32[]{:S(2)}) collective-permute-start(bf16[2,128,128]{2,1,0:T(8,128)(2,1)S(1)} %residual.3), channel_id=1, source_target_pairs={{0,8},{2,10},{4,12},{6,14},{8,0},{10,2},{12,4},{14,6},{16,24},{18,... | collective-permute-start | bytes 196616 | tf_op jit(solution)/shard_map/ppermute | solution.py:297
  30.2 3.2 %collective-permute-start.5 = (bf16[2,128,128]{2,1,0:T(8,128)(2,1)S(1)}, bf16[2,128,128]{2,1,0:T(8,128)(2,1)S(1)}, u32[]{:S(2)}, u32[]{:S(2)}) collective-permute-start(bf16[2,128,128]{2,1,0:T(8,128)(2,1)S(1)} %residual.2), channel_id=1, source_target_pairs={{0,8},{2,10},{4,12},{6,14},{8,0},{10,2},{12,4},{14,6},{16,24},{18,... | collective-permute-start | bytes 196616 | tf_op jit(solution)/shard_map/ppermute | solution.py:297
  31.8 3.9 %collective-permute-start.14 = (bf16[4,128,128]{2,1,0:T(8,128)(2,1)S(1)}, bf16[4,128,128]{2,1,0:T(8,128)(2,1)S(1)}, u32[]{:S(2)}, u32[]{:S(2)}) collective-permute-start(bf16[4,128,128]{2,1,0:T(8,128)(2,1)S(1)} %pad_maximum_fusion.5), channel_id=1, source_target_pairs={{0,2},{2,0},{4,6},{6,4},{8,10},{10,8},{12,14},{14,12},{16,18},{18,... | collective-permute-start | bytes 393224 | tf_op jit(solution)/shard_map/ppermute | solution.py:297
  33.4 4.0 %collective-permute-start.6 = (bf16[4,128,128]{2,1,0:T(8,128)(2,1)S(1)}, bf16[4,128,128]{2,1,0:T(8,128)(2,1)S(1)}, u32[]{:S(2)}, u32[]{:S(2)}) collective-permute-start(bf16[4,128,128]{2,1,0:T(8,128)(2,1)S(1)} %pad_maximum_fusion.4), channel_id=1, source_target_pairs={{0,4},{2,6},{4,0},{6,2},{8,12},{10,14},{12,8},{14,10},{16,20},{18,... | collective-permute-start | bytes 393224 | tf_op jit(solution)/shard_map/ppermute | solution.py:297
  35.7 5.8 %collective-permute-start.15 = (bf16[8,128,128]{2,1,0:T(8,128)(2,1)S(1)}, bf16[8,128,128]{2,1,0:T(8,128)(2,1)S(1)}, u32[]{:S(2)}, u32[]{:S(2)}) collective-permute-start(bf16[8,128,128]{2,1,0:T(8,128)(2,1)S(1)} %pad_maximum_fusion.1.b_low), channel_id=1, source_target_pairs={{0,4},{2,6},{4,0},{6,2},{8,12},{10,14},{12,8},{14,10},{16,20},{18,... | collective-permute-start | bytes 786440 | tf_op jit(solution)/shard_map/ppermute | solution.py:299
  37.5 6.8 %collective-permute-start.7 = (bf16[8,128,128]{2,1,0:T(8,128)(2,1)S(1)}, bf16[8,128,128]{2,1,0:T(8,128)(2,1)S(1)}, u32[]{:S(2)}, u32[]{:S(2)}) collective-permute-start(bf16[8,128,128]{2,1,0:T(8,128)(2,1)S(1)} %pad_maximum_fusion.a_low), channel_id=1, source_target_pairs={{0,2},{2,0},{4,6},{6,4},{8,10},{10,8},{12,14},{14,12},{16,18},{18,... | collective-permute-start | bytes 786440 | tf_op jit(solution)/shard_map/ppermute | solution.py:299
  49.2 8.3 %collective-permute-start.16 = (f32[16,8,128]{2,1,0:T(8,128)S(1)}, f32[16,8,128]{2,1,0:T(8,128)S(1)}, u32[]{:S(2)}, u32[]{:S(2)}) collective-permute-start(f32[16,8,128]{2,1,0:T(8,128)S(1)} %get-tuple-element.26), channel_id=1, source_target_pairs={{0,1},{1,0},{2,3},{3,2},{4,5},{5,4},{6,7},{7,6},{8,9},{9,8},{10,11... | collective-permute-start | bytes 196616 | tf_op jit(solution)/shard_map/ppermute | solution.py:391
  57.6 9.1 %collective-permute-start.18 = (bf16[576,128]{1,0:T(8,128)(2,1)S(1)}, bf16[576,128]{1,0:T(8,128)(2,1)S(1)}, u32[]{:S(2)}, u32[]{:S(2)}) collective-permute-start(bf16[576,128]{1,0:T(8,128)(2,1)S(1)} %pad_maximum_fusion.3), channel_id=1, source_target_pairs={{2,4},{4,2},{6,8},{8,6},{10,12},{12,10},{14,16},{16,14},{18,20},{2... | collective-permute-start | bytes 442376 | tf_op jit(solution)/shard_map/ppermute | solution.py:401
  58.3 10.2 %collective-permute-start.17 = (bf16[576,128]{1,0:T(8,128)(2,1)S(1)}, bf16[576,128]{1,0:T(8,128)(2,1)S(1)}, u32[]{:S(2)}, u32[]{:S(2)}) collective-permute-start(bf16[576,128]{1,0:T(8,128)(2,1)S(1)} %pad_maximum_fusion.2), channel_id=1, source_target_pairs={{0,2},{2,0},{4,6},{6,4},{8,10},{10,8},{12,14},{14,12},{16,18},{18,... | collective-permute-start | bytes 442376 | tf_op jit(solution)/shard_map/ppermute | solution.py:401

commit v6 on v5

--- a/solution.py
+++ b/solution.py
@@ -57,15 +57,15 @@
     for t in range(tiles):
         part = (slice(None), pl.ds(t * TILE, TILE))
         copy = pltpu.make_async_copy(image.at[part], pixels.at[part], image_sems.at[t])
-        copy.start()
+        copy.start(priority=0)
         image_copies.append(copy)
-    for fetch in range(1):
-        weight_copy(weights, held, sems, fetch).start()
+    for fetch in range(12):
+        weight_copy(weights, held, sems, fetch).start(priority=1)
     total[...] = jnp.zeros_like(total)
     for copy in image_copies:
         copy.wait()
-    for fetch in range(1, slots // FETCH):
-        weight_copy(weights, held, sems, fetch).start()
+    for fetch in range(12, slots // FETCH):
+        weight_copy(weights, held, sems, fetch).start(priority=1)
     for t in range(tiles):
         tile = pixels[:, t * TILE : (t + 1) * TILE, :].reshape(voxels, pixels.shape[2])
         turned[t] = tile.T.astype(jnp.bfloat16)
@@ -141,13 +141,9 @@
     ):
         for i in range(SWEEPS):
             side[i * cols : (i + 1) * cols] = relaxed[start + i].astype(jnp.bfloat16)
-    lane = lax.broadcasted_iota(jnp.int32, (cols, slices), 1)
-    start = jnp.where(cut == 0, slices - EDGE, 0)
-    edges = jnp.zeros((cols, slices), jnp.float32)
     for i in range(rows):
-        moved = pltpu.roll(relaxed[i], (i * EDGE - start + slices) % slices, 1)
-        edges = jnp.where(lane // EDGE == i, moved, edges)
-    strip[...] = edges.T.reshape(rows, EDGE, cols)
+        across = relaxed[i].T
+        strip[i] = jnp.where(cut == 0, across[slices - EDGE :], across[:EDGE])
 
 
 def shifted(x, axis, by):
@@ -177,19 +173,17 @@
 
 
 def patched(rows, strips, cut):
-    count, _, cols = strips.shape
     slices = rows[0].shape[1]
     low_side = cut == 0
-    mine = jnp.where(low_side, strips[:, :EDGE], strips[:, EDGE:]).reshape(count * EDGE, cols)
-    turned = jnp.concatenate([mine] * (slices // (count * EDGE)), axis=0).T
-    lane = lax.broadcasted_iota(jnp.int32, (cols, slices), 1)
-    start = jnp.where(low_side, slices - EDGE, 0)
+    lane = lax.broadcasted_iota(jnp.int32, rows[0].shape, 1)
     first = jnp.where(low_side, slices - SWEEPS, 0)
     patch = (lane >= first) & (lane < first + SWEEPS)
-    return [
-        jnp.where(patch, pltpu.roll(turned, (start - i * EDGE + slices) % slices, 1), row)
-        for i, row in enumerate(rows)
-    ]
+    gap = jnp.zeros((slices - 2 * EDGE, strips.shape[2]), strips.dtype)
+    result = []
+    for i, row in enumerate(rows):
+        across = jnp.concatenate([strips[i, EDGE:], gap, strips[i, :EDGE]], axis=0)
+        result.append(jnp.where(patch, across.T, row))
+    return result
 
 
 def inner_kernel(relaxed, strip, *refs):

time: 74.4 us -> 73.6 us (0.989)
  Pallas kernels: 20.4 us -> 19.5 us
where the time goes in v6:
time: 73.6 us; the launch traced here: 72.2 us
  starting transfers between devices  34.4 us (47%)
  Pallas kernels  19.5 us (26%)
  waiting for transfers between devices  15.7 us (21%)
  between operations  1.49 us (2%)
  other arithmetic  1 us (1%)
    ppermute x6, starting transfers between devices, sum_chain(): got = lax.ppermute(send, 'plane', partner(bit, planes))  8.34 us
    ppermute x1, starting transfers between devices, per_device(): other = lax.ppermute(strip, 'cuts', [(0, 1), (1, 0)])  7.42 us
    ppermute x2, waiting for transfers between devices, spread_chain(): return (piece, lax.ppermute(piece, 'plane', partner(order[0], planes)))  5.9 us
    pallas_call x1, Pallas kernels, per_device(): pl.pallas_call(functools.partial(forward_kernel, orders), out_shape=(kept...  5.85 us
    ppermute x4, starting transfers between devices, spread_chain(): got = lax.ppermute(piece, 'plane', partner(bit, planes))  5.75 us
    pallas_call x1, Pallas kernels, per_device(): pl.pallas_call(functools.partial(backward_kernel, orders), out_shape=(sha...  4.78 us
    ppermute x6, waiting for transfers between devices, sum_chain(): got = lax.ppermute(send, 'plane', partner(bit, planes))  4.68 us
    pallas_call x1, Pallas kernels, per_device(): pl.pallas_call(functools.partial(edge_kernel, planes=planes), out_shape=s...  4.47 us
  transfers between devices with their start and end apart: 19, of which 12 were waited for; matrix products, arithmetic and copies ran while one was open for 1% of the time, Pallas kernels for 6%

profile of v6, /device:TPU:1, one launch (start us, length us, event | category | flops | bytes accessed | tf_op | source)
XLA Modules:
  0.0 72.2 jit_solution(4646440880430496647)
XLA Ops:
  1.3 5.8 %forward.1 = (f32[8,128,128]{2,1,0:T(8,128)S(1)}, bf16[8,128,128]{2,1,0:T(8,128)(2,1)S(1)}, f32[8,128,128]{2,1,0:T(8,128)S(1)}, bf16[8,128,128]{2,1,0:T(8,128)(2...) custom-call(s32[96]{0:T(128)} %tile_ids.3, s32[96]{0:T(128)} %blocks.3, s32[16]{0:T(128)} %owner.3, ...), custom_call_target="tpu_custom_call" | custom-call | tf_op jit(solution)/shard_map/forward/pallas_call | solution.py:331
  7.2 2.1 %collective-permute-start.8 = (bf16[8,128,128]{2,1,0:T(8,128)(2,1)S(1)}, bf16[8,128,128]{2,1,0:T(8,128)(2,1)S(1)}, u32[]{:S(2)}, u32[]{:S(2)}) collective-permute-start(bf16[8,128,128]{2,1,0:T(8,128)(2,1)S(1)} %get-tuple-element.22), channel_id=1, source_target_pairs={{0,4},{2,6},{4,0},{6,2},{8,12},{10,14},{12,8},{14,10},{16,20},{18,... | collective-permute-start | bytes 786440 | tf_op jit(solution)/shard_map/ppermute | solution.py:282
  9.3 1.2 %collective-permute-start = (bf16[8,128,128]{2,1,0:T(8,128)(2,1)S(1)}, bf16[8,128,128]{2,1,0:T(8,128)(2,1)S(1)}, u32[]{:S(2)}, u32[]{:S(2)}) collective-permute-start(bf16[8,128,128]{2,1,0:T(8,128)(2,1)S(1)} %get-tuple-element.18), channel_id=1, source_target_pairs={{0,2},{2,0},{4,6},{6,4},{8,10},{10,8},{12,14},{14,12},{16,18},{18,... | collective-permute-start | bytes 786440 | tf_op jit(solution)/shard_map/ppermute | solution.py:282
  10.5 2.4 %collective-permute-start.12 = (f32[1,128,128]{2,1,0:T(8,128)S(1)}, f32[1,128,128]{2,1,0:T(8,128)S(1)}, u32[]{:S(2)}, u32[]{:S(2)}) collective-permute-start(f32[1,128,128]{2,1,0:T(8,128)S(1)} %get-tuple-element.38), channel_id=1, source_target_pairs={{0,16},{2,18},{4,20},{6,22},{8,24},{10,26},{12,28},{14,30},{16,0},... | collective-permute-start | bytes 196616 | tf_op jit(solution)/shard_map/ppermute | solution.py:350
  13.0 2.4 %collective-permute-done.8 = bf16[8,128,128]{2,1,0:T(8,128)(2,1)S(1)} collective-permute-done((bf16[8,128,128]{2,1,0:T(8,128)(2,1)S(1)}, bf16[8,128,128]{2,1,0:T(8,128)(2,1)S(1)}, u32[]{:S(2)}, u32[]{:S(2)}) %collective-permute-start.8) | collective-permute-done | bytes 262176 | tf_op jit(solution)/shard_map/ppermute | solution.py:282
  15.4 1.2 %collective-permute-start.9 = (bf16[4,128,128]{2,1,0:T(8,128)(2,1)S(1)}, bf16[4,128,128]{2,1,0:T(8,128)(2,1)S(1)}, u32[]{:S(2)}, u32[]{:S(2)}) collective-permute-start(bf16[4,128,128]{2,1,0:T(8,128)(2,1)S(1)} %slice.84), channel_id=1, source_target_pairs={{0,2},{2,0},{4,6},{6,4},{8,10},{10,8},{12,14},{14,12},{16,18},{18,... | collective-permute-start | bytes 393224 | tf_op jit(solution)/shard_map/ppermute | solution.py:282
  16.7 1.3 %collective-permute-start.1 = (bf16[4,128,128]{2,1,0:T(8,128)(2,1)S(1)}, bf16[4,128,128]{2,1,0:T(8,128)(2,1)S(1)}, u32[]{:S(2)}, u32[]{:S(2)}) collective-permute-start(bf16[4,128,128]{2,1,0:T(8,128)(2,1)S(1)} %slice.85), channel_id=1, source_target_pairs={{0,4},{2,6},{4,0},{6,2},{8,12},{10,14},{12,8},{14,10},{16,20},{18,... | collective-permute-start | bytes 393224 | tf_op jit(solution)/shard_map/ppermute | solution.py:282
  18.0 1.4 %collective-permute-done.9 = bf16[4,128,128]{2,1,0:T(8,128)(2,1)S(1)} collective-permute-done((bf16[4,128,128]{2,1,0:T(8,128)(2,1)S(1)}, bf16[4,128,128]{2,1,0:T(8,128)(2,1)S(1)}, u32[]{:S(2)}, u32[]{:S(2)}) %collective-permute-start.9) | collective-permute-done | bytes 131104 | tf_op jit(solution)/shard_map/ppermute | solution.py:282
  19.5 1.2 %collective-permute-start.10 = (bf16[2,128,128]{2,1,0:T(8,128)(2,1)S(1)}, bf16[2,128,128]{2,1,0:T(8,128)(2,1)S(1)}, u32[]{:S(2)}, u32[]{:S(2)}) collective-permute-start(bf16[2,128,128]{2,1,0:T(8,128)(2,1)S(1)} %slice.86), channel_id=1, source_target_pairs={{0,8},{2,10},{4,12},{6,14},{8,0},{10,2},{12,4},{14,6},{16,24},{18,... | collective-permute-start | bytes 196616 | tf_op jit(solution)/shard_map/ppermute | solution.py:282
  20.9 1.4 %collective-permute-start.2 = (bf16[2,128,128]{2,1,0:T(8,128)(2,1)S(1)}, bf16[2,128,128]{2,1,0:T(8,128)(2,1)S(1)}, u32[]{:S(2)}, u32[]{:S(2)}) collective-permute-start(bf16[2,128,128]{2,1,0:T(8,128)(2,1)S(1)} %slice.87), channel_id=1, source_target_pairs={{0,8},{2,10},{4,12},{6,14},{8,0},{10,2},{12,4},{14,6},{16,24},{18,... | collective-permute-start | bytes 196616 | tf_op jit(solution)/shard_map/ppermute | solution.py:282
  23.0 2.3 %collective-permute-start.11 = (bf16[2,128,128]{2,1,0:T(8,128)(2,1)S(1)}, bf16[2,128,128]{2,1,0:T(8,128)(2,1)S(1)}, u32[]{:S(2)}, u32[]{:S(2)}) collective-permute-start(bf16[2,128,128]{2,1,0:T(8,128)(2,1)S(1)} %get-tuple-element.32), channel_id=1, source_target_pairs={{0,16},{2,18},{4,20},{6,22},{8,24},{10,26},{12,28},{14,30},{16,0},... | collective-permute-start | bytes 196616 | tf_op jit(solution)/shard_map/ppermute | solution.py:286
  25.3 1.3 %collective-permute-start.3 = (bf16[2,128,128]{2,1,0:T(8,128)(2,1)S(1)}, bf16[2,128,128]{2,1,0:T(8,128)(2,1)S(1)}, u32[]{:S(2)}, u32[]{:S(2)}) collective-permute-start(bf16[2,128,128]{2,1,0:T(8,128)(2,1)S(1)} %get-tuple-element.34), channel_id=1, source_target_pairs={{0,16},{2,18},{4,20},{6,22},{8,24},{10,26},{12,28},{14,30},{16,0},... | collective-permute-start | bytes 196616 | tf_op jit(solution)/shard_map/ppermute | solution.py:286
  27.3 1.6 %collective-permute-start.13 = (bf16[2,128,128]{2,1,0:T(8,128)(2,1)S(1)}, bf16[2,128,128]{2,1,0:T(8,128)(2,1)S(1)}, u32[]{:S(2)}, u32[]{:S(2)}) collective-permute-start(bf16[2,128,128]{2,1,0:T(8,128)(2,1)S(1)} %residual.3), channel_id=1, source_target_pairs={{0,8},{2,10},{4,12},{6,14},{8,0},{10,2},{12,4},{14,6},{16,24},{18,... | collective-permute-start | bytes 196616 | tf_op jit(solution)/shard_map/ppermute | solution.py:291
  29.5 1.6 %collective-permute-start.5 = (bf16[2,128,128]{2,1,0:T(8,128)(2,1)S(1)}, bf16[2,128,128]{2,1,0:T(8,128)(2,1)S(1)}, u32[]{:S(2)}, u32[]{:S(2)}) collective-permute-start(bf16[2,128,128]{2,1,0:T(8,128)(2,1)S(1)} %residual.2), channel_id=1, source_target_pairs={{0,8},{2,10},{4,12},{6,14},{8,0},{10,2},{12,4},{14,6},{16,24},{18,... | collective-permute-start | bytes 196616 | tf_op jit(solution)/shard_map/ppermute | solution.py:291
  31.1 1.5 %collective-permute-start.14 = (bf16[4,128,128]{2,1,0:T(8,128)(2,1)S(1)}, bf16[4,128,128]{2,1,0:T(8,128)(2,1)S(1)}, u32[]{:S(2)}, u32[]{:S(2)}) collective-permute-start(bf16[4,128,128]{2,1,0:T(8,128)(2,1)S(1)} %pad_maximum_fusion.5), channel_id=1, source_target_pairs={{0,2},{2,0},{4,6},{6,4},{8,10},{10,8},{12,14},{14,12},{16,18},{18,... | collective-permute-start | bytes 393224 | tf_op jit(solution)/shard_map/ppermute | solution.py:291
  35.0 1.8 %collective-permute-start.15 = (bf16[8,128,128]{2,1,0:T(8,128)(2,1)S(1)}, bf16[8,128,128]{2,1,0:T(8,128)(2,1)S(1)}, u32[]{:S(2)}, u32[]{:S(2)}) collective-permute-start(bf16[8,128,128]{2,1,0:T(8,128)(2,1)S(1)} %pad_maximum_fusion.1.b_low), channel_id=1, source_target_pairs={{0,4},{2,6},{4,0},{6,2},{8,12},{10,14},{12,8},{14,10},{16,20},{18,... | collective-permute-start | bytes 786440 | tf_op jit(solution)/shard_map/ppermute | solution.py:293
  37.8 3.1 %collective-permute-done.15.b_high = bf16[8,128,128]{2,1,0:T(8,128)(2,1)S(1)} collective-permute-done((bf16[8,128,128]{2,1,0:T(8,128)(2,1)S(1)}, bf16[8,128,128]{2,1,0:T(8,128)(2,1)S(1)}, u32[]{:S(2)}, u32[]{:S(2)}) %collective-permute-start.15) | collective-permute-done | bytes 262176 | tf_op jit(solution)/shard_map/ppermute | solution.py:293
  40.9 2.8 %collective-permute-done.7.a_high = bf16[8,128,128]{2,1,0:T(8,128)(2,1)S(1)} collective-permute-done((bf16[8,128,128]{2,1,0:T(8,128)(2,1)S(1)}, bf16[8,128,128]{2,1,0:T(8,128)(2,1)S(1)}, u32[]{:S(2)}, u32[]{:S(2)}) %collective-permute-start.7) | collective-permute-done | bytes 262176 | tf_op jit(solution)/shard_map/ppermute | solution.py:293
  43.7 4.8 %backward.1 = (f32[16,128,128]{2,1,0:T(8,128)S(1)}, bf16[512,128]{1,0:T(8,128)(2,1)S(1)}, bf16[512,128]{1,0:T(8,128)(2,1)S(1)}, f32[16,8,128]{2,1,0:T(8,128)S(1)}) custom-call(s32[96]{0:T(128)} %tile_ids.3, s32[96]{0:T(128)} %blocks.3, s32[16]{0:T(128)} %owner.3, s32[1]{0:T(128)S(6)} %copy.9.count, bf16[8,128,128]{2,1,0:T(8,128)(2,1)S(1)} %pad_maximum_fusion.a_low, ...), custom_call_target="tpu_custom_call" | custom-call | tf_op jit(solution)/shard_map/backward/pallas_call | solution.py:366
  48.5 7.4 %collective-permute-start.16 = (f32[16,8,128]{2,1,0:T(8,128)S(1)}, f32[16,8,128]{2,1,0:T(8,128)S(1)}, u32[]{:S(2)}, u32[]{:S(2)}) collective-permute-start(f32[16,8,128]{2,1,0:T(8,128)S(1)} %get-tuple-element.26), channel_id=1, source_target_pairs={{0,1},{1,0},{2,3},{3,2},{4,5},{5,4},{6,7},{7,6},{8,9},{9,8},{10,11... | collective-permute-start | bytes 196616 | tf_op jit(solution)/shard_map/ppermute | solution.py:385
  57.6 3.5 %collective-permute-start.17 = (bf16[576,128]{1,0:T(8,128)(2,1)S(1)}, bf16[576,128]{1,0:T(8,128)(2,1)S(1)}, u32[]{:S(2)}, u32[]{:S(2)}) collective-permute-start(bf16[576,128]{1,0:T(8,128)(2,1)S(1)} %pad_maximum_fusion.2), channel_id=1, source_target_pairs={{0,2},{2,0},{4,6},{6,4},{8,10},{10,8},{12,14},{14,12},{16,18},{18,... | collective-permute-start | bytes 442376 | tf_op jit(solution)/shard_map/ppermute | solution.py:395
  61.7 4.2 %inner_sweeps.1 = (f32[8,128,128]{2,1,0:T(8,128)S(1)}, f32[4,4,128,128]{3,2,1,0:T(8,128)S(1)}, f32[4,4,16,128]{3,2,1,0:T(8,128)S(1)}) custom-call(f32[16,128,128]{2,1,0:T(8,128)S(1)} %get-tuple-element.25.relaxed, f32[16,16,128]{2,1,0:T(8,128)S(1)} %maximum_select_fusion.strip), custom_call_target="tpu_custom_call" | custom-call | tf_op jit(solution)/shard_map/inner_sweeps/pallas_call | solution.py:403
  65.9 1.9 %collective-permute-done.17.from_near = bf16[576,128]{1,0:T(8,128)(2,1)S(1)} collective-permute-done((bf16[576,128]{1,0:T(8,128)(2,1)S(1)}, bf16[576,128]{1,0:T(8,128)(2,1)S(1)}, u32[]{:S(2)}, u32[]{:S(2)}) %collective-permute-start.17) | collective-permute-done | bytes 147488 | tf_op jit(solution)/shard_map/ppermute | solution.py:395
  67.8 4.5 %edge_sweeps.1 = f32[16,128,128]{2,1,0:T(8,128)} custom-call(f32[8,128,128]{2,1,0:T(8,128)S(1)} %get-tuple-element.27.inner, f32[4,4,128,128]{3,2,1,0:T(8,128)S(1)} %get-tuple-element.28.saved, f32[4,4,16,128]{3,2,1,0:T(8,128)S(1)} %get-tuple-element.29.saved_strip, bf16[576,128]{1,0:T(8,128)(2,1)S(1)} %collective-permute-done.17.from_near, ...), custom_call_target="tpu_custom_call" | custom-call | tf_op jit(solution)/shard_map/edge_sweeps/pallas_call | solution.py:415
  (44 shorter events, 8.3 us)
Async XLA Ops:
  0.6 9.9 %copy-start = (f32[1,256,128]{2,1,0:T(8,128)S(1)}, f32[1,256,128]{2,1,0:T(8,128)}, u32[]{:S(2)}) copy-start(f32[1,256,128]{2,1,0:T(8,128)} %measured.3) | copy-start | bytes 393220
  7.2 8.2 %collective-permute-start.8 = (bf16[8,128,128]{2,1,0:T(8,128)(2,1)S(1)}, bf16[8,128,128]{2,1,0:T(8,128)(2,1)S(1)}, u32[]{:S(2)}, u32[]{:S(2)}) collective-permute-start(bf16[8,128,128]{2,1,0:T(8,128)(2,1)S(1)} %get-tuple-element.22), channel_id=1, source_target_pairs={{0,4},{2,6},{4,0},{6,2},{8,12},{10,14},{12,8},{14,10},{16,20},{18,... | collective-permute-start | bytes 786440 | tf_op jit(solution)/shard_map/ppermute | solution.py:282
  9.3 7.3 %collective-permute-start = (bf16[8,128,128]{2,1,0:T(8,128)(2,1)S(1)}, bf16[8,128,128]{2,1,0:T(8,128)(2,1)S(1)}, u32[]{:S(2)}, u32[]{:S(2)}) collective-permute-start(bf16[8,128,128]{2,1,0:T(8,128)(2,1)S(1)} %get-tuple-element.18), channel_id=1, source_target_pairs={{0,2},{2,0},{4,6},{6,4},{8,10},{10,8},{12,14},{14,12},{16,18},{18,... | collective-permute-start | bytes 786440 | tf_op jit(solution)/shard_map/ppermute | solution.py:282
  10.5 16.0 %collective-permute-start.12 = (f32[1,128,128]{2,1,0:T(8,128)S(1)}, f32[1,128,128]{2,1,0:T(8,128)S(1)}, u32[]{:S(2)}, u32[]{:S(2)}) collective-permute-start(f32[1,128,128]{2,1,0:T(8,128)S(1)} %get-tuple-element.38), channel_id=1, source_target_pairs={{0,16},{2,18},{4,20},{6,22},{8,24},{10,26},{12,28},{14,30},{16,0},... | collective-permute-start | bytes 196616 | tf_op jit(solution)/shard_map/ppermute | solution.py:350
  12.9 15.9 %collective-permute-start.4 = (f32[1,128,128]{2,1,0:T(8,128)S(1)}, f32[1,128,128]{2,1,0:T(8,128)S(1)}, u32[]{:S(2)}, u32[]{:S(2)}) collective-permute-start(f32[1,128,128]{2,1,0:T(8,128)S(1)} %get-tuple-element.39), channel_id=1, source_target_pairs={{0,16},{2,18},{4,20},{6,22},{8,24},{10,26},{12,28},{14,30},{16,0},... | collective-permute-start | bytes 196616 | tf_op jit(solution)/shard_map/ppermute | solution.py:350
  15.4 4.0 %collective-permute-start.9 = (bf16[4,128,128]{2,1,0:T(8,128)(2,1)S(1)}, bf16[4,128,128]{2,1,0:T(8,128)(2,1)S(1)}, u32[]{:S(2)}, u32[]{:S(2)}) collective-permute-start(bf16[4,128,128]{2,1,0:T(8,128)(2,1)S(1)} %slice.84), channel_id=1, source_target_pairs={{0,2},{2,0},{4,6},{6,4},{8,10},{10,8},{12,14},{14,12},{16,18},{18,... | collective-permute-start | bytes 393224 | tf_op jit(solution)/shard_map/ppermute | solution.py:282
  16.7 4.2 %collective-permute-start.1 = (bf16[4,128,128]{2,1,0:T(8,128)(2,1)S(1)}, bf16[4,128,128]{2,1,0:T(8,128)(2,1)S(1)}, u32[]{:S(2)}, u32[]{:S(2)}) collective-permute-start(bf16[4,128,128]{2,1,0:T(8,128)(2,1)S(1)} %slice.85), channel_id=1, source_target_pairs={{0,4},{2,6},{4,0},{6,2},{8,12},{10,14},{12,8},{14,10},{16,20},{18,... | collective-permute-start | bytes 393224 | tf_op jit(solution)/shard_map/ppermute | solution.py:282
  19.5 3.5 %collective-permute-start.10 = (bf16[2,128,128]{2,1,0:T(8,128)(2,1)S(1)}, bf16[2,128,128]{2,1,0:T(8,128)(2,1)S(1)}, u32[]{:S(2)}, u32[]{:S(2)}) collective-permute-start(bf16[2,128,128]{2,1,0:T(8,128)(2,1)S(1)} %slice.86), channel_id=1, source_target_pairs={{0,8},{2,10},{4,12},{6,14},{8,0},{10,2},{12,4},{14,6},{16,24},{18,... | collective-permute-start | bytes 196616 | tf_op jit(solution)/shard_map/ppermute | solution.py:282
  20.9 4.3 %collective-permute-start.2 = (bf16[2,128,128]{2,1,0:T(8,128)(2,1)S(1)}, bf16[2,128,128]{2,1,0:T(8,128)(2,1)S(1)}, u32[]{:S(2)}, u32[]{:S(2)}) collective-permute-start(bf16[2,128,128]{2,1,0:T(8,128)(2,1)S(1)} %slice.87), channel_id=1, source_target_pairs={{0,8},{2,10},{4,12},{6,14},{8,0},{10,2},{12,4},{14,6},{16,24},{18,... | collective-permute-start | bytes 196616 | tf_op jit(solution)/shard_map/ppermute | solution.py:282
  23.0 4.1 %collective-permute-start.11 = (bf16[2,128,128]{2,1,0:T(8,128)(2,1)S(1)}, bf16[2,128,128]{2,1,0:T(8,128)(2,1)S(1)}, u32[]{:S(2)}, u32[]{:S(2)}) collective-permute-start(bf16[2,128,128]{2,1,0:T(8,128)(2,1)S(1)} %get-tuple-element.32), channel_id=1, source_target_pairs={{0,16},{2,18},{4,20},{6,22},{8,24},{10,26},{12,28},{14,30},{16,0},... | collective-permute-start | bytes 196616 | tf_op jit(solution)/shard_map/ppermute | solution.py:286
  25.3 4.1 %collective-permute-start.3 = (bf16[2,128,128]{2,1,0:T(8,128)(2,1)S(1)}, bf16[2,128,128]{2,1,0:T(8,128)(2,1)S(1)}, u32[]{:S(2)}, u32[]{:S(2)}) collective-permute-start(bf16[2,128,128]{2,1,0:T(8,128)(2,1)S(1)} %get-tuple-element.34), channel_id=1, source_target_pairs={{0,16},{2,18},{4,20},{6,22},{8,24},{10,26},{12,28},{14,30},{16,0},... | collective-permute-start | bytes 196616 | tf_op jit(solution)/shard_map/ppermute | solution.py:286
  27.3 3.8 %collective-permute-start.13 = (bf16[2,128,128]{2,1,0:T(8,128)(2,1)S(1)}, bf16[2,128,128]{2,1,0:T(8,128)(2,1)S(1)}, u32[]{:S(2)}, u32[]{:S(2)}) collective-permute-start(bf16[2,128,128]{2,1,0:T(8,128)(2,1)S(1)} %residual.3), channel_id=1, source_target_pairs={{0,8},{2,10},{4,12},{6,14},{8,0},{10,2},{12,4},{14,6},{16,24},{18,... | collective-permute-start | bytes 196616 | tf_op jit(solution)/shard_map/ppermute | solution.py:291
  29.5 3.2 %collective-permute-start.5 = (bf16[2,128,128]{2,1,0:T(8,128)(2,1)S(1)}, bf16[2,128,128]{2,1,0:T(8,128)(2,1)S(1)}, u32[]{:S(2)}, u32[]{:S(2)}) collective-permute-start(bf16[2,128,128]{2,1,0:T(8,128)(2,1)S(1)} %residual.2), channel_id=1, source_target_pairs={{0,8},{2,10},{4,12},{6,14},{8,0},{10,2},{12,4},{14,6},{16,24},{18,... | collective-permute-start | bytes 196616 | tf_op jit(solution)/shard_map/ppermute | solution.py:291
  31.1 3.9 %collective-permute-start.14 = (bf16[4,128,128]{2,1,0:T(8,128)(2,1)S(1)}, bf16[4,128,128]{2,1,0:T(8,128)(2,1)S(1)}, u32[]{:S(2)}, u32[]{:S(2)}) collective-permute-start(bf16[4,128,128]{2,1,0:T(8,128)(2,1)S(1)} %pad_maximum_fusion.5), channel_id=1, source_target_pairs={{0,2},{2,0},{4,6},{6,4},{8,10},{10,8},{12,14},{14,12},{16,18},{18,... | collective-permute-start | bytes 393224 | tf_op jit(solution)/shard_map/ppermute | solution.py:291
  32.8 4.1 %collective-permute-start.6 = (bf16[4,128,128]{2,1,0:T(8,128)(2,1)S(1)}, bf16[4,128,128]{2,1,0:T(8,128)(2,1)S(1)}, u32[]{:S(2)}, u32[]{:S(2)}) collective-permute-start(bf16[4,128,128]{2,1,0:T(8,128)(2,1)S(1)} %pad_maximum_fusion.4), channel_id=1, source_target_pairs={{0,4},{2,6},{4,0},{6,2},{8,12},{10,14},{12,8},{14,10},{16,20},{18,... | collective-permute-start | bytes 393224 | tf_op jit(solution)/shard_map/ppermute | solution.py:291
  35.0 5.9 %collective-permute-start.15 = (bf16[8,128,128]{2,1,0:T(8,128)(2,1)S(1)}, bf16[8,128,128]{2,1,0:T(8,128)(2,1)S(1)}, u32[]{:S(2)}, u32[]{:S(2)}) collective-permute-start(bf16[8,128,128]{2,1,0:T(8,128)(2,1)S(1)} %pad_maximum_fusion.1.b_low), channel_id=1, source_target_pairs={{0,4},{2,6},{4,0},{6,2},{8,12},{10,14},{12,8},{14,10},{16,20},{18,... | collective-permute-start | bytes 786440 | tf_op jit(solution)/shard_map/ppermute | solution.py:293
  36.9 6.8 %collective-permute-start.7 = (bf16[8,128,128]{2,1,0:T(8,128)(2,1)S(1)}, bf16[8,128,128]{2,1,0:T(8,128)(2,1)S(1)}, u32[]{:S(2)}, u32[]{:S(2)}) collective-permute-start(bf16[8,128,128]{2,1,0:T(8,128)(2,1)S(1)} %pad_maximum_fusion.a_low), channel_id=1, source_target_pairs={{0,2},{2,0},{4,6},{6,4},{8,10},{10,8},{12,14},{14,12},{16,18},{18,... | collective-permute-start | bytes 786440 | tf_op jit(solution)/shard_map/ppermute | solution.py:293
  48.5 8.3 %collective-permute-start.16 = (f32[16,8,128]{2,1,0:T(8,128)S(1)}, f32[16,8,128]{2,1,0:T(8,128)S(1)}, u32[]{:S(2)}, u32[]{:S(2)}) collective-permute-start(f32[16,8,128]{2,1,0:T(8,128)S(1)} %get-tuple-element.26), channel_id=1, source_target_pairs={{0,1},{1,0},{2,3},{3,2},{4,5},{5,4},{6,7},{7,6},{8,9},{9,8},{10,11... | collective-permute-start | bytes 196616 | tf_op jit(solution)/shard_map/ppermute | solution.py:385
  56.9 9.0 %collective-permute-start.18 = (bf16[576,128]{1,0:T(8,128)(2,1)S(1)}, bf16[576,128]{1,0:T(8,128)(2,1)S(1)}, u32[]{:S(2)}, u32[]{:S(2)}) collective-permute-start(bf16[576,128]{1,0:T(8,128)(2,1)S(1)} %pad_maximum_fusion.3), channel_id=1, source_target_pairs={{2,4},{4,2},{6,8},{8,6},{10,12},{12,10},{14,16},{16,14},{18,20},{2... | collective-permute-start | bytes 442376 | tf_op jit(solution)/shard_map/ppermute | solution.py:395
  57.6 10.2 %collective-permute-start.17 = (bf16[576,128]{1,0:T(8,128)(2,1)S(1)}, bf16[576,128]{1,0:T(8,128)(2,1)S(1)}, u32[]{:S(2)}, u32[]{:S(2)}) collective-permute-start(bf16[576,128]{1,0:T(8,128)(2,1)S(1)} %pad_maximum_fusion.2), channel_id=1, source_target_pairs={{0,2},{2,0},{4,6},{6,4},{8,10},{10,8},{12,14},{14,12},{16,18},{18,... | collective-permute-start | bytes 442376 | tf_op jit(solution)/shard_map/ppermute | solution.py:395

commit v7 on v6

--- a/solution.py
+++ b/solution.py
@@ -12,7 +12,7 @@
 EDGE = 8
 FETCH = 8
 FORWARD_GROUP = 16
-BACKWARD_GROUP = 48
+BACKWARD_GROUP = 96
 
 smooth_square = 0.09
 flow_step = 0.04
@@ -212,8 +212,8 @@
 
 
 def edge_kernel(
-    inner, saved, saved_strip, from_near, from_far, volume,
-    low_field, low_strip, high_field, high_strip, ends, sems, *, planes,
+    inner, saved, saved_strip, from_near, ends_near, from_far, volume,
+    low_field, low_strip, high_field, high_strip, finished, sems, *, planes,
 ):
     rows, cols, slices = volume.shape
     me, cut = lax.axis_index("plane"), lax.axis_index("cuts")
@@ -221,13 +221,14 @@
     inner_copy.start()
     body_rows = SWEEPS * cols
     even = lax.rem(me, 2) == 0
-    for other, this, field, strip, at in (
-        (from_near, from_far, low_field, low_strip, (slice(0, 4),)),
-        (from_far, from_near, high_field, high_strip, (0, slice(2, 6))),
+    for far_side, field, strip, at in (
+        (even, low_field, low_strip, (slice(0, 4),)),
+        (~even, high_field, high_strip, (0, slice(2, 6))),
     ):
-        halo = jnp.where(even, this[...], other[...])
-        field[at] = halo[:body_rows].astype(jnp.float32).reshape(SWEEPS, cols, slices)
-        strip[at] = halo[body_rows:].astype(jnp.float32).reshape(SWEEPS, 2 * EDGE, cols)
+        halo = jnp.where(far_side, from_far[:body_rows], from_near[...])
+        ends = jnp.where(far_side, from_far[body_rows:], ends_near[...])
+        field[at] = halo.astype(jnp.float32).reshape(SWEEPS, cols, slices)
+        strip[at] = ends.astype(jnp.float32).reshape(SWEEPS, 2 * EDGE, cols)
     pairs = ((low_field, high_field, saved), (low_strip, high_strip, saved_strip))
     for k in range(SWEEPS):
         now, later = k % 2, (k + 1) % 2
@@ -260,15 +261,12 @@
     last = SWEEPS % 2
     outer = [low_field[i] for i in range(SWEEPS)] + [high_field[last, 2 + i] for i in range(SWEEPS)]
     strips = jnp.concatenate([low_strip[0:4], high_strip[last, 2:6]], axis=0)
+    copies = [inner_copy]
     for i, row in enumerate(patched(outer, strips, cut)):
-        ends[i] = row
-    copies = [
-        inner_copy,
-        pltpu.make_async_copy(ends.at[pl.ds(0, SWEEPS)], volume.at[pl.ds(0, SWEEPS)], sems.at[1]),
-        pltpu.make_async_copy(ends.at[pl.ds(SWEEPS, SWEEPS)], volume.at[pl.ds(rows - SWEEPS, SWEEPS)], sems.at[2]),
-    ]
-    for copy in copies[1:]:
-        copy.start()
+        finished[i] = row
+        place = i if i < SWEEPS else rows - 2 * SWEEPS + i
+        copies.append(pltpu.make_async_copy(finished.at[i], volume.at[place], sems.at[1 + i]))
+        copies[-1].start()
     for copy in copies:
         copy.wait()
 
@@ -390,14 +388,16 @@
     even = lax.rem(lax.axis_index("plane"), 2) == 0
     ends = both[rows - SWEEPS :], both[:SWEEPS]
 
-    def trade(main, end_even, end_odd, pairs):
-        end = jnp.where(even, end_even, end_odd).astype(bf16).reshape(-1, cols)
-        return lax.ppermute(jnp.concatenate([main, end], axis=0), "plane", pairs)
+    def ends_for(end_even, end_odd):
+        return jnp.where(even, end_even, end_odd).astype(bf16).reshape(-1, cols)
 
     near = [(i, i ^ 1) for i in range(planes)]
     far = [(i, i + 1 if i % 2 else i - 1) for i in range(1, planes - 1)]
-    from_far = trade(to_far, ends[1], ends[0], far)
-    from_near = trade(to_near, ends[0], ends[1], near)
+    from_near = lax.ppermute(to_near, "plane", near)
+    from_far = lax.ppermute(
+        jnp.concatenate([to_far, ends_for(ends[1], ends[0])], axis=0), "plane", far
+    )
+    ends_near = lax.ppermute(ends_for(ends[0], ends[1]), "plane", near)
 
     spans = (cols, slices), (2 * EDGE, cols)
     inner, saved, saved_strip = pl.pallas_call(
@@ -415,17 +415,17 @@
     volume = pl.pallas_call(
         functools.partial(edge_kernel, planes=planes),
         out_shape=shape((rows, cols, slices), f32),
-        in_specs=[VMEM] * 5,
+        in_specs=[VMEM] * 6,
         out_specs=HBM,
         scratch_shapes=[
             *(pltpu.VMEM((6, *span), f32) for span in spans),
             *(pltpu.VMEM((2, 6, *span), f32) for span in spans),
             pltpu.VMEM((2 * SWEEPS, cols, slices), f32),
-            pltpu.SemaphoreType.DMA((3,)),
+            pltpu.SemaphoreType.DMA((1 + 2 * SWEEPS,)),
         ],
         compiler_params=PARAMS,
         name="edge_sweeps",
-    )(inner, saved, saved_strip, from_near, from_far)
+    )(inner, saved, saved_strip, from_near, ends_near, from_far)
     return (volume, residual)
 
 

time: 73.6 us -> 73.3 us (level)
    ppermute x2 -> x3, starting transfers between devices: 4.21 us -> 4.31 us  [the longest x1 3.54 us: per_device(): from_near = lax.ppermute(to_near, 'plane', near)]
    ppermute x2 -> x3, waiting for transfers between devices: 1.85 us -> 1.79 us  [the longest x1 1.79 us: per_device(): ends_near = lax.ppermute(ends_for(ends[0], ends[1]), 'plane', near)]
  transfers between devices with their start and end apart: 19 -> 20, of which waited for: 12 -> 12; matrix products, arithmetic and copies ran while one was open for 1% -> 1% of each run, Pallas kernels for 6% -> 6%
where the time goes in v7:
time: 73.3 us; the launch traced here: 72 us
  starting transfers between devices  34.5 us (47%)
  Pallas kernels  19.3 us (26%)
  waiting for transfers between devices  15.6 us (21%)
  between operations  1.48 us (2%)
  other arithmetic  0.98 us (1%)
    ppermute x6, starting transfers between devices, sum_chain(): got = lax.ppermute(send, 'plane', partner(bit, planes))  8.34 us
    ppermute x1, starting transfers between devices, per_device(): other = lax.ppermute(strip, 'cuts', [(0, 1), (1, 0)])  7.42 us
    ppermute x2, waiting for transfers between devices, spread_chain(): return (piece, lax.ppermute(piece, 'plane', partner(order[0], planes)))  5.9 us
    pallas_call x1, Pallas kernels, per_device(): pl.pallas_call(functools.partial(forward_kernel, orders), out_shape=(kept...  5.85 us
    ppermute x4, starting transfers between devices, spread_chain(): got = lax.ppermute(piece, 'plane', partner(bit, planes))  5.75 us
    ppermute x6, waiting for transfers between devices, sum_chain(): got = lax.ppermute(send, 'plane', partner(bit, planes))  4.68 us
    pallas_call x1, Pallas kernels, per_device(): pl.pallas_call(functools.partial(backward_kernel, orders), out_shape=(sha...  4.62 us
    pallas_call x1, Pallas kernels, per_device(): pl.pallas_call(functools.partial(edge_kernel, planes=planes), out_shape=s...  4.41 us
  transfers between devices with their start and end apart: 20, of which 12 were waited for; matrix products, arithmetic and copies ran while one was open for 1% of the time, Pallas kernels for 6%

profile of v7, /device:TPU:1, one launch (start us, length us, event | category | flops | bytes accessed | tf_op | source)
XLA Modules:
  0.0 72.0 jit_solution(2899950291432043083)
XLA Ops:
  1.3 5.8 %forward.1 = (f32[8,128,128]{2,1,0:T(8,128)S(1)}, bf16[8,128,128]{2,1,0:T(8,128)(2,1)S(1)}, f32[8,128,128]{2,1,0:T(8,128)S(1)}, bf16[8,128,128]{2,1,0:T(8,128)(2...) custom-call(s32[96]{0:T(128)} %tile_ids.3, s32[96]{0:T(128)} %blocks.3, s32[16]{0:T(128)} %owner.3, ...), custom_call_target="tpu_custom_call" | custom-call | tf_op jit(solution)/shard_map/forward/pallas_call | solution.py:329
  7.2 2.1 %collective-permute-start.8 = (bf16[8,128,128]{2,1,0:T(8,128)(2,1)S(1)}, bf16[8,128,128]{2,1,0:T(8,128)(2,1)S(1)}, u32[]{:S(2)}, u32[]{:S(2)}) collective-permute-start(bf16[8,128,128]{2,1,0:T(8,128)(2,1)S(1)} %get-tuple-element.22), channel_id=1, source_target_pairs={{0,4},{2,6},{4,0},{6,2},{8,12},{10,14},{12,8},{14,10},{16,20},{18,... | collective-permute-start | bytes 786440 | tf_op jit(solution)/shard_map/ppermute | solution.py:280
  9.3 1.2 %collective-permute-start = (bf16[8,128,128]{2,1,0:T(8,128)(2,1)S(1)}, bf16[8,128,128]{2,1,0:T(8,128)(2,1)S(1)}, u32[]{:S(2)}, u32[]{:S(2)}) collective-permute-start(bf16[8,128,128]{2,1,0:T(8,128)(2,1)S(1)} %get-tuple-element.18), channel_id=1, source_target_pairs={{0,2},{2,0},{4,6},{6,4},{8,10},{10,8},{12,14},{14,12},{16,18},{18,... | collective-permute-start | bytes 786440 | tf_op jit(solution)/shard_map/ppermute | solution.py:280
  10.5 2.4 %collective-permute-start.12 = (f32[1,128,128]{2,1,0:T(8,128)S(1)}, f32[1,128,128]{2,1,0:T(8,128)S(1)}, u32[]{:S(2)}, u32[]{:S(2)}) collective-permute-start(f32[1,128,128]{2,1,0:T(8,128)S(1)} %get-tuple-element.38), channel_id=1, source_target_pairs={{0,16},{2,18},{4,20},{6,22},{8,24},{10,26},{12,28},{14,30},{16,0},... | collective-permute-start | bytes 196616 | tf_op jit(solution)/shard_map/ppermute | solution.py:348
  13.0 2.4 %collective-permute-done.8 = bf16[8,128,128]{2,1,0:T(8,128)(2,1)S(1)} collective-permute-done((bf16[8,128,128]{2,1,0:T(8,128)(2,1)S(1)}, bf16[8,128,128]{2,1,0:T(8,128)(2,1)S(1)}, u32[]{:S(2)}, u32[]{:S(2)}) %collective-permute-start.8) | collective-permute-done | bytes 262176 | tf_op jit(solution)/shard_map/ppermute | solution.py:280
  15.4 1.2 %collective-permute-start.9 = (bf16[4,128,128]{2,1,0:T(8,128)(2,1)S(1)}, bf16[4,128,128]{2,1,0:T(8,128)(2,1)S(1)}, u32[]{:S(2)}, u32[]{:S(2)}) collective-permute-start(bf16[4,128,128]{2,1,0:T(8,128)(2,1)S(1)} %slice.84), channel_id=1, source_target_pairs={{0,2},{2,0},{4,6},{6,4},{8,10},{10,8},{12,14},{14,12},{16,18},{18,... | collective-permute-start | bytes 393224 | tf_op jit(solution)/shard_map/ppermute | solution.py:280
  16.7 1.3 %collective-permute-start.1 = (bf16[4,128,128]{2,1,0:T(8,128)(2,1)S(1)}, bf16[4,128,128]{2,1,0:T(8,128)(2,1)S(1)}, u32[]{:S(2)}, u32[]{:S(2)}) collective-permute-start(bf16[4,128,128]{2,1,0:T(8,128)(2,1)S(1)} %slice.85), channel_id=1, source_target_pairs={{0,4},{2,6},{4,0},{6,2},{8,12},{10,14},{12,8},{14,10},{16,20},{18,... | collective-permute-start | bytes 393224 | tf_op jit(solution)/shard_map/ppermute | solution.py:280
  18.0 1.4 %collective-permute-done.9 = bf16[4,128,128]{2,1,0:T(8,128)(2,1)S(1)} collective-permute-done((bf16[4,128,128]{2,1,0:T(8,128)(2,1)S(1)}, bf16[4,128,128]{2,1,0:T(8,128)(2,1)S(1)}, u32[]{:S(2)}, u32[]{:S(2)}) %collective-permute-start.9) | collective-permute-done | bytes 131104 | tf_op jit(solution)/shard_map/ppermute | solution.py:280
  19.5 1.2 %collective-permute-start.10 = (bf16[2,128,128]{2,1,0:T(8,128)(2,1)S(1)}, bf16[2,128,128]{2,1,0:T(8,128)(2,1)S(1)}, u32[]{:S(2)}, u32[]{:S(2)}) collective-permute-start(bf16[2,128,128]{2,1,0:T(8,128)(2,1)S(1)} %slice.86), channel_id=1, source_target_pairs={{0,8},{2,10},{4,12},{6,14},{8,0},{10,2},{12,4},{14,6},{16,24},{18,... | collective-permute-start | bytes 196616 | tf_op jit(solution)/shard_map/ppermute | solution.py:280
  20.9 1.4 %collective-permute-start.2 = (bf16[2,128,128]{2,1,0:T(8,128)(2,1)S(1)}, bf16[2,128,128]{2,1,0:T(8,128)(2,1)S(1)}, u32[]{:S(2)}, u32[]{:S(2)}) collective-permute-start(bf16[2,128,128]{2,1,0:T(8,128)(2,1)S(1)} %slice.87), channel_id=1, source_target_pairs={{0,8},{2,10},{4,12},{6,14},{8,0},{10,2},{12,4},{14,6},{16,24},{18,... | collective-permute-start | bytes 196616 | tf_op jit(solution)/shard_map/ppermute | solution.py:280
  23.0 2.3 %collective-permute-start.11 = (bf16[2,128,128]{2,1,0:T(8,128)(2,1)S(1)}, bf16[2,128,128]{2,1,0:T(8,128)(2,1)S(1)}, u32[]{:S(2)}, u32[]{:S(2)}) collective-permute-start(bf16[2,128,128]{2,1,0:T(8,128)(2,1)S(1)} %get-tuple-element.32), channel_id=1, source_target_pairs={{0,16},{2,18},{4,20},{6,22},{8,24},{10,26},{12,28},{14,30},{16,0},... | collective-permute-start | bytes 196616 | tf_op jit(solution)/shard_map/ppermute | solution.py:284
  25.3 1.3 %collective-permute-start.3 = (bf16[2,128,128]{2,1,0:T(8,128)(2,1)S(1)}, bf16[2,128,128]{2,1,0:T(8,128)(2,1)S(1)}, u32[]{:S(2)}, u32[]{:S(2)}) collective-permute-start(bf16[2,128,128]{2,1,0:T(8,128)(2,1)S(1)} %get-tuple-element.34), channel_id=1, source_target_pairs={{0,16},{2,18},{4,20},{6,22},{8,24},{10,26},{12,28},{14,30},{16,0},... | collective-permute-start | bytes 196616 | tf_op jit(solution)/shard_map/ppermute | solution.py:284
  27.3 1.6 %collective-permute-start.13 = (bf16[2,128,128]{2,1,0:T(8,128)(2,1)S(1)}, bf16[2,128,128]{2,1,0:T(8,128)(2,1)S(1)}, u32[]{:S(2)}, u32[]{:S(2)}) collective-permute-start(bf16[2,128,128]{2,1,0:T(8,128)(2,1)S(1)} %residual.3), channel_id=1, source_target_pairs={{0,8},{2,10},{4,12},{6,14},{8,0},{10,2},{12,4},{14,6},{16,24},{18,... | collective-permute-start | bytes 196616 | tf_op jit(solution)/shard_map/ppermute | solution.py:289
  29.5 1.6 %collective-permute-start.5 = (bf16[2,128,128]{2,1,0:T(8,128)(2,1)S(1)}, bf16[2,128,128]{2,1,0:T(8,128)(2,1)S(1)}, u32[]{:S(2)}, u32[]{:S(2)}) collective-permute-start(bf16[2,128,128]{2,1,0:T(8,128)(2,1)S(1)} %residual.2), channel_id=1, source_target_pairs={{0,8},{2,10},{4,12},{6,14},{8,0},{10,2},{12,4},{14,6},{16,24},{18,... | collective-permute-start | bytes 196616 | tf_op jit(solution)/shard_map/ppermute | solution.py:289
  31.1 1.5 %collective-permute-start.14 = (bf16[4,128,128]{2,1,0:T(8,128)(2,1)S(1)}, bf16[4,128,128]{2,1,0:T(8,128)(2,1)S(1)}, u32[]{:S(2)}, u32[]{:S(2)}) collective-permute-start(bf16[4,128,128]{2,1,0:T(8,128)(2,1)S(1)} %pad_maximum_fusion.4), channel_id=1, source_target_pairs={{0,2},{2,0},{4,6},{6,4},{8,10},{10,8},{12,14},{14,12},{16,18},{18,... | collective-permute-start | bytes 393224 | tf_op jit(solution)/shard_map/ppermute | solution.py:289
  35.0 1.8 %collective-permute-start.15 = (bf16[8,128,128]{2,1,0:T(8,128)(2,1)S(1)}, bf16[8,128,128]{2,1,0:T(8,128)(2,1)S(1)}, u32[]{:S(2)}, u32[]{:S(2)}) collective-permute-start(bf16[8,128,128]{2,1,0:T(8,128)(2,1)S(1)} %pad_maximum_fusion.1.b_low), channel_id=1, source_target_pairs={{0,4},{2,6},{4,0},{6,2},{8,12},{10,14},{12,8},{14,10},{16,20},{18,... | collective-permute-start | bytes 786440 | tf_op jit(solution)/shard_map/ppermute | solution.py:291
  37.8 3.1 %collective-permute-done.15.b_high = bf16[8,128,128]{2,1,0:T(8,128)(2,1)S(1)} collective-permute-done((bf16[8,128,128]{2,1,0:T(8,128)(2,1)S(1)}, bf16[8,128,128]{2,1,0:T(8,128)(2,1)S(1)}, u32[]{:S(2)}, u32[]{:S(2)}) %collective-permute-start.15) | collective-permute-done | bytes 262176 | tf_op jit(solution)/shard_map/ppermute | solution.py:291
  40.9 2.8 %collective-permute-done.7.a_high = bf16[8,128,128]{2,1,0:T(8,128)(2,1)S(1)} collective-permute-done((bf16[8,128,128]{2,1,0:T(8,128)(2,1)S(1)}, bf16[8,128,128]{2,1,0:T(8,128)(2,1)S(1)}, u32[]{:S(2)}, u32[]{:S(2)}) %collective-permute-start.7) | collective-permute-done | bytes 262176 | tf_op jit(solution)/shard_map/ppermute | solution.py:291
  43.7 4.6 %backward.1 = (f32[16,128,128]{2,1,0:T(8,128)S(1)}, bf16[512,128]{1,0:T(8,128)(2,1)S(1)}, bf16[512,128]{1,0:T(8,128)(2,1)S(1)}, f32[16,8,128]{2,1,0:T(8,128)S(1)}) custom-call(s32[96]{0:T(128)} %tile_ids.3, s32[96]{0:T(128)} %blocks.3, s32[16]{0:T(128)} %owner.3, s32[1]{0:T(128)S(6)} %copy.9.count, bf16[8,128,128]{2,1,0:T(8,128)(2,1)S(1)} %pad_maximum_fusion.a_low, ...), custom_call_target="tpu_custom_call" | custom-call | tf_op jit(solution)/shard_map/backward/pallas_call | solution.py:364
  48.3 7.4 %collective-permute-start.16 = (f32[16,8,128]{2,1,0:T(8,128)S(1)}, f32[16,8,128]{2,1,0:T(8,128)S(1)}, u32[]{:S(2)}, u32[]{:S(2)}) collective-permute-start(f32[16,8,128]{2,1,0:T(8,128)S(1)} %get-tuple-element.26), channel_id=1, source_target_pairs={{0,1},{1,0},{2,3},{3,2},{4,5},{5,4},{6,7},{7,6},{8,9},{9,8},{10,11... | collective-permute-start | bytes 196616 | tf_op jit(solution)/shard_map/ppermute | solution.py:383
  57.4 3.5 %collective-permute-start.17 = (bf16[512,128]{1,0:T(8,128)(2,1)S(1)}, bf16[512,128]{1,0:T(8,128)(2,1)S(1)}, u32[]{:S(2)}, u32[]{:S(2)}) collective-permute-start(bf16[512,128]{1,0:T(8,128)(2,1)S(1)} %get-tuple-element.30), channel_id=1, source_target_pairs={{0,2},{2,0},{4,6},{6,4},{8,10},{10,8},{12,14},{14,12},{16,18},{18,... | collective-permute-start | bytes 393224 | tf_op jit(solution)/shard_map/ppermute | solution.py:396
  61.7 4.2 %inner_sweeps.1 = (f32[8,128,128]{2,1,0:T(8,128)S(1)}, f32[4,4,128,128]{3,2,1,0:T(8,128)S(1)}, f32[4,4,16,128]{3,2,1,0:T(8,128)S(1)}) custom-call(f32[16,128,128]{2,1,0:T(8,128)S(1)} %get-tuple-element.25.relaxed, f32[16,16,128]{2,1,0:T(8,128)S(1)} %maximum_select_fusion.strip), custom_call_target="tpu_custom_call" | custom-call | tf_op jit(solution)/shard_map/inner_sweeps/pallas_call | solution.py:403
  65.8 1.8 %collective-permute-done.18.ends_near = bf16[64,128]{1,0:T(8,128)(2,1)S(1)} collective-permute-done((bf16[64,128]{1,0:T(8,128)(2,1)S(1)}, bf16[64,128]{1,0:T(8,128)(2,1)S(1)}, u32[]{:S(2)}, u32[]{:S(2)}) %collective-permute-start.18) | collective-permute-done | bytes 16416 | tf_op jit(solution)/shard_map/ppermute | solution.py:400
  67.6 4.4 %edge_sweeps.1 = f32[16,128,128]{2,1,0:T(8,128)} custom-call(f32[8,128,128]{2,1,0:T(8,128)S(1)} %get-tuple-element.27.inner, f32[4,4,128,128]{3,2,1,0:T(8,128)S(1)} %get-tuple-element.28.saved, f32[4,4,16,128]{3,2,1,0:T(8,128)S(1)} %get-tuple-element.29.saved_strip, bf16[512,128]{1,0:T(8,128)(2,1)S(1)} %collective-permute-done.17.from_near, ...), custom_call_target="tpu_custom_call" | custom-call | tf_op jit(solution)/shard_map/edge_sweeps/pallas_call | solution.py:415
  (45 shorter events, 8.4 us)
Async XLA Ops:
  0.6 9.9 %copy-start = (f32[1,256,128]{2,1,0:T(8,128)S(1)}, f32[1,256,128]{2,1,0:T(8,128)}, u32[]{:S(2)}) copy-start(f32[1,256,128]{2,1,0:T(8,128)} %measured.3) | copy-start | bytes 393220
  7.2 8.2 %collective-permute-start.8 = (bf16[8,128,128]{2,1,0:T(8,128)(2,1)S(1)}, bf16[8,128,128]{2,1,0:T(8,128)(2,1)S(1)}, u32[]{:S(2)}, u32[]{:S(2)}) collective-permute-start(bf16[8,128,128]{2,1,0:T(8,128)(2,1)S(1)} %get-tuple-element.22), channel_id=1, source_target_pairs={{0,4},{2,6},{4,0},{6,2},{8,12},{10,14},{12,8},{14,10},{16,20},{18,... | collective-permute-start | bytes 786440 | tf_op jit(solution)/shard_map/ppermute | solution.py:280
  9.3 7.3 %collective-permute-start = (bf16[8,128,128]{2,1,0:T(8,128)(2,1)S(1)}, bf16[8,128,128]{2,1,0:T(8,128)(2,1)S(1)}, u32[]{:S(2)}, u32[]{:S(2)}) collective-permute-start(bf16[8,128,128]{2,1,0:T(8,128)(2,1)S(1)} %get-tuple-element.18), channel_id=1, source_target_pairs={{0,2},{2,0},{4,6},{6,4},{8,10},{10,8},{12,14},{14,12},{16,18},{18,... | collective-permute-start | bytes 786440 | tf_op jit(solution)/shard_map/ppermute | solution.py:280
  10.5 16.0 %collective-permute-start.12 = (f32[1,128,128]{2,1,0:T(8,128)S(1)}, f32[1,128,128]{2,1,0:T(8,128)S(1)}, u32[]{:S(2)}, u32[]{:S(2)}) collective-permute-start(f32[1,128,128]{2,1,0:T(8,128)S(1)} %get-tuple-element.38), channel_id=1, source_target_pairs={{0,16},{2,18},{4,20},{6,22},{8,24},{10,26},{12,28},{14,30},{16,0},... | collective-permute-start | bytes 196616 | tf_op jit(solution)/shard_map/ppermute | solution.py:348
  12.9 15.9 %collective-permute-start.4 = (f32[1,128,128]{2,1,0:T(8,128)S(1)}, f32[1,128,128]{2,1,0:T(8,128)S(1)}, u32[]{:S(2)}, u32[]{:S(2)}) collective-permute-start(f32[1,128,128]{2,1,0:T(8,128)S(1)} %get-tuple-element.39), channel_id=1, source_target_pairs={{0,16},{2,18},{4,20},{6,22},{8,24},{10,26},{12,28},{14,30},{16,0},... | collective-permute-start | bytes 196616 | tf_op jit(solution)/shard_map/ppermute | solution.py:348
  15.4 4.0 %collective-permute-start.9 = (bf16[4,128,128]{2,1,0:T(8,128)(2,1)S(1)}, bf16[4,128,128]{2,1,0:T(8,128)(2,1)S(1)}, u32[]{:S(2)}, u32[]{:S(2)}) collective-permute-start(bf16[4,128,128]{2,1,0:T(8,128)(2,1)S(1)} %slice.84), channel_id=1, source_target_pairs={{0,2},{2,0},{4,6},{6,4},{8,10},{10,8},{12,14},{14,12},{16,18},{18,... | collective-permute-start | bytes 393224 | tf_op jit(solution)/shard_map/ppermute | solution.py:280
  16.7 4.2 %collective-permute-start.1 = (bf16[4,128,128]{2,1,0:T(8,128)(2,1)S(1)}, bf16[4,128,128]{2,1,0:T(8,128)(2,1)S(1)}, u32[]{:S(2)}, u32[]{:S(2)}) collective-permute-start(bf16[4,128,128]{2,1,0:T(8,128)(2,1)S(1)} %slice.85), channel_id=1, source_target_pairs={{0,4},{2,6},{4,0},{6,2},{8,12},{10,14},{12,8},{14,10},{16,20},{18,... | collective-permute-start | bytes 393224 | tf_op jit(solution)/shard_map/ppermute | solution.py:280
  19.5 3.5 %collective-permute-start.10 = (bf16[2,128,128]{2,1,0:T(8,128)(2,1)S(1)}, bf16[2,128,128]{2,1,0:T(8,128)(2,1)S(1)}, u32[]{:S(2)}, u32[]{:S(2)}) collective-permute-start(bf16[2,128,128]{2,1,0:T(8,128)(2,1)S(1)} %slice.86), channel_id=1, source_target_pairs={{0,8},{2,10},{4,12},{6,14},{8,0},{10,2},{12,4},{14,6},{16,24},{18,... | collective-permute-start | bytes 196616 | tf_op jit(solution)/shard_map/ppermute | solution.py:280
  20.9 4.3 %collective-permute-start.2 = (bf16[2,128,128]{2,1,0:T(8,128)(2,1)S(1)}, bf16[2,128,128]{2,1,0:T(8,128)(2,1)S(1)}, u32[]{:S(2)}, u32[]{:S(2)}) collective-permute-start(bf16[2,128,128]{2,1,0:T(8,128)(2,1)S(1)} %slice.87), channel_id=1, source_target_pairs={{0,8},{2,10},{4,12},{6,14},{8,0},{10,2},{12,4},{14,6},{16,24},{18,... | collective-permute-start | bytes 196616 | tf_op jit(solution)/shard_map/ppermute | solution.py:280
  23.0 4.1 %collective-permute-start.11 = (bf16[2,128,128]{2,1,0:T(8,128)(2,1)S(1)}, bf16[2,128,128]{2,1,0:T(8,128)(2,1)S(1)}, u32[]{:S(2)}, u32[]{:S(2)}) collective-permute-start(bf16[2,128,128]{2,1,0:T(8,128)(2,1)S(1)} %get-tuple-element.32), channel_id=1, source_target_pairs={{0,16},{2,18},{4,20},{6,22},{8,24},{10,26},{12,28},{14,30},{16,0},... | collective-permute-start | bytes 196616 | tf_op jit(solution)/shard_map/ppermute | solution.py:284
  25.3 4.1 %collective-permute-start.3 = (bf16[2,128,128]{2,1,0:T(8,128)(2,1)S(1)}, bf16[2,128,128]{2,1,0:T(8,128)(2,1)S(1)}, u32[]{:S(2)}, u32[]{:S(2)}) collective-permute-start(bf16[2,128,128]{2,1,0:T(8,128)(2,1)S(1)} %get-tuple-element.34), channel_id=1, source_target_pairs={{0,16},{2,18},{4,20},{6,22},{8,24},{10,26},{12,28},{14,30},{16,0},... | collective-permute-start | bytes 196616 | tf_op jit(solution)/shard_map/ppermute | solution.py:284
  27.3 3.8 %collective-permute-start.13 = (bf16[2,128,128]{2,1,0:T(8,128)(2,1)S(1)}, bf16[2,128,128]{2,1,0:T(8,128)(2,1)S(1)}, u32[]{:S(2)}, u32[]{:S(2)}) collective-permute-start(bf16[2,128,128]{2,1,0:T(8,128)(2,1)S(1)} %residual.3), channel_id=1, source_target_pairs={{0,8},{2,10},{4,12},{6,14},{8,0},{10,2},{12,4},{14,6},{16,24},{18,... | collective-permute-start | bytes 196616 | tf_op jit(solution)/shard_map/ppermute | solution.py:289
  29.5 3.2 %collective-permute-start.5 = (bf16[2,128,128]{2,1,0:T(8,128)(2,1)S(1)}, bf16[2,128,128]{2,1,0:T(8,128)(2,1)S(1)}, u32[]{:S(2)}, u32[]{:S(2)}) collective-permute-start(bf16[2,128,128]{2,1,0:T(8,128)(2,1)S(1)} %residual.2), channel_id=1, source_target_pairs={{0,8},{2,10},{4,12},{6,14},{8,0},{10,2},{12,4},{14,6},{16,24},{18,... | collective-permute-start | bytes 196616 | tf_op jit(solution)/shard_map/ppermute | solution.py:289
  31.1 3.9 %collective-permute-start.14 = (bf16[4,128,128]{2,1,0:T(8,128)(2,1)S(1)}, bf16[4,128,128]{2,1,0:T(8,128)(2,1)S(1)}, u32[]{:S(2)}, u32[]{:S(2)}) collective-permute-start(bf16[4,128,128]{2,1,0:T(8,128)(2,1)S(1)} %pad_maximum_fusion.4), channel_id=1, source_target_pairs={{0,2},{2,0},{4,6},{6,4},{8,10},{10,8},{12,14},{14,12},{16,18},{18,... | collective-permute-start | bytes 393224 | tf_op jit(solution)/shard_map/ppermute | solution.py:289
  32.8 4.1 %collective-permute-start.6 = (bf16[4,128,128]{2,1,0:T(8,128)(2,1)S(1)}, bf16[4,128,128]{2,1,0:T(8,128)(2,1)S(1)}, u32[]{:S(2)}, u32[]{:S(2)}) collective-permute-start(bf16[4,128,128]{2,1,0:T(8,128)(2,1)S(1)} %pad_maximum_fusion.3), channel_id=1, source_target_pairs={{0,4},{2,6},{4,0},{6,2},{8,12},{10,14},{12,8},{14,10},{16,20},{18,... | collective-permute-start | bytes 393224 | tf_op jit(solution)/shard_map/ppermute | solution.py:289
  35.0 5.9 %collective-permute-start.15 = (bf16[8,128,128]{2,1,0:T(8,128)(2,1)S(1)}, bf16[8,128,128]{2,1,0:T(8,128)(2,1)S(1)}, u32[]{:S(2)}, u32[]{:S(2)}) collective-permute-start(bf16[8,128,128]{2,1,0:T(8,128)(2,1)S(1)} %pad_maximum_fusion.1.b_low), channel_id=1, source_target_pairs={{0,4},{2,6},{4,0},{6,2},{8,12},{10,14},{12,8},{14,10},{16,20},{18,... | collective-permute-start | bytes 786440 | tf_op jit(solution)/shard_map/ppermute | solution.py:291
  36.9 6.8 %collective-permute-start.7 = (bf16[8,128,128]{2,1,0:T(8,128)(2,1)S(1)}, bf16[8,128,128]{2,1,0:T(8,128)(2,1)S(1)}, u32[]{:S(2)}, u32[]{:S(2)}) collective-permute-start(bf16[8,128,128]{2,1,0:T(8,128)(2,1)S(1)} %pad_maximum_fusion.a_low), channel_id=1, source_target_pairs={{0,2},{2,0},{4,6},{6,4},{8,10},{10,8},{12,14},{14,12},{16,18},{18,... | collective-permute-start | bytes 786440 | tf_op jit(solution)/shard_map/ppermute | solution.py:291
  48.3 8.3 %collective-permute-start.16 = (f32[16,8,128]{2,1,0:T(8,128)S(1)}, f32[16,8,128]{2,1,0:T(8,128)S(1)}, u32[]{:S(2)}, u32[]{:S(2)}) collective-permute-start(f32[16,8,128]{2,1,0:T(8,128)S(1)} %get-tuple-element.26), channel_id=1, source_target_pairs={{0,1},{1,0},{2,3},{3,2},{4,5},{5,4},{6,7},{7,6},{8,9},{9,8},{10,11... | collective-permute-start | bytes 196616 | tf_op jit(solution)/shard_map/ppermute | solution.py:383
  56.7 10.9 %collective-permute-start.19 = (bf16[576,128]{1,0:T(8,128)(2,1)S(1)}, bf16[576,128]{1,0:T(8,128)(2,1)S(1)}, u32[]{:S(2)}, u32[]{:S(2)}) collective-permute-start(bf16[576,128]{1,0:T(8,128)(2,1)S(1)} %pad_maximum_fusion.2), channel_id=1, source_target_pairs={{2,4},{4,2},{6,8},{8,6},{10,12},{12,10},{14,16},{16,14},{18,20},{2... | collective-permute-start | bytes 442376 | tf_op jit(solution)/shard_map/ppermute | solution.py:397
  57.4 10.2 %collective-permute-start.17 = (bf16[512,128]{1,0:T(8,128)(2,1)S(1)}, bf16[512,128]{1,0:T(8,128)(2,1)S(1)}, u32[]{:S(2)}, u32[]{:S(2)}) collective-permute-start(bf16[512,128]{1,0:T(8,128)(2,1)S(1)} %get-tuple-element.30), channel_id=1, source_target_pairs={{0,2},{2,0},{4,6},{6,4},{8,10},{10,8},{12,14},{14,12},{16,18},{18,... | collective-permute-start | bytes 393224 | tf_op jit(solution)/shard_map/ppermute | solution.py:396
  60.9 6.7 %collective-permute-start.18 = (bf16[64,128]{1,0:T(8,128)(2,1)S(1)}, bf16[64,128]{1,0:T(8,128)(2,1)S(1)}, u32[]{:S(2)}, u32[]{:S(2)}) collective-permute-start(bf16[64,128]{1,0:T(8,128)(2,1)S(1)} %bitcast.3), channel_id=1, source_target_pairs={{0,2},{2,0},{4,6},{6,4},{8,10},{10,8},{12,14},{14,12},{16,18},{18,... | collective-permute-start | bytes 49160 | tf_op jit(solution)/shard_map/ppermute | solution.py:400
